TPU v7x, 128 devices: a whole 4x4x4 slice. The times are simulated.
128 devices in a mesh: row: 8 (over y_hi, x), col: 16 (over y_lo, z, core).
Axes of the slice: x: 4, y: 4 (y_hi: 2, y_lo: 2; y = y_hi * 2 + y_lo), z: 4, core: 2. Of those that a mesh axis runs over, the one named last changes fastest.
Arguments:
- gate_out: bfloat16 [32, 512, 2048], P(None, 'row', 'col'), may hold values from -6 to 6
- gate_in: bfloat16 [32, 512, 2048], P(None, 'row', 'col'), may hold values from -6 to 6
- values: bfloat16 [32, 512, 2048], P(None, 'row', 'col'), may hold values from -6 to 6
- filter_spec: float32 [2, 32, 1024, 2048], P(None, 'row', 'col'), may hold values from -6 to 6
- skip: float32 [32], replicated, may hold values from -3 to 3
Outputs:
- gated_output: float32 [32, 512, 2048], P(None, 'row', 'col')
All inputs are finite; a program needn't handle non-finite values.
Results may differ from a plain program's by a relative error of at most 0.0049.
Values may be sent and summed in bfloat16 or wider, within the bound.
No kernel may reach another device: no remote copies, remote signals or barrier semaphores. Data moves between devices by JAX's collectives and lax.ppermute only.
A program may use at most 128 MiB of HBM per device.

v0:
```python
import math

import jax
import jax.numpy as jnp
import ml_dtypes
import numpy as np
from jax import lax
from jax.experimental import pallas as pl
from jax.experimental.pallas import tpu as pltpu
from jax.sharding import PartitionSpec as P

ROWS = 1024
COLS = 2048
OUTER = 64
INNER = 32
HALF = ROWS // 2
TOTAL = ROWS * COLS
LANES = 128
BLOCKS = 8
PER = HALF // BLOCKS
TWO_PI = 2.0 * math.pi
BF16 = jnp.bfloat16
F32 = jnp.float32


def grid_angle(first, second, modulus):
    product = (np.asarray(first, np.int64)[:, None] * np.asarray(second, np.int64)[None, :]) % modulus
    return product.astype(np.float32) * np.float32(TWO_PI / modulus)


def narrow(array):
    return np.asarray(array, np.float32).astype(ml_dtypes.bfloat16)


def row_table():
    angle = grid_angle(np.arange(HALF), np.arange(HALF), ROWS)
    cosines, sines = np.cos(angle), -np.sin(angle)
    sines[:, 0] = 1.0 - 2.0 * (np.arange(HALF) % 2)
    parts = np.stack([cosines, sines], 0).reshape(2, HALF, BLOCKS, PER).transpose(1, 2, 0, 3)
    return narrow(np.repeat(parts[:, :, :, None, :], 2, 3).reshape(HALF, BLOCKS * 2 * 2 * PER))


def outer_tables():
    near = grid_angle(np.arange(OUTER), np.arange(OUTER), OUTER)
    far = grid_angle(np.arange(OUTER) + 1, np.arange(OUTER), OUTER)
    c, s, cm, sm = np.cos(near), np.sin(near), np.cos(far), np.sin(far)
    return narrow(
        np.stack(
            [
                np.block([[c, s], [-s, c]]),
                np.block([[cm, -sm], [-sm, -cm]]),
                np.block([[c.T, -s.T], [s.T, c.T]]),
                np.block([[cm.T, -sm.T], [-sm.T, -cm.T]]),
            ]
        )
    )


def inner_tables():
    angle = grid_angle(np.arange(INNER), np.arange(INNER), INNER)
    c, s = np.kron(np.eye(4), np.cos(angle)), np.kron(np.eye(4), np.sin(angle))
    return narrow(np.stack([np.block([[c, s], [-s, c]]), np.block([[c, -s], [s, c]])]))


def middle_tables():
    angle = grid_angle(np.arange(OUTER + 1), np.arange(INNER), COLS).reshape(-1, 1)
    angle = np.broadcast_to(angle, (angle.shape[0], LANES))
    return np.stack([np.cos(angle), np.sin(angle)]).astype(np.float32)


def half_step_tables():
    place = np.broadcast_to(grid_angle(np.arange(LANES), [1], 2 * COLS), (LANES, LANES))
    block = np.broadcast_to(grid_angle(LANES * np.arange(16), [1], 2 * COLS), (16, LANES))
    both = [np.stack([np.cos(x), np.sin(x)]).astype(np.float32) for x in (place, block)]
    return both


def twist_base():
    angle = grid_angle(np.arange(HALF), np.arange(LANES), TOTAL)
    angle = angle.reshape(BLOCKS, PER, LANES).transpose(0, 2, 1)
    angle = np.concatenate([angle, angle], 2)
    return np.stack([np.cos(angle), np.sin(angle)]).astype(np.float32)


def filter_moves():
    moves = np.zeros((2, 272, 256), np.float32)
    for side in range(2):
        low, high = (0, 128) if side == 0 else (128, 0)
        for copy in range(2):
            for e in range(PER):
                lane = copy * PER + e
                moves[side, low + copy * PER + e, lane] = 1.0
                if e == 0:
                    moves[side, 256 + copy, 128 + lane] = 1.0
                else:
                    moves[side, high + copy * PER + PER - e, 128 + lane] = 1.0
    return narrow(moves)


def rotate(real, imag, cosine, sine):
    return real * cosine - imag * sine, imag * cosine + real * sine


def row_forward_body(x_ref, table_ref, base_ref, phase_ref, out_ref, turned_ref):
    block = pl.program_id(0)

    @pl.when(block == 0)
    def _():
        for chan in range(4):
            part = x_ref[:, chan].reshape(HALF, LANES)
            turned_ref[chan * LANES : (chan + 1) * LANES, :] = part.T

    sums = jnp.dot(turned_ref[...], table_ref[...], preferred_element_type=F32)
    first = lax.broadcasted_iota(jnp.int32, (LANES, LANES), 1) < PER
    cosine, sine = rotate(base_ref[0, 0], base_ref[1, 0], phase_ref[0, 0], phase_ref[1, 0])
    for pair in range(2):
        upper = sums[pair * 256 : pair * 256 + 128]
        lower = sums[pair * 256 + 128 : pair * 256 + 256]
        real = jnp.where(first, upper[:, :LANES], lower[:, :LANES])
        imag = jnp.where(first, upper[:, LANES:], lower[:, LANES:])
        real, imag = rotate(real, imag, cosine, -sine)
        place = block if pair == 0 else 15 - block
        out_ref[place, 0] = real.astype(BF16)
        out_ref[place, 1] = imag.astype(BF16)


def row_forward(x, table, base, phase):
    return pl.pallas_call(
        row_forward_body,
        grid=(BLOCKS,),
        in_specs=[
            pl.BlockSpec((8, 4, 64, LANES), lambda i: (0, 0, 0, 0)),
            pl.BlockSpec((HALF, 256), lambda i: (0, i)),
            pl.BlockSpec((2, 1, LANES, LANES), lambda i: (0, i, 0, 0)),
            pl.BlockSpec((2, 1, 1, LANES), lambda i: (0, i, 0, 0)),
        ],
        out_specs=pl.BlockSpec((16, 2, LANES, LANES), lambda i: (0, 0, 0, 0)),
        out_shape=jax.ShapeDtypeStruct((16, 2, LANES, LANES), BF16),
        scratch_shapes=[pltpu.VMEM((4 * LANES, HALF), BF16)],
        compiler_params=pltpu.CompilerParams(vmem_limit_bytes=24 * 1024 * 1024),
        cost_estimate=pl.CostEstimate(flops=1_100_000_000, bytes_accessed=5_000_000, transcendentals=0),
        name="row_forward",
    )(x, table, base, phase)


def filter_body(own_ref, got_ref, extra_ref, moves_ref, out_ref):
    for part in range(2):
        total = None
        for source, low, high in ((own_ref, 0, 128), (got_ref, 128, 256), (extra_ref, 256, 272)):
            term = lax.dot_general(
                source[part],
                moves_ref[low:high, :],
                (((0,), (0,)), ((), ())),
                preferred_element_type=F32,
            )
            total = term if total is None else total + term
        out_ref[0, part] = total[:, :LANES].astype(BF16)
        out_ref[1, part] = total[:, LANES:].astype(BF16)


def filter_layout(own, got, extra, moves):
    step = 256
    return pl.pallas_call(
        filter_body,
        grid=(COLS // step,),
        in_specs=[
            pl.BlockSpec((2, 128, step), lambda i: (0, 0, i)),
            pl.BlockSpec((2, 128, step), lambda i: (0, 0, i)),
            pl.BlockSpec((2, 16, step), lambda i: (0, 0, i)),
            pl.BlockSpec((272, 256), lambda i: (0, 0)),
        ],
        out_specs=pl.BlockSpec((2, 2, step, LANES), lambda i: (0, 0, i, 0)),
        out_shape=jax.ShapeDtypeStruct((2, 2, COLS, LANES), BF16),
        compiler_params=pltpu.CompilerParams(vmem_limit_bytes=16 * 1024 * 1024),
        cost_estimate=pl.CostEstimate(flops=600_000_000, bytes_accessed=5_000_000, transcendentals=0),
        name="filter_layout",
    )(own, got, extra, moves)


def column_body(
    y_ref, filt_ref, outer_ref, inner_ref, mid_ref, place_ref, block_ref, base_ref, phase_ref, special_ref,
    out_ref, wide_ref, work_ref,
):
    special = special_ref[...] > 0.5

    def spread(block, carry):
        rows = pl.ds(pl.multiple_of(block * LANES, LANES), LANES)
        real = y_ref[block, 0].astype(F32)
        imag = y_ref[block, 1].astype(F32)
        cosine, sine = rotate(
            place_ref[0], place_ref[1], block_ref[0, pl.ds(block, 1), :], block_ref[1, pl.ds(block, 1), :]
        )
        wide_ref[0, rows, :] = real
        wide_ref[1, rows, :] = jnp.where(special, 0.0, imag)
        wide_ref[2, rows, :] = jnp.where(special, imag * cosine, real)
        wide_ref[3, rows, :] = jnp.where(special, -imag * sine, imag)
        return carry

    lax.fori_loop(0, 16, spread, 0)

    def gather(ref, which, at):
        return ref[which, pl.ds(at, OUTER, stride=INNER), :].astype(BF16)

    def pair_of(ref, which, at):
        return jnp.concatenate(
            [
                jnp.concatenate([gather(ref, which, at), gather(ref, which + 1, at)], 0),
                jnp.concatenate([gather(ref, which, at + 1), gather(ref, which + 1, at + 1)], 0),
            ],
            1,
        )

    def outer_forward(step, carry):
        at = step * 2
        for side in range(2):
            sums = jnp.dot(outer_ref[side], pair_of(wide_ref, 2 * side, at), preferred_element_type=F32)
            for part in range(2):
                for shift in range(2):
                    work_ref[2 * side + part, pl.ds(at + shift, OUTER, stride=INNER), :] = sums[
                        part * OUTER : (part + 1) * OUTER, shift * LANES : (shift + 1) * LANES
                    ]
        return carry

    lax.fori_loop(0, INNER // 2, outer_forward, 0)

    def inner_step(step, carry):
        rows = pl.ds(pl.multiple_of(step * LANES, LANES), LANES)
        turns = []
        for side in range(2):
            at = pl.ds(pl.multiple_of(step * LANES + side * INNER, INNER), LANES)
            turns.append((mid_ref[0, at, :], mid_ref[1, at, :]))
        sides = []
        for side in range(2):
            real, imag = rotate(
                work_ref[2 * side, rows, :], work_ref[2 * side + 1, rows, :], turns[side][0], -turns[side][1]
            )
            sides.append(jnp.concatenate([real.astype(BF16), imag.astype(BF16)], 0))
        spectrum = jnp.dot(inner_ref[0], jnp.concatenate(sides, 1), preferred_element_type=F32)
        sides = []
        for side in range(2):
            lanes = slice(side * LANES, (side + 1) * LANES)
            real, imag = rotate(
                spectrum[:LANES, lanes],
                spectrum[LANES:, lanes],
                filt_ref[side, 0, rows, :].astype(F32),
                filt_ref[side, 1, rows, :].astype(F32),
            )
            sides.append(jnp.concatenate([real.astype(BF16), imag.astype(BF16)], 0))
        middle = jnp.dot(inner_ref[1], jnp.concatenate(sides, 1), preferred_element_type=F32)
        for side in range(2):
            lanes = slice(side * LANES, (side + 1) * LANES)
            real, imag = rotate(middle[:LANES, lanes], middle[LANES:, lanes], turns[side][0], turns[side][1])
            work_ref[2 * side, rows, :] = real
            work_ref[2 * side + 1, rows, :] = imag
        return carry

    lax.fori_loop(0, 16, inner_step, 0)

    def outer_inverse(step, carry):
        at = step * 2
        near = jnp.dot(outer_ref[2], pair_of(work_ref, 0, at), preferred_element_type=F32)
        far = jnp.dot(outer_ref[3], pair_of(work_ref, 2, at), preferred_element_type=F32)
        for shift in range(2):
            lanes = slice(shift * LANES, (shift + 1) * LANES)
            near_re, near_im = near[:OUTER, lanes], near[OUTER:, lanes]
            far_re, far_im = far[:OUTER, lanes], far[OUTER:, lanes]
            rows = pl.ds(at + shift, OUTER, stride=INNER)
            wide_ref[0, rows, :] = jnp.where(special, near_re, near_re + far_re)
            wide_ref[1, rows, :] = jnp.where(special, far_re, near_im + far_im)
            wide_ref[2, rows, :] = far_im
        return carry

    lax.fori_loop(0, INNER // 2, outer_inverse, 0)

    def finish(block, carry):
        rows = pl.ds(pl.multiple_of(block * LANES, LANES), LANES)
        cosine, sine = rotate(
            place_ref[0], place_ref[1], block_ref[0, pl.ds(block, 1), :], block_ref[1, pl.ds(block, 1), :]
        )
        real = wide_ref[0, rows, :]
        imag = wide_ref[1, rows, :]
        imag = jnp.where(special, imag * cosine - wide_ref[2, rows, :] * sine, imag)
        cosine, sine = rotate(
            base_ref[0], base_ref[1], phase_ref[0, pl.ds(block, 1), :], phase_ref[1, pl.ds(block, 1), :]
        )
        real, imag = rotate(real, imag, cosine, sine)
        out_ref[block, 0] = real.astype(BF16)
        out_ref[block, 1] = imag.astype(BF16)
        return carry

    lax.fori_loop(0, 16, finish, 0)


def column_step(y, filt, outer, inner, mid, place, block, base, phase, special):
    whole = pl.BlockSpec(memory_space=pltpu.VMEM)
    return pl.pallas_call(
        column_body,
        in_specs=[whole] * 10,
        out_specs=whole,
        out_shape=jax.ShapeDtypeStruct((16, 2, LANES, LANES), BF16),
        scratch_shapes=[pltpu.VMEM((4, COLS, LANES), F32), pltpu.VMEM((4, COLS, LANES), F32)],
        compiler_params=pltpu.CompilerParams(vmem_limit_bytes=32 * 1024 * 1024),
        cost_estimate=pl.CostEstimate(flops=2_000_000_000, bytes_accessed=9_000_000, transcendentals=0),
        name="column_step",
    )(y, filt, outer, inner, mid, place, block, base, phase, special)


def row_inverse_body(z_ref, table_ref, out_ref, split_ref):
    @pl.when(pl.program_id(0) == 0)
    def _():
        first = lax.broadcasted_iota(jnp.int32, (LANES, LANES), 1) < PER
        for place in range(16):
            pair, block = (0, place) if place < 8 else (1, 15 - place)
            for part in range(2):
                values = z_ref[place, part]
                lanes = slice((block * 2 + part) * LANES, (block * 2 + part + 1) * LANES)
                zero = jnp.zeros_like(values)
                split_ref[pair * 256 : pair * 256 + 128, lanes] = jnp.where(first, values, zero)
                split_ref[pair * 256 + 128 : pair * 256 + 256, lanes] = jnp.where(first, zero, values)

    sums = lax.dot_general(
        table_ref[...], split_ref[...], (((1,), (1,)), ((), ())), preferred_element_type=F32
    ) * (1.0 / TOTAL)
    for row in range(2):
        for chan in range(4):
            out_ref[row, chan] = sums[row * 64 : (row + 1) * 64, chan * LANES : (chan + 1) * LANES].astype(BF16)


def row_inverse(z, table):
    return pl.pallas_call(
        row_inverse_body,
        grid=(4,),
        in_specs=[
            pl.BlockSpec((16, 2, LANES, LANES), lambda i: (0, 0, 0, 0)),
            pl.BlockSpec((LANES, COLS), lambda i: (i, 0)),
        ],
        out_specs=pl.BlockSpec((2, 4, 64, LANES), lambda i: (i, 0, 0, 0)),
        out_shape=jax.ShapeDtypeStruct((8, 4, 64, LANES), BF16),
        scratch_shapes=[pltpu.VMEM((4 * LANES, COLS), BF16)],
        compiler_params=pltpu.CompilerParams(vmem_limit_bytes=16 * 1024 * 1024),
        cost_estimate=pl.CostEstimate(flops=1_100_000_000, bytes_accessed=4_000_000, transcendentals=0),
        name="row_inverse",
    )(z, table)


def turn(first, second, modulus):
    angle = ((first * second) % modulus).astype(F32) * (TWO_PI / modulus)
    return jnp.stack([jnp.cos(angle), jnp.sin(angle)])


def per_device(gate_out, gate_in, values, filter_spec, skip):
    col = lax.axis_index("col")
    low_side = col < 8
    table = jnp.asarray(row_table())

    gated = gate_in.astype(F32) * values.astype(F32)
    x = lax.all_to_all(gated.astype(BF16), "row", split_axis=0, concat_axis=0, tiled=True)

    mine = jnp.where(low_side, 0, 2)
    own = lax.dynamic_slice_in_dim(filter_spec, mine, 2, axis=1).astype(BF16)
    other = lax.dynamic_slice_in_dim(filter_spec, 2 - mine, 2, axis=1).astype(BF16)
    got = lax.ppermute(other, "col", [(i, 15 - i) for i in range(16)])
    extra_low = lax.ppermute(
        filter_spec[:, :2, 0, :].astype(BF16), "col", [(i, (16 - i) % 8) for i in range(8, 16)]
    )
    extra_high = lax.ppermute(
        filter_spec[:, 2:, 0, :].astype(BF16), "col", [(i, 8 + (i - 1) % 8) for i in range(8, 16)]
    )
    extra = jnp.where(low_side, extra_low, extra_high)
    extra = jnp.pad(extra, ((0, 0), (0, 14), (0, 0)))
    moves = jnp.where(low_side, filter_moves()[0], filter_moves()[1])
    filt = filter_layout(own.reshape(2, 128, COLS), got.reshape(2, 128, COLS), extra, moves)

    lane = jnp.arange(LANES, dtype=jnp.int32) % PER
    all_k1 = (PER * jnp.arange(BLOCKS, dtype=jnp.int32))[:, None, None] + lane[None, None, :]
    y = row_forward(x.reshape(8, 4, 64, LANES), table, twist_base(), turn(all_k1, col, ROWS * 16))
    y = lax.all_to_all(y, "col", split_axis=0, concat_axis=0, tiled=True)

    own_k1 = PER * jnp.where(low_side, col, 15 - col) + lane
    place, block = half_step_tables()
    base = turn(jnp.arange(LANES, dtype=jnp.int32)[:, None], own_k1[None, :], TOTAL)
    phase = turn(jnp.arange(16, dtype=jnp.int32)[:, None], own_k1[None, :], ROWS * 16)
    special = (own_k1 == 0).astype(F32)[None, :]
    z = column_step(
        y, filt, outer_tables(), inner_tables(), middle_tables(), place, block, base, phase, special
    )
    z = lax.all_to_all(z, "col", split_axis=0, concat_axis=0, tiled=True)

    convolved = row_inverse(z, table).reshape(32, 64, LANES)
    convolved = lax.all_to_all(convolved, "row", split_axis=0, concat_axis=0, tiled=True)
    return gate_out.astype(F32) * (convolved.astype(F32) + skip[:, None, None] * gated)


def solution(mesh):
    return jax.shard_map(
        per_device,
        mesh=mesh,
        in_specs=(
            P(None, "row", "col"),
            P(None, "row", "col"),
            P(None, "row", "col"),
            P(None, "row", "col", None),
            P(),
        ),
        out_specs=P(None, "row", "col"),
        check_vma=False,
    )
```

profile of v0, /device:TPU:0, one launch (start us, length us, event | category | flops | bytes accessed | tf_op | source)
XLA Modules:
  0.0 137.2 jit_solution(11312590645298182857)
XLA Ops:
  0.0 3.7 %dynamic-slice_convert_fusion = (bf16[2,2,64,2048]{3,2,1,0:T(8,128)(2,1)}, bf16[2,2,64,2048]{3,2,1,0:T(8,128)(2,1)S(1)}) fusion(f32[2,4,64,2048]{3,2,1,0:T(8,128)} %param.17, s32[]{:T(128)S(6)} %select_n.109, s32[]{:T(128)S(6)} %select_n.108), kind=kLoop, calls=%fused_computation.1 | loop fusion | bytes 4194312 | tf_op jit(solution)/shard_map/convert_element_type | solution.py:361
  3.7 4.6 %collective-permute-start = (bf16[2,2,64,2048]{3,2,1,0:T(8,128)(2,1)}, bf16[2,2,64,2048]{3,2,1,0:T(8,128)(2,1)S(1)}, u32[]{:S(2)}, u32[]{:S(2)}) collective-permute-start(bf16[2,2,64,2048]{3,2,1,0:T(8,128)(2,1)} %get-tuple-element.5), channel_id=1, source_target_pairs={{0,15},{1,14},{2,13},{3,12},{4,11},{5,10},{6,9},{7,8},{8,7},{9,6},... | collective-permute-start | bytes 3145736 | tf_op jit(solution)/shard_map/ppermute | solution.py:362
  8.3 2.7 %copy.19 = bf16[2,4,64,2048]{3,1,0,2:T(4,128)(2,1)S(1)} copy(f32[2,4,64,2048]{3,2,1,0:T(8,128)S(1)} %copy-done.11) | data formatting | bytes 6291456 | tf_op args[3]
  11.0 1.3 collective-permute-start.1
  12.3 0.7 collective-permute-start.2
  13.0 1.0 fusion
  14.0 6.6 %all-to-all-start = ((bf16[32,64,128]{2,1,0:T(8,128)(2,1)}), bf16[32,64,128]{2,1,0:T(8,128)(2,1)S(1)}, u32[]{:S(2)}, u32[]{:S(2)}) async-start(bf16[32,64,128]{2,1,0:T(8,128)(2,1)} %fusion), calls=%async_computation | async-start | bytes 1048576 | tf_op jit(solution)/shard_map/all_to_all | solution.py:357
  20.6 0.1 fusion.16
  20.7 0.1 multiply_cosine_fusion
  20.9 0.1 fusion.18
  20.9 0.3 fusion.8
  21.2 19.8 %all-to-all-done = bf16[32,64,128]{2,1,0:T(8,128)(2,1)S(1)} async-done(((bf16[32,64,128]{2,1,0:T(8,128)(2,1)}), bf16[32,64,128]{2,1,0:T(8,128)(2,1)S(1)}, u32[]{:S(2)}, u32[]{:S(2)}) %all-to-all-start) | async-done | bytes 524320 | tf_op jit(solution)/shard_map/all_to_all | solution.py:357
  41.0 1.6 %copy-done = bf16[512,2048]{1,0:T(8,128)(2,1)S(1)} copy-done((bf16[512,2048]{1,0:T(8,128)(2,1)S(1)}, bf16[512,2048]{1,0:T(8,128)(2,1)}, u32[]{:S(2)}) %copy-start) | copy-done | bytes 2097176
  42.6 1.2 copy-done.4
  43.8 4.1 %row_forward.1 = bf16[16,2,128,128]{3,2,1,0:T(8,128)(2,1)} custom-call(bf16[8,4,64,128]{3,2,1,0:T(8,128)(2,1)S(1)} %bitcast.10, bf16[512,2048]{1,0:T(8,128)(2,1)S(1)} %copy-done, f32[2,8,128,128]{3,2,1,0:T(8,128)S(1)} %copy-done.4, f32[2,8,1,128]{3,2,1,0:T(1,128)S(1)} %pad_maximum_fusion.2.phase_ref), custom_call_target="tpu_custom_call" | custom-call | flops 1100000000 | bytes 5000000 | tf_op jit(solution)/shard_map/row_forward/pallas_call | solution.py:128
  47.9 4.5 %all-to-all-start.1 = ((bf16[16,2,128,128]{3,2,1,0:T(8,128)(2,1)}), bf16[16,2,128,128]{3,2,1,0:T(8,128)(2,1)}, u32[]{:S(2)}, u32[]{:S(2)}) async-start(bf16[16,2,128,128]{3,2,1,0:T(8,128)(2,1)} %row_forward.1), calls=%async_computation.1 | async-start | bytes 2097152 | tf_op jit(solution)/shard_map/all_to_all | solution.py:377
  52.5 0.6 compare_convert_fusion.special_ref
  53.1 1.0 copy-done.2
  54.1 1.2 copy-done.3
  55.3 3.7 %filter_layout.1.filt_ref = bf16[2,2,2048,128]{3,2,1,0:T(8,128)(2,1)S(1)} custom-call(bf16[2,128,2048]{2,1,0:T(8,128)(2,1)S(1)} %bitcast.9, bf16[2,128,2048]{2,1,0:T(8,128)(2,1)S(1)} %bitcast.11, bf16[2,16,2048]{2,1,0:T(8,128)(2,1)S(1)} %pad.4.extra_ref, bf16[272,256]{1,0:T(8,128)(2,1)S(1)} %broadcast_select_fusion.moves_ref), custom_call_target="tpu_custom_call" | custom-call | flops 600000000 | bytes 5000000 | tf_op jit(solution)/shard_map/filter_layout/pallas_call | solution.py:163
  59.0 10.0 %all-to-all-done.1.y_ref = bf16[16,2,128,128]{3,2,1,0:T(8,128)(2,1)} async-done(((bf16[16,2,128,128]{3,2,1,0:T(8,128)(2,1)}), bf16[16,2,128,128]{3,2,1,0:T(8,128)(2,1)}, u32[]{:S(2)}, u32[]{:S(2)}) %all-to-all-start.1) | async-done | bytes 1048608 | tf_op jit(solution)/shard_map/all_to_all | solution.py:377
  69.0 1.6 %copy-done.5 = f32[2,2080,128]{2,1,0:T(8,128)S(1)} copy-done((f32[2,2080,128]{2,1,0:T(8,128)S(1)}, f32[2,2080,128]{2,1,0:T(8,128)}, u32[]{:S(2)}) %copy-start.5) | copy-done | bytes 2129944
  70.6 0.9 copy-done.7
  71.5 0.9 copy-done.8
  72.4 0.7 copy-done.9
  73.1 0.7 copy-done.10
  73.8 23.7 %column_step.1 = bf16[16,2,128,128]{3,2,1,0:T(8,128)(2,1)S(1)} custom-call(bf16[16,2,128,128]{3,2,1,0:T(8,128)(2,1)} %all-to-all-done.1.y_ref, bf16[2,2,2048,128]{3,2,1,0:T(8,128)(2,1)S(1)} %filter_layout.1.filt_ref, bf16[4,128,128]{2,1,0:T(8,128)(2,1)S(1)} %copy-done.7, bf16[2,256,256]{2,1,0:T(8,128)(2,1)S(1)} %copy-done.6, f32[2,2080,128]{2,1,0:T(8,128)S(1)} %copy-done.5, ...), custom_call_target="tpu_custom_call" | custom-call | flops 2000000000 | bytes 9000000 | tf_op jit(solution)/shard_map/column_step/pallas_call | solution.py:296
  97.5 0.0 copy-start.1
  97.6 19.2 %all_to_all.20.z_ref = bf16[16,2,128,128]{3,2,1,0:T(8,128)(2,1)S(1)} all-to-all(bf16[16,2,128,128]{3,2,1,0:T(8,128)(2,1)S(1)} %column_step.1), channel_id=1, replica_groups=mesh['row'=8,'col'=16] {'col'}, dimensions={0} | all-to-all | bytes 2097152 | tf_op jit(solution)/shard_map/all_to_all | solution.py:387
  116.8 3.9 %row_inverse.1 = bf16[8,4,64,128]{3,2,1,0:T(8,128)(2,1)S(1)} custom-call(bf16[16,2,128,128]{3,2,1,0:T(8,128)(2,1)S(1)} %all_to_all.20.z_ref, bf16[512,2048]{1,0:T(8,128)(2,1)S(1)} %copy-done.1), custom_call_target="tpu_custom_call" | custom-call | flops 1100000000 | bytes 4000000 | tf_op jit(solution)/shard_map/row_inverse/pallas_call | solution.py:330
  120.7 15.2 %all_to_all.21 = bf16[32,64,128]{2,1,0:T(8,128)(2,1)S(1)} all-to-all(bf16[32,64,128]{2,1,0:T(8,128)(2,1)S(1)} %bitcast.12), channel_id=1, replica_groups=mesh['row'=8,'col'=16] {'row'}, dimensions={0} | all-to-all | bytes 1048576 | tf_op jit(solution)/shard_map/all_to_all | solution.py:390
  135.9 1.3 add_multiply_fusion
  (42 shorter events, 0.2 us)
Async XLA Ops:
  0.0 8.3 %copy-start.11 = (f32[2,4,64,2048]{3,2,1,0:T(8,128)S(1)}, f32[2,4,64,2048]{3,2,1,0:T(8,128)}, u32[]{:S(2)}) copy-start(f32[2,4,64,2048]{3,2,1,0:T(8,128)} %param.17) | copy-start | bytes 12582916
  3.7 9.3 %copy-start.12 = (bf16[32,64,128]{2,1,0:T(8,128)(2,1)S(1)}, bf16[32,64,128]{2,1,0:T(8,128)(2,1)}, u32[]{:S(2)}) copy-start(bf16[32,64,128]{2,1,0:T(8,128)(2,1)} %param.16) | copy-start | bytes 1572868
  3.7 9.3 %copy-start.14 = (bf16[32,64,128]{2,1,0:T(8,128)(2,1)S(1)}, bf16[32,64,128]{2,1,0:T(8,128)(2,1)}, u32[]{:S(2)}) copy-start(bf16[32,64,128]{2,1,0:T(8,128)(2,1)} %param.15) | copy-start | bytes 1572868
  3.7 49.4 %collective-permute-start = (bf16[2,2,64,2048]{3,2,1,0:T(8,128)(2,1)}, bf16[2,2,64,2048]{3,2,1,0:T(8,128)(2,1)S(1)}, u32[]{:S(2)}, u32[]{:S(2)}) collective-permute-start(bf16[2,2,64,2048]{3,2,1,0:T(8,128)(2,1)} %get-tuple-element.5), channel_id=1, source_target_pairs={{0,15},{1,14},{2,13},{3,12},{4,11},{5,10},{6,9},{7,8},{8,7},{9,6},... | collective-permute-start | bytes 3145736 | tf_op jit(solution)/shard_map/ppermute | solution.py:362
  11.0 42.1 %collective-permute-start.1 = (bf16[2,2,2048]{2,1,0:T(2,128)(2,1)S(1)}, bf16[2,2,2048]{2,1,0:T(2,128)(2,1)S(1)}, u32[]{:S(2)}, u32[]{:S(2)}) collective-permute-start(bf16[2,2,2048]{2,1,0:T(2,128)(2,1)S(1)} %get-tuple-element.8), channel_id=1, source_target_pairs={{8,0},{9,7},{10,6},{11,5},{12,4},{13,3},{14,2},{15,1},{24,16},{25,... | collective-permute-start | bytes 49160 | tf_op jit(solution)/shard_map/ppermute | solution.py:363
  12.3 40.8 %collective-permute-start.2 = (bf16[2,2,2048]{2,1,0:T(2,128)(2,1)S(1)}, bf16[2,2,2048]{2,1,0:T(2,128)(2,1)S(1)}, u32[]{:S(2)}, u32[]{:S(2)}) collective-permute-start(bf16[2,2,2048]{2,1,0:T(2,128)(2,1)S(1)} %get-tuple-element.7), channel_id=1, source_target_pairs={{8,15},{9,8},{10,9},{11,10},{12,11},{13,12},{14,13},{15,14},{24,31... | collective-permute-start | bytes 49160 | tf_op jit(solution)/shard_map/ppermute | solution.py:366
  14.0 27.1 %all-to-all-start = ((bf16[32,64,128]{2,1,0:T(8,128)(2,1)}), bf16[32,64,128]{2,1,0:T(8,128)(2,1)S(1)}, u32[]{:S(2)}, u32[]{:S(2)}) async-start(bf16[32,64,128]{2,1,0:T(8,128)(2,1)} %fusion), calls=%async_computation | async-start | bytes 1048576 | tf_op jit(solution)/shard_map/all_to_all | solution.py:357
  41.0 1.6 %copy-start = (bf16[512,2048]{1,0:T(8,128)(2,1)S(1)}, bf16[512,2048]{1,0:T(8,128)(2,1)}, u32[]{:S(2)}) copy-start(bf16[512,2048]{1,0:T(8,128)(2,1)} %constant.97.clone.table_ref) | copy-start | bytes 6291460
  42.6 1.2 copy-start.4
  47.9 4.5 %copy-start.17 = (bf16[272,256]{1,0:T(8,128)(2,1)S(1)}, bf16[272,256]{1,0:T(8,128)(2,1)}, u32[]{:S(2)}) copy-start(bf16[272,256]{1,0:T(8,128)(2,1)} %constant.98.clone) | copy-start | bytes 417796
  47.9 4.5 %copy-start.18 = (bf16[272,256]{1,0:T(8,128)(2,1)S(1)}, bf16[272,256]{1,0:T(8,128)(2,1)}, u32[]{:S(2)}) copy-start(bf16[272,256]{1,0:T(8,128)(2,1)} %constant.99.clone) | copy-start | bytes 417796
  47.9 21.1 %all-to-all-start.1 = ((bf16[16,2,128,128]{3,2,1,0:T(8,128)(2,1)}), bf16[16,2,128,128]{3,2,1,0:T(8,128)(2,1)}, u32[]{:S(2)}, u32[]{:S(2)}) async-start(bf16[16,2,128,128]{3,2,1,0:T(8,128)(2,1)} %row_forward.1), calls=%async_computation.1 | async-start | bytes 2097152 | tf_op jit(solution)/shard_map/all_to_all | solution.py:377
  53.1 1.0 copy-start.2
  54.1 1.2 copy-start.3
  55.3 13.7 %copy-start.6 = (bf16[2,256,256]{2,1,0:T(8,128)(2,1)S(1)}, bf16[2,256,256]{2,1,0:T(8,128)(2,1)}, u32[]{:S(2)}) copy-start(bf16[2,256,256]{2,1,0:T(8,128)(2,1)} %constant.102.clone.inner_ref) | copy-start | bytes 786436
  69.0 1.6 %copy-start.5 = (f32[2,2080,128]{2,1,0:T(8,128)S(1)}, f32[2,2080,128]{2,1,0:T(8,128)}, u32[]{:S(2)}) copy-start(f32[2,2080,128]{2,1,0:T(8,128)} %constant.103.clone.mid_ref) | copy-start | bytes 6389764
  70.6 0.9 copy-start.7
  71.5 0.9 copy-start.8
  72.4 0.7 copy-start.9
  73.1 0.7 copy-start.10
  97.5 19.3 %copy-start.1 = (bf16[512,2048]{1,0:T(8,128)(2,1)S(1)}, bf16[512,2048]{1,0:T(8,128)(2,1)}, u32[]{:S(2)}) copy-start(bf16[512,2048]{1,0:T(8,128)(2,1)} %constant.97.clone.table_ref) | copy-start | bytes 6291460
  116.8 19.1 %copy-start.13 = (bf16[32,64,128]{2,1,0:T(8,128)(2,1)S(1)}, bf16[32,64,128]{2,1,0:T(8,128)(2,1)}, u32[]{:S(2)}) copy-start(bf16[32,64,128]{2,1,0:T(8,128)(2,1)} %param.16) | copy-start | bytes 1572868
  116.8 19.1 %copy-start.15 = (bf16[32,64,128]{2,1,0:T(8,128)(2,1)S(1)}, bf16[32,64,128]{2,1,0:T(8,128)(2,1)}, u32[]{:S(2)}) copy-start(bf16[32,64,128]{2,1,0:T(8,128)(2,1)} %param.15) | copy-start | bytes 1572868
  116.8 19.1 %copy-start.16 = (bf16[32,64,128]{2,1,0:T(8,128)(2,1)S(1)}, bf16[32,64,128]{2,1,0:T(8,128)(2,1)}, u32[]{:S(2)}) copy-start(bf16[32,64,128]{2,1,0:T(8,128)(2,1)} %param.14) | copy-start | bytes 1572868
  116.8 19.1 %copy-start.19 = (f32[32]{0:T(128)S(1)}, f32[32]{0:T(128)}, u32[]{:S(2)}) copy-start(f32[32]{0:T(128)} %param.18) | copy-start | bytes 388
where the time goes:
time: 138 us; the launch traced here: 137 us
  Pallas kernels  35.3 us (26%)
  blocking collectives  34.5 us (25%)
  waiting for transfers between devices  29.8 us (22%)
  starting transfers between devices  17.7 us (13%)
  local copies, waits for them, and re-layouts  16.3 us (12%)
  other arithmetic  3.48 us (3%)
    pallas_call x1, Pallas kernels, column_step(): pl.pallas_call(column_body, in_specs=[whole] * 10, out_specs=whole, out_s...  23.7 us
    all_to_all x1, waiting for transfers between devices, per_device(): lax.all_to_all(gated.astype(BF16), 'row', split_axis=0, concat_axis=0, ti...  19.8 us
    all_to_all x1, blocking collectives, per_device(): z = lax.all_to_all(z, 'col', split_axis=0, concat_axis=0, tiled=True)  19.2 us
    all_to_all x1, blocking collectives, per_device(): lax.all_to_all(convolved, 'row', split_axis=0, concat_axis=0, tiled=True)  15.2 us
    unnamed x41, local copies, waits for them, and re-layouts  12.5 us
    all_to_all x1, waiting for transfers between devices, per_device(): y = lax.all_to_all(y, 'col', split_axis=0, concat_axis=0, tiled=True)  9.98 us
    all_to_all x1, starting transfers between devices, per_device(): lax.all_to_all(gated.astype(BF16), 'row', split_axis=0, concat_axis=0, ti...  6.64 us
    ppermute x1, starting transfers between devices, per_device(): got = lax.ppermute(other, 'col', [(i, 15 - i) for i in range(16)])  4.57 us
  transfers between devices with their start and end apart: 5, of which 2 were waited for; matrix products, arithmetic and copies ran while one was open for 4% of the time, Pallas kernels for 6%

commit v1 on v0

v1 whole, which is shorter than its diff:
```python
import math

import jax
import jax.numpy as jnp
import ml_dtypes
import numpy as np
from jax import lax
from jax.experimental import pallas as pl
from jax.experimental.pallas import tpu as pltpu
from jax.sharding import PartitionSpec as P

ROWS = 1024
COLS = 2048
OUTER = 64
INNER = 32
HALF = ROWS // 2
TOTAL = ROWS * COLS
LANES = 128
BLOCKS = 8
PER = HALF // BLOCKS
TWO_PI = 2.0 * math.pi
BF16 = jnp.bfloat16
F32 = jnp.float32


def grid_angle(first, second, modulus):
    product = (np.asarray(first, np.int64)[:, None] * np.asarray(second, np.int64)[None, :]) % modulus
    return product.astype(np.float32) * np.float32(TWO_PI / modulus)


def narrow(array):
    return np.asarray(array, np.float32).astype(ml_dtypes.bfloat16)


def row_table():
    angle = grid_angle(np.arange(HALF), np.arange(HALF), ROWS)
    cosines, sines = np.cos(angle), -np.sin(angle)
    sines[:, 0] = 1.0 - 2.0 * (np.arange(HALF) % 2)
    parts = np.stack([cosines, sines], 0).reshape(2, HALF, BLOCKS, PER).transpose(1, 2, 0, 3)
    return narrow(np.repeat(parts[:, :, :, None, :], 2, 3).reshape(HALF, BLOCKS * 2 * 2 * PER))


def pair_order(table, first, second):
    rows, cols = table.shape[0] // 2, table.shape[1] // 2
    out = np.zeros((2, rows // first, 2, first, 2, cols // second, 2, second), np.float32)
    for which in range(2):
        out[:, :, which, :, :, :, which, :] = table.reshape(2, rows // first, first, 2, cols // second, second)
    return out.reshape(4 * rows, 4 * cols)


def outer_tables():
    near = grid_angle(np.arange(OUTER), np.arange(OUTER), OUTER)
    far = grid_angle(np.arange(OUTER) + 1, np.arange(OUTER), OUTER)
    c, s, cm, sm = np.cos(near), np.sin(near), np.cos(far), np.sin(far)
    return [
        pair_order(np.block([[c, s], [-s, c]]), 1, 4),
        pair_order(np.block([[cm, -sm], [-sm, -cm]]), 1, 4),
        pair_order(np.block([[c.T, -s.T], [s.T, c.T]]), 4, 1),
        pair_order(np.block([[cm.T, -sm.T], [-sm.T, -cm.T]]), 4, 1),
    ]


def inner_tables():
    angle = grid_angle(np.arange(INNER), np.arange(INNER), INNER)
    c, s = np.cos(angle), np.sin(angle)
    spread = np.zeros((2, 4, INNER, 2, INNER // 2, 4, 2), np.float32)
    for k in range(4):
        spread[:, k, :, :, :, k, :] = np.block([[c, s], [-s, c]]).reshape(2, INNER, 2, INNER // 2, 2)
    spread = spread.reshape(256, 256)
    return [spread, spread.T]


def step_tables():
    return narrow(np.stack(outer_tables() + inner_tables()))


def middle_tables():
    angle = grid_angle(np.arange(OUTER + 1), np.arange(INNER), COLS)
    sides = []
    for side in range(2):
        own = angle[side : side + OUTER].reshape(16, 4, 16, 2).transpose(0, 2, 1, 3).reshape(COLS, 1)
        own = np.broadcast_to(own, (COLS, LANES))
        sides.append(np.stack([np.cos(own), np.sin(own)]))
    return np.stack(sides).astype(np.float32)


def place_order():
    return np.arange(LANES).reshape(4, INNER).T.reshape(-1)


def place_moves():
    return narrow(np.eye(LANES)[place_order()])


def twist_base():
    angle = grid_angle(np.arange(HALF), place_order(), TOTAL)
    angle = angle.reshape(BLOCKS, PER, LANES).transpose(0, 2, 1)
    angle = np.concatenate([angle, angle], 2)
    return np.stack([np.cos(angle), np.sin(angle)]).astype(np.float32)


def filter_moves():
    moves = np.zeros((2, 272, 256), np.float32)
    for side in range(2):
        low, high = (0, 128) if side == 0 else (128, 0)
        for copy in range(2):
            for e in range(PER):
                lane = copy * PER + e
                moves[side, low + copy * PER + e, lane] = 1.0
                if e == 0:
                    moves[side, 256 + copy, 128 + lane] = 1.0
                else:
                    moves[side, high + copy * PER + PER - e, 128 + lane] = 1.0
    return narrow(moves)


def rotate(real, imag, cosine, sine):
    return real * cosine - imag * sine, imag * cosine + real * sine


def row_forward_body(x_hbm, table_ref, twist_ref, order_ref, out_hbm, x_ref, turned_ref, out_ref, sems):
    loads = []
    for chan in range(4):
        loads.append(pltpu.make_async_copy(x_hbm.at[:, chan], x_ref.at[chan], sems.at[chan]))
        loads[-1].start()
    for chan in range(4):
        loads[chan].wait()
        turned_ref[chan * LANES : (chan + 1) * LANES, :] = lax.dot_general(
            order_ref[...],
            x_ref[chan].reshape(HALF, LANES),
            (((1,), (1,)), ((), ())),
            preferred_element_type=F32,
        ).astype(BF16)

    first = lax.broadcasted_iota(jnp.int32, (LANES, LANES), 1) < PER
    stores = []
    for block in range(BLOCKS):
        sums = jnp.dot(
            turned_ref[...], table_ref[:, block * 256 : (block + 1) * 256], preferred_element_type=F32
        )
        cosine, sine = twist_ref[0, block], twist_ref[1, block]
        for pair in range(2):
            upper = sums[pair * 256 : pair * 256 + 128]
            lower = sums[pair * 256 + 128 : pair * 256 + 256]
            real = jnp.where(first, upper[:, :LANES], lower[:, :LANES])
            imag = jnp.where(first, upper[:, LANES:], lower[:, LANES:])
            real, imag = rotate(real, imag, cosine, -sine)
            place = block if pair == 0 else 15 - block
            out_ref[place, 0] = real.astype(BF16)
            out_ref[place, 1] = imag.astype(BF16)
            stores.append(pltpu.make_async_copy(out_ref.at[place], out_hbm.at[place], sems.at[4 + place]))
            stores[-1].start()
    for copy in stores:
        copy.wait()


def row_forward(x, table, twist, order):
    anywhere = pl.BlockSpec(memory_space=pl.ANY)
    inside = pl.BlockSpec(memory_space=pltpu.VMEM)
    block = (16, 2, LANES, LANES)
    return pl.pallas_call(
        row_forward_body,
        in_specs=[anywhere, inside, inside, inside],
        out_specs=anywhere,
        out_shape=jax.ShapeDtypeStruct(block, BF16),
        scratch_shapes=[
            pltpu.VMEM((4, 8, 64, LANES), BF16),
            pltpu.VMEM((4 * LANES, HALF), BF16),
            pltpu.VMEM(block, BF16),
            pltpu.SemaphoreType.DMA((20,)),
        ],
        compiler_params=pltpu.CompilerParams(vmem_limit_bytes=16 * 1024 * 1024),
        cost_estimate=pl.CostEstimate(flops=1_100_000_000, bytes_accessed=5_000_000, transcendentals=0),
        name="row_forward",
    )(x, table, twist, order)


def filter_send_body(half_ref, spec_ref, out_ref):
    out_ref[...] = spec_ref[...].astype(BF16)


def filter_send(spec, half):
    return pl.pallas_call(
        filter_send_body,
        grid_spec=pltpu.PrefetchScalarGridSpec(
            num_scalar_prefetch=1,
            grid=(4,),
            in_specs=[pl.BlockSpec((1, 1, 64, COLS), lambda i, half: (i // 2, 2 * half[0] + i % 2, 0, 0))],
            out_specs=pl.BlockSpec((1, 1, 64, COLS), lambda i, half: (i // 2, i % 2, 0, 0)),
        ),
        out_shape=jax.ShapeDtypeStruct((2, 2, 64, COLS), BF16),
        compiler_params=pltpu.CompilerParams(vmem_limit_bytes=16 * 1024 * 1024),
        cost_estimate=pl.CostEstimate(flops=0, bytes_accessed=3_000_000, transcendentals=0),
        name="filter_send",
    )(half, spec)


def filter_body(half_ref, own_ref, got_ref, extra_ref, moves_ref, out_ref):
    for part in range(2):
        own = own_ref[part].reshape(LANES, own_ref.shape[3]).astype(BF16)
        total = None
        for source, low, high in ((own, 0, 128), (got_ref[part], 128, 256), (extra_ref[part], 256, 272)):
            term = lax.dot_general(
                source, moves_ref[low:high, :], (((0,), (0,)), ((), ())), preferred_element_type=F32
            )
            total = term if total is None else total + term
        out_ref[0, part] = total[:, :LANES].astype(BF16)
        out_ref[1, part] = total[:, LANES:].astype(BF16)


def filter_layout(spec, half, got, extra, moves):
    step = 512
    return pl.pallas_call(
        filter_body,
        grid_spec=pltpu.PrefetchScalarGridSpec(
            num_scalar_prefetch=1,
            grid=(COLS // step,),
            in_specs=[
                pl.BlockSpec((2, 2, 64, step), lambda i, half: (0, half[0], 0, i)),
                pl.BlockSpec((2, 128, step), lambda i, half: (0, 0, i)),
                pl.BlockSpec((2, 16, step), lambda i, half: (0, 0, i)),
                pl.BlockSpec((272, 256), lambda i, half: (0, 0)),
            ],
            out_specs=pl.BlockSpec((2, 2, step, LANES), lambda i, half: (0, 0, i, 0)),
        ),
        out_shape=jax.ShapeDtypeStruct((2, 2, COLS, LANES), BF16),
        compiler_params=pltpu.CompilerParams(vmem_limit_bytes=24 * 1024 * 1024),
        cost_estimate=pl.CostEstimate(flops=600_000_000, bytes_accessed=5_000_000, transcendentals=0),
        name="filter_layout",
    )(half, spec, got, extra, moves)


def column_body(
    y_hbm, turn_hbm, filt_hbm, step_hbm, mid_hbm, special_ref, out_hbm,
    y_ref, turn_ref, filt_ref, step_ref, mid_ref, work_ref, out_ref, sems,
):
    copies = []

    def fetch(source, target):
        copies.append(pltpu.make_async_copy(source, target, sems.at[len(copies)]))
        copies[-1].start()
        return copies[-1]

    step_copy = fetch(step_hbm, step_ref)
    in_copies = []
    for part in range(4):
        rows = pl.ds(part * 32, 32)
        in_copies.append(
            (
                fetch(y_hbm.at[:, :, rows], y_ref.at[:, :, rows]),
                fetch(turn_hbm.at[:, :, rows], turn_ref.at[:, :, rows]),
            )
        )
    mid_copies = []
    for part in range(2):
        rows = pl.ds(part * 1024, 1024)
        mid_copies.append(
            (
                fetch(mid_hbm.at[:, :, rows], mid_ref.at[:, :, rows]),
                fetch(filt_hbm.at[:, :, rows], filt_ref.at[:, :, rows]),
            )
        )

    special = special_ref[...] > 0.5
    step_copy.wait()

    def outer_forward(step):
        if step % 2 == 0:
            for copy in in_copies[step // 2]:
                copy.wait()
        rows = slice(step * 16, step * 16 + 16)
        parts = [[], [], [], []]
        for block in range(16):
            real = y_ref[block, 0, rows, :].astype(F32)
            imag = y_ref[block, 1, rows, :].astype(F32)
            parts[0].append(real)
            parts[1].append(jnp.where(special, 0.0, imag))
            parts[2].append(jnp.where(special, imag * turn_ref[0, block, rows, :], real))
            parts[3].append(jnp.where(special, imag * turn_ref[1, block, rows, :], imag))
        for side in range(2):
            data = [
                jnp.concatenate(
                    [x[half * 8 : half * 8 + 8] for x in parts[2 * side] + parts[2 * side + 1]], 0
                ).astype(BF16)
                for half in range(2)
            ]
            sums = jnp.dot(step_ref[side], jnp.concatenate(data, 1), preferred_element_type=F32)
            for part in range(2):
                for group in range(16):
                    for half in range(2):
                        at = group * LANES + step * 16 + half * 8
                        work_ref[2 * side + part, at : at + 8, :] = sums[
                            part * LANES + group * 8 : part * LANES + group * 8 + 8,
                            half * LANES : (half + 1) * LANES,
                        ]

    def inner_step(step):
        if step % 8 == 0:
            for copy in mid_copies[step // 8]:
                copy.wait()
        rows = slice(step * LANES, (step + 1) * LANES)
        sides = []
        for side in range(2):
            real, imag = rotate(
                work_ref[2 * side, rows, :],
                work_ref[2 * side + 1, rows, :],
                mid_ref[side, 0, rows, :],
                -mid_ref[side, 1, rows, :],
            )
            sides.append(jnp.concatenate([real.astype(BF16), imag.astype(BF16)], 0))
        spectrum = jnp.dot(step_ref[4], jnp.concatenate(sides, 1), preferred_element_type=F32)
        sides = []
        for side in range(2):
            lanes = slice(side * LANES, (side + 1) * LANES)
            real, imag = rotate(
                spectrum[:LANES, lanes],
                spectrum[LANES:, lanes],
                filt_ref[side, 0, rows, :].astype(F32),
                filt_ref[side, 1, rows, :].astype(F32),
            )
            sides.append(jnp.concatenate([real.astype(BF16), imag.astype(BF16)], 0))
        middle = jnp.dot(step_ref[5], jnp.concatenate(sides, 1), preferred_element_type=F32)
        for side in range(2):
            lanes = slice(side * LANES, (side + 1) * LANES)
            real, imag = rotate(
                middle[:LANES, lanes], middle[LANES:, lanes], mid_ref[side, 0, rows, :], mid_ref[side, 1, rows, :]
            )
            work_ref[2 * side, rows, :] = real
            work_ref[2 * side + 1, rows, :] = imag

    def outer_inverse(step):
        rows = slice(step * 16, step * 16 + 16)
        sums = []
        for side in range(2):
            data = []
            for half in range(2):
                pieces = []
                for part in range(2):
                    for group in range(16):
                        at = group * LANES + step * 16 + half * 8
                        pieces.append(work_ref[2 * side + part, at : at + 8, :])
                data.append(jnp.concatenate(pieces, 0).astype(BF16))
            sums.append(jnp.dot(step_ref[2 + side], jnp.concatenate(data, 1), preferred_element_type=F32))
        near, far = sums
        for block in range(16):

            def both(sums, part):
                at = part * LANES + block * 8
                return jnp.concatenate([sums[at : at + 8, :LANES], sums[at : at + 8, LANES:]], 0)

            near_re, near_im, far_re, far_im = both(near, 0), both(near, 1), both(far, 0), both(far, 1)
            cosine, sine = turn_ref[0, block, rows, :], turn_ref[1, block, rows, :]
            total_re, total_im = near_re + far_re, near_im + far_im
            real = jnp.where(special, near_re, total_re * cosine - total_im * sine)
            imag = jnp.where(special, far_re, total_im) * cosine + jnp.where(special, far_im, total_re) * sine
            out_ref[block, 0, rows, :] = real.astype(BF16)
            out_ref[block, 1, rows, :] = imag.astype(BF16)

    for step in range(8):
        outer_forward(step)
    for step in range(16):
        inner_step(step)
    out_copies = []
    for step in range(8):
        outer_inverse(step)
        if step % 2 == 1:
            rows = pl.ds((step - 1) * 16, 32)
            out_copies.append(fetch(out_ref.at[:, :, rows], out_hbm.at[:, :, rows]))
    for copy in out_copies:
        copy.wait()


def column_step(y, turns, filt, steps, mid, special):
    anywhere = pl.BlockSpec(memory_space=pl.ANY)
    block = (16, 2, LANES, LANES)
    return pl.pallas_call(
        column_body,
        in_specs=[anywhere] * 5 + [pl.BlockSpec(memory_space=pltpu.VMEM)],
        out_specs=anywhere,
        out_shape=jax.ShapeDtypeStruct(block, BF16),
        scratch_shapes=[
            pltpu.VMEM(block, BF16),
            pltpu.VMEM((2, 16, LANES, LANES), F32),
            pltpu.VMEM((2, 2, COLS, LANES), BF16),
            pltpu.VMEM((6, 256, 256), BF16),
            pltpu.VMEM((2, 2, COLS, LANES), F32),
            pltpu.VMEM((4, COLS, LANES), F32),
            pltpu.VMEM(block, BF16),
            pltpu.SemaphoreType.DMA((17,)),
        ],
        compiler_params=pltpu.CompilerParams(vmem_limit_bytes=60 * 1024 * 1024),
        cost_estimate=pl.CostEstimate(flops=2_000_000_000, bytes_accessed=10_000_000, transcendentals=0),
        name="column_step",
    )(y, turns, filt, steps, mid, special)


def row_inverse_body(z_ref, table_ref, order_ref, out_ref, split_ref):
    first = lax.broadcasted_iota(jnp.int32, (LANES, LANES), 1) < PER
    for place in range(16):
        pair, block = (0, place) if place < 8 else (1, 15 - place)
        for part in range(2):
            values = z_ref[place, part]
            lanes = slice((block * 2 + part) * LANES, (block * 2 + part + 1) * LANES)
            zero = jnp.zeros_like(values)
            split_ref[pair * 256 : pair * 256 + 128, lanes] = jnp.where(first, values, zero)
            split_ref[pair * 256 + 128 : pair * 256 + 256, lanes] = jnp.where(first, zero, values)

    for chan in range(4):
        sums = lax.dot_general(
            table_ref[...],
            split_ref[chan * LANES : (chan + 1) * LANES, :],
            (((1,), (1,)), ((), ())),
            preferred_element_type=F32,
        ) * (1.0 / TOTAL)
        sums = jnp.dot(sums.astype(BF16), order_ref[...], preferred_element_type=F32).astype(BF16)
        for row in range(8):
            out_ref[row, chan] = sums[row * 64 : (row + 1) * 64]


def row_inverse(z, table, order):
    inside = pl.BlockSpec(memory_space=pltpu.VMEM)
    return pl.pallas_call(
        row_inverse_body,
        in_specs=[inside] * 3,
        out_specs=inside,
        out_shape=jax.ShapeDtypeStruct((8, 4, 64, LANES), BF16),
        scratch_shapes=[pltpu.VMEM((4 * LANES, COLS), BF16)],
        compiler_params=pltpu.CompilerParams(vmem_limit_bytes=16 * 1024 * 1024),
        cost_estimate=pl.CostEstimate(flops=1_100_000_000, bytes_accessed=4_000_000, transcendentals=0),
        name="row_inverse",
    )(z, table, order)


def turn(first, second, modulus):
    angle = ((first * second) % modulus).astype(F32) * (TWO_PI / modulus)
    return jnp.stack([jnp.cos(angle), jnp.sin(angle)])


def per_device(gate_out, gate_in, values, filter_spec, skip):
    col = lax.axis_index("col")
    low_side = col < 8
    table = jnp.asarray(row_table())

    order = jnp.asarray(place_moves())

    half = jnp.where(low_side, 0, 1).astype(jnp.int32)[None]
    other = filter_send(filter_spec, 1 - half)
    got = lax.ppermute(other, "col", [(i, 15 - i) for i in range(16)])

    gated = gate_in.astype(F32) * values.astype(F32)
    x = lax.all_to_all(gated.astype(BF16), "row", split_axis=0, concat_axis=0, tiled=True)

    extra_low = lax.ppermute(other[:, :, 0, :], "col", [(i, (16 - i) % 8) for i in range(8, 16)])
    extra_high = lax.ppermute(
        filter_spec[:, 2:, 0, :].astype(BF16), "col", [(i, 8 + (i - 1) % 8) for i in range(8, 16)]
    )
    extra = jnp.pad(jnp.where(low_side, extra_low, extra_high), ((0, 0), (0, 14), (0, 0)))
    moves = jnp.where(low_side, filter_moves()[0], filter_moves()[1])
    filt = filter_layout(filter_spec, half, got.reshape(2, 128, COLS), extra, moves)

    lane = jnp.arange(LANES, dtype=jnp.int32) % PER
    all_k1 = (PER * jnp.arange(BLOCKS, dtype=jnp.int32))[:, None, None] + lane[None, None, :]
    base = jnp.asarray(twist_base())
    phase = turn(all_k1, col, ROWS * 16)
    twist = jnp.stack(rotate(base[0], base[1], phase[0], phase[1]))
    y = row_forward(x.reshape(8, 4, 64, LANES), table, twist, order)
    y = lax.all_to_all(y, "col", split_axis=0, concat_axis=0, tiled=True)

    own_k1 = PER * jnp.where(low_side, col, 15 - col) + lane
    special = own_k1 == 0
    turn_k1 = jnp.where(special, -HALF, own_k1)
    within = turn(jnp.asarray(place_order(), jnp.int32)[:, None], turn_k1[None, :], TOTAL)[:, None]
    between = turn(jnp.arange(16, dtype=jnp.int32)[:, None, None], turn_k1[None, None, :], ROWS * 16)
    turns = jnp.stack(rotate(within[0], within[1], between[0], between[1]))
    z = column_step(
        y, turns, filt, jnp.asarray(step_tables()), jnp.asarray(middle_tables()), special.astype(F32)[None, :]
    )
    z = lax.all_to_all(z, "col", split_axis=0, concat_axis=0, tiled=True)

    convolved = row_inverse(z, table, order).reshape(32, 64, LANES)
    convolved = lax.all_to_all(convolved, "row", split_axis=0, concat_axis=0, tiled=True)
    return gate_out.astype(F32) * (convolved.astype(F32) + skip[:, None, None] * gated)


def solution(mesh):
    return jax.shard_map(
        per_device,
        mesh=mesh,
        in_specs=(
            P(None, "row", "col"),
            P(None, "row", "col"),
            P(None, "row", "col"),
            P(None, "row", "col", None),
            P(),
        ),
        out_specs=P(None, "row", "col"),
        check_vma=False,
    )
```

time: 138 us -> 110 us (0.80)
  waiting for transfers between devices: 29.8 us -> 14.9 us
  Pallas kernels: 35.3 us -> 22.1 us
  local copies, waits for them, and re-layouts: 16.3 us -> 4.99 us
  other arithmetic: 3.48 us -> 9.29 us
  starting transfers between devices: 17.7 us -> 20.7 us
  blocking collectives: 34.5 us -> 36.9 us
    all_to_all x1, waiting for transfers between devices: 19.8 us -> 0.01 us  [per_device(): lax.all_to_all(gated.astype(BF16), 'row', split_axis=0, concat_axis=0, ti...]
    pallas_call x4 -> x5, Pallas kernels: 35.3 us -> 22.1 us  [the longest x1 7.94 us: column_step(): pl.pallas_call(column_body, in_specs=[anywhere] * 5 + [pl.BlockSpec(memor...]
    unnamed x41 -> x32, local copies, waits for them, and re-layouts: 12.5 us -> 4 us
    ppermute x1, waiting for transfers between devices: 0.01 us -> 7.01 us  [per_device(): lax.ppermute(other[:, :, 0, :], 'col', [(i, (16 - i) % 8) for i in range(...]
    all_to_all x1, starting transfers between devices: 4.49 us -> 8.41 us  [per_device(): y = lax.all_to_all(y, 'col', split_axis=0, concat_axis=0, tiled=True)]
    convert_element_type x2 -> x0, local copies, waits for them, and re-layouts: 3.7 us -> none  [the longest x1 3.67 us: per_device(): lax.dynamic_slice_in_dim(filter_spec, 2 - mine, 2, axis=1).astype(BF16)]
    all_to_all x1, waiting for transfers between devices: 9.98 us -> 6.52 us  [per_device(): y = lax.all_to_all(y, 'col', split_axis=0, concat_axis=0, tiled=True)]
    another operation x3 -> x2, other arithmetic: 0.02 us -> 2.96 us  [the longest x1 2.89 us: per_device(): turns = jnp.stack(rotate(within[0], within[1], between[0], between[1]))]
  transfers between devices with their start and end apart: 5 -> 5, of which waited for: 2 -> 3; matrix products, arithmetic and copies ran while one was open for 4% -> 6% of each run, Pallas kernels for 6% -> 8%
where the time goes in v1:
time: 110 us; the launch traced here: 109 us
  blocking collectives  36.9 us (34%)
  Pallas kernels  22.1 us (20%)
  starting transfers between devices  20.7 us (19%)
  waiting for transfers between devices  14.9 us (14%)
  other arithmetic  9.29 us (8%)
  local copies, waits for them, and re-layouts  4.99 us (5%)
    all_to_all x1, blocking collectives, per_device(): z = lax.all_to_all(z, 'col', split_axis=0, concat_axis=0, tiled=True)  20.3 us
    all_to_all x1, blocking collectives, per_device(): lax.all_to_all(convolved, 'row', split_axis=0, concat_axis=0, tiled=True)  16.5 us
    all_to_all x1, starting transfers between devices, per_device(): y = lax.all_to_all(y, 'col', split_axis=0, concat_axis=0, tiled=True)  8.41 us
    pallas_call x1, Pallas kernels, column_step(): pl.pallas_call(column_body, in_specs=[anywhere] * 5 + [pl.BlockSpec(memor...  7.94 us
    all_to_all x1, starting transfers between devices, per_device(): lax.all_to_all(gated.astype(BF16), 'row', split_axis=0, concat_axis=0, ti...  7.01 us
    ppermute x1, waiting for transfers between devices, per_device(): lax.ppermute(other[:, :, 0, :], 'col', [(i, (16 - i) % 8) for i in range(...  7.01 us
    all_to_all x1, waiting for transfers between devices, per_device(): y = lax.all_to_all(y, 'col', split_axis=0, concat_axis=0, tiled=True)  6.52 us
    pallas_call x1, Pallas kernels, row_inverse(): pl.pallas_call(row_inverse_body, in_specs=[inside] * 3, out_specs=inside,...  5.03 us
  transfers between devices with their start and end apart: 5, of which 3 were waited for; matrix products, arithmetic and copies ran while one was open for 6% of the time, Pallas kernels for 8%

profile of v1, /device:TPU:0, one launch (start us, length us, event | category | flops | bytes accessed | tf_op | source)
XLA Modules:
  0.0 109.2 jit_solution(14330082230906928588)
XLA Ops:
  0.0 2.2 %fusion = bf16[32,64,128]{2,1,0:T(8,128)(2,1)} fusion(bf16[32,64,128]{2,1,0:T(8,128)(2,1)} %param.15, bf16[32,64,128]{2,1,0:T(8,128)(2,1)} %param.14), kind=kLoop, calls=%fused_computation.6 | loop fusion | flops 1048576 | bytes 1572864 | tf_op jit(solution)/shard_map/convert_element_type | solution.py:451
  2.2 7.0 %all-to-all-start = ((bf16[32,64,128]{2,1,0:T(8,128)(2,1)}), bf16[32,64,128]{2,1,0:T(8,128)(2,1)}, u32[]{:S(2)}, u32[]{:S(2)}) async-start(bf16[32,64,128]{2,1,0:T(8,128)(2,1)} %fusion), calls=%async_computation | async-start | bytes 1048576 | tf_op jit(solution)/shard_map/all_to_all | solution.py:451
  9.2 2.2 %copy-done = f32[2,4,64,2048]{3,2,1,0:T(8,128)S(1)} copy-done((f32[2,4,64,2048]{3,2,1,0:T(8,128)S(1)}, f32[2,4,64,2048]{3,2,1,0:T(8,128)}, u32[]{:S(2)}) %copy-start) | copy-done | bytes 4194328
  11.4 1.6 %filter_send.1 = bf16[2,2,64,2048]{3,2,1,0:T(8,128)(2,1)} custom-call(s32[1]{0:T(128)S(6)} %sub.23.half_ref, f32[2,4,64,2048]{3,2,1,0:T(8,128)S(1)} %copy-done), custom_call_target="tpu_custom_call" | custom-call | bytes 3000000 | tf_op jit(solution)/shard_map/filter_send/pallas_call | solution.py:183
  12.9 3.3 %collective-permute-start = (bf16[2,2,64,2048]{3,2,1,0:T(8,128)(2,1)}, bf16[2,2,64,2048]{3,2,1,0:T(8,128)(2,1)}, u32[]{:S(2)}, u32[]{:S(2)}) collective-permute-start(bf16[2,2,64,2048]{3,2,1,0:T(8,128)(2,1)} %filter_send.1), channel_id=1, source_target_pairs={{0,15},{1,14},{2,13},{3,12},{4,11},{5,10},{6,9},{7,8},{8,7},{9,6},... | collective-permute-start | bytes 3145736 | tf_op jit(solution)/shard_map/ppermute | solution.py:448
  16.3 1.0 slice.21
  17.2 1.3 %collective-permute-start.1 = (bf16[2,2,2048]{2,1,0:T(2,128)(2,1)S(1)}, bf16[2,2,2048]{2,1,0:T(2,128)(2,1)S(1)}, u32[]{:S(2)}, u32[]{:S(2)}) collective-permute-start(bf16[2,2,2048]{2,1,0:T(2,128)(2,1)S(1)} %bitcast.11), channel_id=1, source_target_pairs={{8,0},{9,7},{10,6},{11,5},{12,4},{13,3},{14,2},{15,1},{24,16},{25,... | collective-permute-start | bytes 49160 | tf_op jit(solution)/shard_map/ppermute | solution.py:453
  18.6 0.7 collective-permute-start.2
  19.3 0.1 fusion.19
  19.4 0.3 fusion.5
  19.8 0.1 multiply_subtract_fusion.1
  19.9 0.1 fusion.17
  20.0 0.0 copy-start.3
  20.0 0.0 copy-start.4
  20.0 0.1 pad_maximum_fusion.1.twist_ref
  20.1 1.6 %multiply_subtract_fusion = (f32[1,16,128,128]{3,2,1,0:T(8,128)}, f32[1,16,128,128]{3,2,1,0:T(8,128)}) fusion(f32[16,128]{1,0:T(8,128)S(1)} %get-tuple-element.14, f32[128,128]{1,0:T(8,128)S(1)} %get-tuple-element.10, f32[16,128]{1,0:T(8,128)S(1)} %get-tuple-element.13, f32[128,128]{1,0:T(8,128)S(1)} %get-tuple-element.9), kind=kLoop, calls=%fused_computation.4 | loop fusion | flops 1572864 | bytes 2244608 | tf_op jit(solution)/shard_map/sub | solution.py:118
  21.7 0.4 copy-done.3
  22.2 3.6 %row_forward.1 = bf16[16,2,128,128]{3,2,1,0:T(8,128)(2,1)} custom-call(bf16[8,4,64,128]{3,2,1,0:T(8,128)(2,1)} %bitcast.x_hbm, bf16[512,2048]{1,0:T(8,128)(2,1)S(1)} %copy-done.3, f32[2,8,128,128]{3,2,1,0:T(8,128)S(1)} %pad_maximum_fusion.1.twist_ref, bf16[128,128]{1,0:T(8,128)(2,1)S(1)} %copy-done.4), custom_call_target="tpu_custom_call" | custom-call | flops 1100000000 | bytes 5000000 | tf_op jit(solution)/shard_map/row_forward/pallas_call | solution.py:161
  25.8 0.0 copy-start.11
  25.9 8.4 %all-to-all-start.1 = ((bf16[16,2,128,128]{3,2,1,0:T(8,128)(2,1)}), bf16[16,2,128,128]{3,2,1,0:T(8,128)(2,1)}, u32[]{:S(2)}, u32[]{:S(2)}) async-start(bf16[16,2,128,128]{3,2,1,0:T(8,128)(2,1)} %row_forward.1), calls=%async_computation.1 | async-start | bytes 2097152 | tf_op jit(solution)/shard_map/all_to_all | solution.py:467
  34.3 2.9 %pad_maximum_fusion.turn_hbm = f32[2,16,128,128]{3,2,1,0:T(8,128)} fusion(f32[1,16,128,128]{3,2,1,0:T(8,128)} %get-tuple-element.8, f32[1,16,128,128]{3,2,1,0:T(8,128)S(1)} %copy-done.5), kind=kLoop, calls=%fused_computation | loop fusion | flops 524288 | bytes 4194304 | tf_op jit(solution)/shard_map/stack | solution.py:474
  37.2 0.5 compare_convert_fusion.special_ref
  37.7 7.0 %collective-permute-done.1 = bf16[2,2,2048]{2,1,0:T(2,128)(2,1)S(1)} collective-permute-done((bf16[2,2,2048]{2,1,0:T(2,128)(2,1)S(1)}, bf16[2,2,2048]{2,1,0:T(2,128)(2,1)S(1)}, u32[]{:S(2)}, u32[]{:S(2)}) %collective-permute-start.1) | collective-permute-done | bytes 16416 | tf_op jit(solution)/shard_map/ppermute | solution.py:453
  44.8 1.4 %collective-permute-done = bf16[2,2,64,2048]{3,2,1,0:T(8,128)(2,1)} collective-permute-done((bf16[2,2,64,2048]{3,2,1,0:T(8,128)(2,1)}, bf16[2,2,64,2048]{3,2,1,0:T(8,128)(2,1)}, u32[]{:S(2)}, u32[]{:S(2)}) %collective-permute-start) | collective-permute-done | bytes 1048608 | tf_op jit(solution)/shard_map/ppermute | solution.py:448
  46.2 4.0 %filter_layout.1.filt_hbm = bf16[2,2,2048,128]{3,2,1,0:T(8,128)(2,1)S(1)} custom-call(s32[1]{0:T(128)} %bitcast.1.half_ref, f32[2,4,64,2048]{3,2,1,0:T(8,128)S(1)} %copy-done.1, bf16[2,128,2048]{2,1,0:T(8,128)(2,1)} %bitcast.2.got_ref, bf16[2,16,2048]{2,1,0:T(8,128)(2,1)S(1)} %pad.4.extra_ref, bf16[272,256]{1,0:T(8,128)(2,1)S(1)} %broadcast_select_fusion.moves_ref), custom_call_target="tpu_custom_call" | custom-call | flops 600000000 | bytes 5000000 | tf_op jit(solution)/shard_map/filter_layout/pallas_call | solution.py:213
  50.2 1.3 %copy-done.2 = bf16[2,2,2048,128]{3,2,1,0:T(8,128)(2,1)} copy-done((bf16[2,2,2048,128]{3,2,1,0:T(8,128)(2,1)}, bf16[2,2,2048,128]{3,2,1,0:T(8,128)(2,1)S(1)}, u32[]{:S(2)}) %copy-start.2) | copy-done | bytes 2097176
  51.4 6.5 %all-to-all-done.1.y_hbm = bf16[16,2,128,128]{3,2,1,0:T(8,128)(2,1)} async-done(((bf16[16,2,128,128]{3,2,1,0:T(8,128)(2,1)}), bf16[16,2,128,128]{3,2,1,0:T(8,128)(2,1)}, u32[]{:S(2)}, u32[]{:S(2)}) %all-to-all-start.1) | async-done | bytes 1048608 | tf_op jit(solution)/shard_map/all_to_all | solution.py:467
  58.0 7.9 %column_step.1 = bf16[16,2,128,128]{3,2,1,0:T(8,128)(2,1)} custom-call(bf16[16,2,128,128]{3,2,1,0:T(8,128)(2,1)} %all-to-all-done.1.y_hbm, f32[2,16,128,128]{3,2,1,0:T(8,128)} %pad_maximum_fusion.turn_hbm, bf16[2,2,2048,128]{3,2,1,0:T(8,128)(2,1)} %copy-done.2, bf16[6,256,256]{2,1,0:T(8,128)(2,1)} %constant.101.clone.step_hbm, ...), custom_call_target="tpu_custom_call" | custom-call | flops 2000000000 | bytes 10000000 | tf_op jit(solution)/shard_map/column_step/pallas_call | solution.py:376
  65.9 20.3 %all_to_all.20.z_ref = bf16[16,2,128,128]{3,2,1,0:T(8,128)(2,1)S(1)} all-to-all(bf16[16,2,128,128]{3,2,1,0:T(8,128)(2,1)} %column_step.1), channel_id=1, replica_groups=mesh['row'=8,'col'=16] {'col'}, dimensions={0} | all-to-all | bytes 2097152 | tf_op jit(solution)/shard_map/all_to_all | solution.py:478
  86.3 5.0 %row_inverse.1 = bf16[8,4,64,128]{3,2,1,0:T(8,128)(2,1)S(1)} custom-call(bf16[16,2,128,128]{3,2,1,0:T(8,128)(2,1)S(1)} %all_to_all.20.z_ref, bf16[512,2048]{1,0:T(8,128)(2,1)S(1)} %copy-done.3, bf16[128,128]{1,0:T(8,128)(2,1)S(1)} %copy-done.4), custom_call_target="tpu_custom_call" | custom-call | flops 1100000000 | bytes 4000000 | tf_op jit(solution)/shard_map/row_inverse/pallas_call | solution.py:422
  91.3 16.5 %all_to_all.21 = bf16[32,64,128]{2,1,0:T(8,128)(2,1)S(1)} all-to-all(bf16[32,64,128]{2,1,0:T(8,128)(2,1)S(1)} %bitcast.10), channel_id=1, replica_groups=mesh['row'=8,'col'=16] {'row'}, dimensions={0} | all-to-all | bytes 1048576 | tf_op jit(solution)/shard_map/all_to_all | solution.py:481
  107.9 1.3 %add_multiply_fusion = f32[32,64,128]{2,1,0:T(8,128)} fusion(bf16[32,64,128]{2,1,0:T(8,128)(2,1)S(1)} %all_to_all.21, bf16[32,64,128]{2,1,0:T(8,128)(2,1)S(1)} %copy-done.8, bf16[32,64,128]{2,1,0:T(8,128)(2,1)S(1)} %copy-done.6, bf16[32,64,128]{2,1,0:T(8,128)(2,1)S(1)} %copy-done.7, f32[32]{0:T(128)S(1)} %copy-done.14), kind=kLoop, calls=%fused_computation.2 | loop fusion | flops 2097152 | bytes 3145856 | tf_op jit(solution)/shard_map/mul | solution.py:482
  (35 shorter events, 0.2 us)
Async XLA Ops:
  2.2 19.6 %all-to-all-start = ((bf16[32,64,128]{2,1,0:T(8,128)(2,1)}), bf16[32,64,128]{2,1,0:T(8,128)(2,1)}, u32[]{:S(2)}, u32[]{:S(2)}) async-start(bf16[32,64,128]{2,1,0:T(8,128)(2,1)} %fusion), calls=%async_computation | async-start | bytes 1048576 | tf_op jit(solution)/shard_map/all_to_all | solution.py:451
  9.2 2.2 %copy-start = (f32[2,4,64,2048]{3,2,1,0:T(8,128)S(1)}, f32[2,4,64,2048]{3,2,1,0:T(8,128)}, u32[]{:S(2)}) copy-start(f32[2,4,64,2048]{3,2,1,0:T(8,128)} %own_ref.1) | copy-start | bytes 12582916
  11.4 8.0 %copy-start.13 = (s32[128]{0:T(128)S(1)}, s32[128]{0:T(128)}, u32[]{:S(2)}) copy-start(s32[128]{0:T(128)} %constant.100.clone) | copy-start | bytes 1540
  11.4 8.4 %copy-start.9 = (f32[1,8,128,128]{3,2,1,0:T(8,128)S(1)}, f32[1,8,128,128]{3,2,1,0:T(8,128)}, u32[]{:S(2)}) copy-start(f32[1,8,128,128]{3,2,1,0:T(8,128)} %constant.107) | copy-start | bytes 1572868
  11.4 8.4 %copy-start.10 = (f32[1,8,128,128]{3,2,1,0:T(8,128)S(1)}, f32[1,8,128,128]{3,2,1,0:T(8,128)}, u32[]{:S(2)}) copy-start(f32[1,8,128,128]{3,2,1,0:T(8,128)} %constant.106) | copy-start | bytes 1572868
  12.9 33.2 %collective-permute-start = (bf16[2,2,64,2048]{3,2,1,0:T(8,128)(2,1)}, bf16[2,2,64,2048]{3,2,1,0:T(8,128)(2,1)}, u32[]{:S(2)}, u32[]{:S(2)}) collective-permute-start(bf16[2,2,64,2048]{3,2,1,0:T(8,128)(2,1)} %filter_send.1), channel_id=1, source_target_pairs={{0,15},{1,14},{2,13},{3,12},{4,11},{5,10},{6,9},{7,8},{8,7},{9,6},... | collective-permute-start | bytes 3145736 | tf_op jit(solution)/shard_map/ppermute | solution.py:448
  17.2 27.5 %collective-permute-start.1 = (bf16[2,2,2048]{2,1,0:T(2,128)(2,1)S(1)}, bf16[2,2,2048]{2,1,0:T(2,128)(2,1)S(1)}, u32[]{:S(2)}, u32[]{:S(2)}) collective-permute-start(bf16[2,2,2048]{2,1,0:T(2,128)(2,1)S(1)} %bitcast.11), channel_id=1, source_target_pairs={{8,0},{9,7},{10,6},{11,5},{12,4},{13,3},{14,2},{15,1},{24,16},{25,... | collective-permute-start | bytes 49160 | tf_op jit(solution)/shard_map/ppermute | solution.py:453
  18.6 26.2 %collective-permute-start.2 = (bf16[2,2,2048]{2,1,0:T(2,128)(2,1)S(1)}, bf16[2,2,2048]{2,1,0:T(2,128)(2,1)S(1)}, u32[]{:S(2)}, u32[]{:S(2)}) collective-permute-start(bf16[2,2,2048]{2,1,0:T(2,128)(2,1)S(1)} %bitcast.12), channel_id=1, source_target_pairs={{8,15},{9,8},{10,9},{11,10},{12,11},{13,12},{14,13},{15,14},{24,31... | collective-permute-start | bytes 49160 | tf_op jit(solution)/shard_map/ppermute | solution.py:454
  20.0 2.2 %copy-start.3 = (bf16[512,2048]{1,0:T(8,128)(2,1)S(1)}, bf16[512,2048]{1,0:T(8,128)(2,1)}, u32[]{:S(2)}) copy-start(bf16[512,2048]{1,0:T(8,128)(2,1)} %constant.95.clone.table_ref) | copy-start | bytes 6291460
  20.0 2.2 %copy-start.4 = (bf16[128,128]{1,0:T(8,128)(2,1)S(1)}, bf16[128,128]{1,0:T(8,128)(2,1)}, u32[]{:S(2)}) copy-start(bf16[128,128]{1,0:T(8,128)(2,1)} %constant.96.clone.order_ref) | copy-start | bytes 98308
  25.8 8.5 %copy-start.5 = (f32[1,16,128,128]{3,2,1,0:T(8,128)S(1)}, f32[1,16,128,128]{3,2,1,0:T(8,128)}, u32[]{:S(2)}) copy-start(f32[1,16,128,128]{3,2,1,0:T(8,128)} %get-tuple-element.7) | copy-start | bytes 3145732
  25.8 11.4 %copy-start.11 = (bf16[272,256]{1,0:T(8,128)(2,1)S(1)}, bf16[272,256]{1,0:T(8,128)(2,1)}, u32[]{:S(2)}) copy-start(bf16[272,256]{1,0:T(8,128)(2,1)} %constant.97.clone) | copy-start | bytes 417796
  25.9 11.3 %copy-start.12 = (bf16[272,256]{1,0:T(8,128)(2,1)S(1)}, bf16[272,256]{1,0:T(8,128)(2,1)}, u32[]{:S(2)}) copy-start(bf16[272,256]{1,0:T(8,128)(2,1)} %constant.98.clone) | copy-start | bytes 417796
  25.9 32.1 %all-to-all-start.1 = ((bf16[16,2,128,128]{3,2,1,0:T(8,128)(2,1)}), bf16[16,2,128,128]{3,2,1,0:T(8,128)(2,1)}, u32[]{:S(2)}, u32[]{:S(2)}) async-start(bf16[16,2,128,128]{3,2,1,0:T(8,128)(2,1)} %row_forward.1), calls=%async_computation.1 | async-start | bytes 2097152 | tf_op jit(solution)/shard_map/all_to_all | solution.py:467
  34.3 11.9 %copy-start.1 = (f32[2,4,64,2048]{3,2,1,0:T(8,128)S(1)}, f32[2,4,64,2048]{3,2,1,0:T(8,128)}, u32[]{:S(2)}) copy-start(f32[2,4,64,2048]{3,2,1,0:T(8,128)} %own_ref.1) | copy-start | bytes 12582916
  50.1 1.3 %copy-start.2 = (bf16[2,2,2048,128]{3,2,1,0:T(8,128)(2,1)}, bf16[2,2,2048,128]{3,2,1,0:T(8,128)(2,1)S(1)}, u32[]{:S(2)}) copy-start(bf16[2,2,2048,128]{3,2,1,0:T(8,128)(2,1)S(1)} %filter_layout.1.filt_hbm) | copy-start | bytes 6291460
  86.3 21.6 %copy-start.6 = (bf16[32,64,128]{2,1,0:T(8,128)(2,1)S(1)}, bf16[32,64,128]{2,1,0:T(8,128)(2,1)}, u32[]{:S(2)}) copy-start(bf16[32,64,128]{2,1,0:T(8,128)(2,1)} %param.15) | copy-start | bytes 1572868
  86.3 21.6 %copy-start.7 = (bf16[32,64,128]{2,1,0:T(8,128)(2,1)S(1)}, bf16[32,64,128]{2,1,0:T(8,128)(2,1)}, u32[]{:S(2)}) copy-start(bf16[32,64,128]{2,1,0:T(8,128)(2,1)} %param.14) | copy-start | bytes 1572868
  86.3 21.6 %copy-start.8 = (bf16[32,64,128]{2,1,0:T(8,128)(2,1)S(1)}, bf16[32,64,128]{2,1,0:T(8,128)(2,1)}, u32[]{:S(2)}) copy-start(bf16[32,64,128]{2,1,0:T(8,128)(2,1)} %param.13) | copy-start | bytes 1572868
  86.3 21.6 %copy-start.14 = (f32[32]{0:T(128)S(1)}, f32[32]{0:T(128)}, u32[]{:S(2)}) copy-start(f32[32]{0:T(128)} %param.17) | copy-start | bytes 388

commit v2 on v1

v2 whole, which is shorter than its diff:
```python
import functools
import math

import jax
import jax.numpy as jnp
import ml_dtypes
import numpy as np
from jax import lax
from jax.experimental import pallas as pl
from jax.experimental.pallas import tpu as pltpu
from jax.sharding import PartitionSpec as P

ROWS = 1024
COLS = 2048
OUTER = 64
INNER = 32
HALF = ROWS // 2
TOTAL = ROWS * COLS
LANES = 128
BLOCKS = 8
PER = HALF // BLOCKS
TWO_PI = 2.0 * math.pi
BF16 = jnp.bfloat16
F32 = jnp.float32


def grid_angle(first, second, modulus):
    product = (np.asarray(first, np.int64)[:, None] * np.asarray(second, np.int64)[None, :]) % modulus
    return product.astype(np.float32) * np.float32(TWO_PI / modulus)


def narrow(array):
    return np.asarray(array, np.float32).astype(ml_dtypes.bfloat16)


def row_table():
    angle = grid_angle(np.arange(HALF), np.arange(HALF), ROWS)
    cosines, sines = np.cos(angle), -np.sin(angle)
    sines[:, 0] = 1.0 - 2.0 * (np.arange(HALF) % 2)
    parts = np.stack([cosines, sines], 0).reshape(2, HALF, BLOCKS, PER).transpose(1, 2, 0, 3)
    return narrow(np.repeat(parts[:, :, :, None, :], 2, 3).reshape(HALF, BLOCKS * 2 * 2 * PER))


def pair_order(table, first, second):
    rows, cols = table.shape[0] // 2, table.shape[1] // 2
    out = np.zeros((2, rows // first, 2, first, 2, cols // second, 2, second), np.float32)
    for which in range(2):
        out[:, :, which, :, :, :, which, :] = table.reshape(2, rows // first, first, 2, cols // second, second)
    return out.reshape(4 * rows, 4 * cols)


def outer_tables():
    near = grid_angle(np.arange(OUTER), np.arange(OUTER), OUTER)
    far = grid_angle(np.arange(OUTER) + 1, np.arange(OUTER), OUTER)
    c, s, cm, sm = np.cos(near), np.sin(near), np.cos(far), np.sin(far)
    return [
        pair_order(np.block([[c, s], [-s, c]]), 1, 4),
        pair_order(np.block([[cm, -sm], [-sm, -cm]]), 1, 4),
        pair_order(np.block([[c.T, -s.T], [s.T, c.T]]), 4, 1),
        pair_order(np.block([[cm.T, -sm.T], [-sm.T, -cm.T]]), 4, 1),
    ]


def inner_tables():
    angle = grid_angle(np.arange(INNER), np.arange(INNER), INNER)
    c, s = np.cos(angle), np.sin(angle)
    spread = np.zeros((2, 4, INNER, 2, INNER // 2, 4, 2), np.float32)
    for k in range(4):
        spread[:, k, :, :, :, k, :] = np.block([[c, s], [-s, c]]).reshape(2, INNER, 2, INNER // 2, 2)
    spread = spread.reshape(256, 256)
    return [spread, spread.T]


def step_tables():
    return narrow(np.stack(outer_tables() + inner_tables()))


def middle_tables():
    angle = grid_angle(np.arange(OUTER + 1), np.arange(INNER), COLS)
    sides = []
    for side in range(2):
        own = angle[side : side + OUTER].reshape(16, 4, 16, 2).transpose(0, 2, 1, 3).reshape(COLS, 1)
        own = np.pad(own.reshape(16, LANES).T, ((0, 0), (0, LANES - 16)))
        sides.append(np.stack([np.cos(own), np.sin(own)]))
    return np.stack(sides).astype(np.float32)


def place_order():
    return np.arange(LANES).reshape(4, INNER).T.reshape(-1)


def place_moves():
    return narrow(np.eye(LANES)[place_order()])


def twist_base():
    angle = grid_angle(place_order(), np.arange(PER), TOTAL)
    steps = np.pad(grid_angle(place_order(), PER * np.arange(BLOCKS), TOTAL), ((0, 0), (0, LANES - BLOCKS)))
    own = np.concatenate([np.cos(angle), np.sin(angle)], 1)
    return np.stack([own, np.cos(steps), np.sin(steps)]).astype(np.float32)


def filter_moves():
    moves = np.zeros((2, 2, 272, 256), np.float32)
    for copy in range(2):
        for e in range(PER):
            here, there, lane = copy * PER + e, copy * PER + (PER - e) % PER, copy * PER + e
            moves[0, :, here, lane] = 1.0
            moves[1, :, there, LANES + lane] = 1.0
            if e > 0:
                moves[0, :, LANES + there, LANES + lane] = 1.0
                moves[1, :, LANES + here, lane] = 1.0
            else:
                for part in range(2):
                    moves[0, part, 256 + 2 * part + copy, LANES + lane] = 1.0
                    moves[1, part, 256 + 2 * part + copy, lane] = 1.0
    return narrow(moves)


def rotate(real, imag, cosine, sine):
    return real * cosine - imag * sine, imag * cosine + real * sine


def filter_send_body(part, *refs):
    if part == 0:
        half_ref, spec_hbm, send_hbm, rows_ref, wide_ref, narrow_ref, in_sems, out_sems, lead_ref = refs
    else:
        half_ref, spec_hbm, ahead_ref, send_hbm, wide_ref, narrow_ref, in_sems, out_sems = refs
    away = 2 * (1 - half_ref[0])
    loads, stores = [], []

    def load(source, target):
        loads.append(pltpu.make_async_copy(source, target, in_sems.at[len(loads)]))
        loads[-1].start()

    for chan in range(2):
        for cut in range(2):
            rows = pl.ds(cut * 32, 32)
            load(spec_hbm.at[part, away + chan, rows], wide_ref.at[chan, rows])
            stores.append(
                pltpu.make_async_copy(
                    narrow_ref.at[chan, rows], send_hbm.at[chan, rows], out_sems.at[2 * chan + cut]
                )
            )
    if part == 0:
        for chan in range(2):
            load(spec_hbm.at[1, away + chan, pl.ds(0, 8)], lead_ref.at[chan])
    for chan in range(2):
        for cut in range(2):
            rows = pl.ds(cut * 32, 32)
            loads[2 * chan + cut].wait()
            narrow_ref[chan, rows] = wide_ref[chan, rows].astype(BF16)
            stores[2 * chan + cut].start()
    if part == 0:
        for copy in loads[4:]:
            copy.wait()
        firsts = [wide_ref[chan, 0:1, :] for chan in range(2)] + [lead_ref[chan, 0:1, :] for chan in range(2)]
        rows_ref[...] = jnp.concatenate(firsts + [jnp.zeros((12, COLS), F32)], 0).astype(BF16)
    for copy in stores:
        copy.wait()


def filter_send(part, spec, half, ahead=None):
    anywhere = pl.BlockSpec(memory_space=pl.ANY)
    first = part == 0
    return pl.pallas_call(
        functools.partial(filter_send_body, part),
        in_specs=[pl.BlockSpec(memory_space=pltpu.SMEM), anywhere] + ([] if first else [anywhere]),
        out_specs=[anywhere] + ([pl.BlockSpec(memory_space=pltpu.VMEM)] if first else []),
        out_shape=[jax.ShapeDtypeStruct((2, PER, COLS), BF16)]
        + ([jax.ShapeDtypeStruct((16, COLS), BF16)] if first else []),
        scratch_shapes=[
            pltpu.VMEM((2, PER, COLS), F32),
            pltpu.VMEM((2, PER, COLS), BF16),
            pltpu.SemaphoreType.DMA((6,)),
            pltpu.SemaphoreType.DMA((4,)),
        ]
        + ([pltpu.VMEM((2, 8, COLS), F32)] if first else []),
        compiler_params=pltpu.CompilerParams(vmem_limit_bytes=61 * 1024 * 1024),
        cost_estimate=pl.CostEstimate(flops=0, bytes_accessed=1_700_000, transcendentals=0),
        name="filter_send",
    )(*([half, spec] if first else [half, spec, ahead]))


def row_forward_body(
    x_hbm, table_ref, base_ref, phase_ref, order_ref, out_ref, x_ref, turned_ref, sems,
):
    copies = []

    def fetch(source, target):
        copies.append(pltpu.make_async_copy(source, target, sems.at[len(copies)]))
        copies[-1].start()
        return copies[-1]

    x_copies = [fetch(x_hbm.at[:, chan], x_ref.at[chan]) for chan in range(4)]
    for chan in range(4):
        x_copies[chan].wait()
        turned_ref[chan * LANES : (chan + 1) * LANES, :] = lax.dot_general(
            order_ref[...],
            x_ref[chan].reshape(HALF, LANES),
            (((1,), (1,)), ((), ())),
            preferred_element_type=F32,
        ).astype(BF16)

    lane = lax.broadcasted_iota(jnp.int32, (LANES, LANES), 1)
    first = lane < PER
    lead = lane % PER == 0
    base = base_ref[0]
    turned = pltpu.roll(base, PER, 1)
    own = jnp.where(first, base, turned), jnp.where(first, turned, base)

    def emit(place, real, imag):
        out_ref[place, 0] = real.astype(BF16)
        out_ref[place, 1] = imag.astype(BF16)

    high = []
    for block in range(BLOCKS):
        sums = jnp.dot(
            turned_ref[...], table_ref[:, block * 256 : (block + 1) * 256], preferred_element_type=F32
        )
        cosine, sine = rotate(
            *own, base_ref[1, :, block : block + 1], base_ref[2, :, block : block + 1]
        )
        cosine, sine = rotate(cosine, sine, phase_ref[0, block], phase_ref[1, block])
        for pair in range(2):
            upper = sums[pair * 256 : pair * 256 + 128]
            lower = sums[pair * 256 + 128 : pair * 256 + 256]
            real = jnp.where(first, upper[:, :LANES], lower[:, :LANES])
            imag = jnp.where(first, upper[:, LANES:], lower[:, LANES:])
            real, imag = rotate(real, imag, cosine, -sine)
            if pair == 0:
                emit(block, real, imag)
            else:
                high.append((real, imag))
        if block > 0:
            emit(16 - block, *(jnp.where(lead, new, old) for new, old in zip(high[block], high[block - 1])))
    emit(8, *(jnp.where(lead, new, old) for new, old in zip(high[0], high[7])))


def row_forward(x, table, base, phase, order):
    anywhere = pl.BlockSpec(memory_space=pl.ANY)
    inside = pl.BlockSpec(memory_space=pltpu.VMEM)
    block = (16, 2, LANES, LANES)
    return pl.pallas_call(
        row_forward_body,
        in_specs=[anywhere, inside, inside, inside, inside],
        out_specs=inside,
        out_shape=jax.ShapeDtypeStruct(block, BF16),
        scratch_shapes=[
            pltpu.VMEM((4, 8, 64, LANES), BF16),
            pltpu.VMEM((4 * LANES, HALF), BF16),
            pltpu.SemaphoreType.DMA((4,)),
        ],
        compiler_params=pltpu.CompilerParams(vmem_limit_bytes=16 * 1024 * 1024),
        cost_estimate=pl.CostEstimate(flops=1_100_000_000, bytes_accessed=5_000_000, transcendentals=0),
        name="row_forward",
    )(x, table, base, phase, order)


def filter_body(half_ref, own_ref, early_ref, late_ref, extra_ref, moves_ref, out_ref):
    for part in range(2):
        own = own_ref[part].reshape(LANES, own_ref.shape[3]).astype(BF16)
        got = (early_ref, late_ref)[part][...].reshape(LANES, early_ref.shape[2])
        total = None
        for source, low, high in ((own, 0, 128), (got, 128, 256), (extra_ref[...], 256, 272)):
            term = lax.dot_general(
                source, moves_ref[part, low:high, :], (((0,), (0,)), ((), ())), preferred_element_type=F32
            )
            total = term if total is None else total + term
        out_ref[0, part] = total[:, :LANES].astype(BF16)
        out_ref[1, part] = total[:, LANES:].astype(BF16)


def filter_layout(spec, half, early, late, extra, moves):
    step = 512
    return pl.pallas_call(
        filter_body,
        grid_spec=pltpu.PrefetchScalarGridSpec(
            num_scalar_prefetch=1,
            grid=(COLS // step,),
            in_specs=[
                pl.BlockSpec((2, 2, PER, step), lambda i, half: (0, half[0], 0, i)),
                pl.BlockSpec((2, PER, step), lambda i, half: (0, 0, i)),
                pl.BlockSpec((2, PER, step), lambda i, half: (0, 0, i)),
                pl.BlockSpec((16, step), lambda i, half: (0, i)),
                pl.BlockSpec((2, 272, 256), lambda i, half: (0, 0, 0)),
            ],
            out_specs=pl.BlockSpec((2, 2, step, LANES), lambda i, half: (0, 0, i, 0)),
        ),
        out_shape=jax.ShapeDtypeStruct((2, 2, COLS, LANES), BF16),
        compiler_params=pltpu.CompilerParams(vmem_limit_bytes=61 * 1024 * 1024),
        cost_estimate=pl.CostEstimate(flops=600_000_000, bytes_accessed=5_000_000, transcendentals=0),
        name="filter_layout",
    )(half, spec, early, late, extra, moves)


def column_body(
    y_hbm, filt_hbm, step_hbm, mid_ref, within_ref, between_ref, special_ref, out_ref,
    y_ref, turn_ref, filt_ref, step_ref, work_ref, sems,
):
    copies = []

    def fetch(source, target):
        copies.append(pltpu.make_async_copy(source, target, sems.at[len(copies)]))
        copies[-1].start()
        return copies[-1]

    y_copies = [fetch(y_hbm.at[pl.ds(8 * part, 8)], y_ref.at[pl.ds(8 * part, 8)]) for part in range(2)]
    step_copy = fetch(step_hbm.at[pl.ds(0, 2)], step_ref.at[pl.ds(0, 2)])
    later_copy = fetch(step_hbm.at[pl.ds(2, 4)], step_ref.at[pl.ds(2, 4)])
    filt_copies = []
    for part in range(4):
        rows = pl.ds(part * 512, 512)
        filt_copies.append(fetch(filt_hbm.at[:, :, rows], filt_ref.at[:, :, rows]))

    special = special_ref[...] > 0.5
    for copy in y_copies:
        copy.wait()
    step_copy.wait()

    def outer_forward(step):
        rows = slice(step * 16, step * 16 + 16)
        parts = [[], [], [], []]
        for block in range(16):
            real = y_ref[block, 0, rows, :].astype(F32)
            imag = y_ref[block, 1, rows, :].astype(F32)
            cosine, sine = rotate(
                within_ref[0, rows, :],
                within_ref[1, rows, :],
                between_ref[0, block : block + 1, :],
                between_ref[1, block : block + 1, :],
            )
            turn_ref[0, block, rows, :] = cosine
            turn_ref[1, block, rows, :] = sine
            parts[0].append(real)
            parts[1].append(jnp.where(special, 0.0, imag))
            parts[2].append(jnp.where(special, imag * cosine, real))
            parts[3].append(jnp.where(special, imag * sine, imag))
        for side in range(2):
            data = [
                jnp.concatenate(
                    [x[half * 8 : half * 8 + 8] for x in parts[2 * side] + parts[2 * side + 1]], 0
                ).astype(BF16)
                for half in range(2)
            ]
            sums = jnp.dot(step_ref[side], jnp.concatenate(data, 1), preferred_element_type=F32)
            for part in range(2):
                for group in range(16):
                    for half in range(2):
                        at = group * LANES + step * 16 + half * 8
                        work_ref[2 * side + part, at : at + 8, :] = sums[
                            part * LANES + group * 8 : part * LANES + group * 8 + 8,
                            half * LANES : (half + 1) * LANES,
                        ]

    def inner_step(step):
        if step % 4 == 0:
            filt_copies[step // 4].wait()
        rows = slice(step * LANES, (step + 1) * LANES)
        mid = [[mid_ref[side, part, :, step : step + 1] for part in range(2)] for side in range(2)]
        sides = []
        for side in range(2):
            real, imag = rotate(
                work_ref[2 * side, rows, :], work_ref[2 * side + 1, rows, :], mid[side][0], -mid[side][1]
            )
            sides.append(jnp.concatenate([real.astype(BF16), imag.astype(BF16)], 0))
        spectrum = jnp.dot(step_ref[4], jnp.concatenate(sides, 1), preferred_element_type=F32)
        sides = []
        for side in range(2):
            lanes = slice(side * LANES, (side + 1) * LANES)
            real, imag = rotate(
                spectrum[:LANES, lanes],
                spectrum[LANES:, lanes],
                filt_ref[side, 0, rows, :].astype(F32),
                filt_ref[side, 1, rows, :].astype(F32),
            )
            sides.append(jnp.concatenate([real.astype(BF16), imag.astype(BF16)], 0))
        middle = jnp.dot(step_ref[5], jnp.concatenate(sides, 1), preferred_element_type=F32)
        for side in range(2):
            lanes = slice(side * LANES, (side + 1) * LANES)
            real, imag = rotate(middle[:LANES, lanes], middle[LANES:, lanes], mid[side][0], mid[side][1])
            work_ref[2 * side, rows, :] = real
            work_ref[2 * side + 1, rows, :] = imag

    def outer_inverse(step):
        rows = slice(step * 16, step * 16 + 16)
        sums = []
        for side in range(2):
            data = []
            for half in range(2):
                pieces = []
                for part in range(2):
                    for group in range(16):
                        at = group * LANES + step * 16 + half * 8
                        pieces.append(work_ref[2 * side + part, at : at + 8, :])
                data.append(jnp.concatenate(pieces, 0).astype(BF16))
            sums.append(jnp.dot(step_ref[2 + side], jnp.concatenate(data, 1), preferred_element_type=F32))
        near, far = sums
        for block in range(16):

            def both(sums, part):
                at = part * LANES + block * 8
                return jnp.concatenate([sums[at : at + 8, :LANES], sums[at : at + 8, LANES:]], 0)

            near_re, near_im, far_re, far_im = both(near, 0), both(near, 1), both(far, 0), both(far, 1)
            cosine, sine = turn_ref[0, block, rows, :], turn_ref[1, block, rows, :]
            total_re, total_im = near_re + far_re, near_im + far_im
            real = jnp.where(special, near_re, total_re * cosine - total_im * sine)
            imag = jnp.where(special, far_re, total_im) * cosine + jnp.where(special, far_im, total_re) * sine
            out_ref[block, 0, rows, :] = real.astype(BF16)
            out_ref[block, 1, rows, :] = imag.astype(BF16)

    for step in range(8):
        outer_forward(step)
    later_copy.wait()
    for step in range(16):
        inner_step(step)
    for step in range(8):
        outer_inverse(step)


def column_step(y, filt, steps, mid, within, between, special):
    anywhere = pl.BlockSpec(memory_space=pl.ANY)
    block = (16, 2, LANES, LANES)
    return pl.pallas_call(
        column_body,
        in_specs=[anywhere] * 3 + [pl.BlockSpec(memory_space=pltpu.VMEM)] * 4,
        out_specs=pl.BlockSpec(memory_space=pltpu.VMEM),
        out_shape=jax.ShapeDtypeStruct(block, BF16),
        scratch_shapes=[
            pltpu.VMEM(block, BF16),
            pltpu.VMEM((2, 16, LANES, LANES), F32),
            pltpu.VMEM((2, 2, COLS, LANES), BF16),
            pltpu.VMEM((6, 256, 256), BF16),
            pltpu.VMEM((4, COLS, LANES), F32),
            pltpu.SemaphoreType.DMA((8,)),
        ],
        compiler_params=pltpu.CompilerParams(vmem_limit_bytes=60 * 1024 * 1024),
        cost_estimate=pl.CostEstimate(flops=2_000_000_000, bytes_accessed=10_000_000, transcendentals=0),
        name="column_step",
    )(y, filt, steps, mid, within, between, special)


def row_inverse_body(z_ref, table_ref, order_ref, out_ref, split_ref):
    lane = lax.broadcasted_iota(jnp.int32, (LANES, LANES), 1)
    first = lane < PER
    lead = lane % PER == 0
    for pair in range(2):
        for block in range(BLOCKS):
            for part in range(2):
                if pair == 0:
                    values = z_ref[block, part]
                else:
                    values = jnp.where(lead, z_ref[16 - block if block else 8, part], z_ref[15 - block, part])
                lanes = slice((block * 2 + part) * LANES, (block * 2 + part + 1) * LANES)
                zero = jnp.zeros_like(values)
                split_ref[pair * 256 : pair * 256 + 128, lanes] = jnp.where(first, values, zero)
                split_ref[pair * 256 + 128 : pair * 256 + 256, lanes] = jnp.where(first, zero, values)
        sums = lax.dot_general(
            table_ref[...],
            split_ref[pair * 256 : (pair + 1) * 256, :],
            (((1,), (1,)), ((), ())),
            preferred_element_type=F32,
        ) * (1.0 / TOTAL)
        for copy in range(2):
            own = sums[:, copy * LANES : (copy + 1) * LANES].astype(BF16)
            own = jnp.dot(own, order_ref[...], preferred_element_type=F32).astype(BF16)
            for row in range(8):
                out_ref[row, 2 * pair + copy] = own[row * 64 : (row + 1) * 64]


def row_inverse(z, table, order):
    inside = pl.BlockSpec(memory_space=pltpu.VMEM)
    return pl.pallas_call(
        row_inverse_body,
        in_specs=[inside] * 3,
        out_specs=inside,
        out_shape=jax.ShapeDtypeStruct((8, 4, 64, LANES), BF16),
        scratch_shapes=[pltpu.VMEM((4 * LANES, COLS), BF16)],
        compiler_params=pltpu.CompilerParams(vmem_limit_bytes=16 * 1024 * 1024),
        cost_estimate=pl.CostEstimate(flops=1_100_000_000, bytes_accessed=4_000_000, transcendentals=0),
        name="row_inverse",
    )(z, table, order)


def turn(first, second, modulus):
    angle = ((first * second) % modulus).astype(F32) * (TWO_PI / modulus)
    return jnp.stack([jnp.cos(angle), jnp.sin(angle)])


def per_device(gate_out, gate_in, values, filter_spec, skip):
    col = lax.axis_index("col")
    low_side = col < 8
    table = jnp.asarray(row_table())

    order = jnp.asarray(place_moves())

    half = jnp.where(low_side, 0, 1).astype(jnp.int32)[None]
    mirror = [(i, 15 - i) for i in range(16)]
    early_half, first_rows = filter_send(0, filter_spec, half)
    early = lax.ppermute(early_half, "col", mirror)
    extra = lax.ppermute(first_rows, "col", [(i, 16 - i if i % 8 else 8 - i) for i in range(16)])
    early_half, gate_in = lax.optimization_barrier((early_half, gate_in))
    gated = gate_in.astype(F32) * values.astype(F32)
    gated = gated.astype(BF16)
    x = lax.all_to_all(gated, "row", split_axis=0, concat_axis=0, tiled=True)
    late = lax.ppermute(filter_send(1, filter_spec, half, gated)[0], "col", mirror)
    moves = jnp.where(low_side, filter_moves()[0], filter_moves()[1])
    filt = filter_layout(filter_spec, half, early, late, extra, moves)

    lane = jnp.arange(LANES, dtype=jnp.int32) % PER
    all_k1 = (PER * jnp.arange(BLOCKS, dtype=jnp.int32))[:, None, None] + lane[None, None, :]
    phase = turn(all_k1, col, ROWS * 16)
    y = row_forward(x.reshape(8, 4, 64, LANES), table, twist_base(), phase, order)
    y = lax.all_to_all(y, "col", split_axis=0, concat_axis=0, tiled=True)

    own_k1 = PER * jnp.where(low_side, col, jnp.where(lane == 0, (16 - col) % 8, 15 - col)) + lane
    special = own_k1 == 0
    turn_k1 = jnp.where(special, -HALF, own_k1)
    within = turn(jnp.asarray(place_order(), jnp.int32)[:, None], turn_k1[None, :], TOTAL)
    between = turn(jnp.arange(16, dtype=jnp.int32)[:, None], turn_k1[None, :], ROWS * 16)
    z = column_step(
        y,
        filt,
        jnp.asarray(step_tables()),
        jnp.asarray(middle_tables()),
        within,
        between,
        special.astype(F32)[None, :],
    )
    z = lax.all_to_all(z, "col", split_axis=0, concat_axis=0, tiled=True)

    convolved = row_inverse(z, table, order).reshape(32, 64, LANES)
    convolved = lax.all_to_all(convolved, "row", split_axis=0, concat_axis=0, tiled=True)
    gated = gate_in.astype(F32) * values.astype(F32)
    return gate_out.astype(F32) * (convolved.astype(F32) + skip[:, None, None] * gated)


def solution(mesh):
    return jax.shard_map(
        per_device,
        mesh=mesh,
        in_specs=(
            P(None, "row", "col"),
            P(None, "row", "col"),
            P(None, "row", "col"),
            P(None, "row", "col", None),
            P(),
        ),
        out_specs=P(None, "row", "col"),
        check_vma=False,
    )
```

time: 110 us -> 103 us (0.936)
  local copies, waits for them, and re-layouts: 4.99 us -> 0.67 us
  starting transfers between devices: 20.7 us -> 16.5 us
  other arithmetic: 9.29 us -> 5.48 us
  waiting for transfers between devices: 14.9 us -> 18.5 us
  Pallas kernels: 22.1 us -> 24.2 us
    all_to_all x1, waiting for transfers between devices: 0.01 us -> 10.7 us  [per_device(): x = lax.all_to_all(gated, 'row', split_axis=0, concat_axis=0, tiled=True)]
    ppermute x3, waiting for transfers between devices: 8.36 us -> 0.01 us  [the longest x1 0.01 us: per_device(): lax.ppermute(filter_send(1, filter_spec, half, gated)[0], 'col', mirror)]
    all_to_all x1, starting transfers between devices: 8.41 us -> 4.49 us  [per_device(): y = lax.all_to_all(y, 'col', split_axis=0, concat_axis=0, tiled=True)]
    pallas_call x2 -> x3, Pallas kernels: 9.49 us -> 13.1 us  [the longest x1 8.35 us: column_step(): pl.pallas_call(column_body, in_specs=[anywhere] * 3 + [pl.BlockSpec(memor...]
    unnamed x32 -> x28, local copies, waits for them, and re-layouts: 4 us -> 0.67 us
    pallas_call x1, Pallas kernels: 5.03 us -> 2.85 us  [row_inverse(): pl.pallas_call(row_inverse_body, in_specs=[inside] * 3, out_specs=inside,...]
    sub x2 -> x0, other arithmetic: 1.77 us -> none  [rotate(): return (real * cosine - imag * sine, imag * cosine + real * sine)]
    another operation x2 -> x3, other arithmetic: 2.96 us -> 1.28 us  [turn(): return jnp.stack([jnp.cos(angle), jnp.sin(angle)])]
  transfers between devices with their start and end apart: 5 -> 5, of which waited for: 3 -> 2; matrix products, arithmetic and copies ran while one was open for 6% -> 4% of each run, Pallas kernels for 8% -> 10%
where the time goes in v2:
time: 103 us
  blocking collectives  37.3 us (36%)
  Pallas kernels  24.2 us (23%)
  waiting for transfers between devices  18.5 us (18%)
  starting transfers between devices  16.5 us (16%)
  other arithmetic  5.48 us (5%)
    all_to_all x1, blocking collectives, per_device(): z = lax.all_to_all(z, 'col', split_axis=0, concat_axis=0, tiled=True)  20.3 us
    all_to_all x1, blocking collectives, per_device(): lax.all_to_all(convolved, 'row', split_axis=0, concat_axis=0, tiled=True)  17 us
    all_to_all x1, waiting for transfers between devices, per_device(): x = lax.all_to_all(gated, 'row', split_axis=0, concat_axis=0, tiled=True)  10.7 us
    pallas_call x1, Pallas kernels, column_step(): pl.pallas_call(column_body, in_specs=[anywhere] * 3 + [pl.BlockSpec(memor...  8.35 us
    all_to_all x1, waiting for transfers between devices, per_device(): y = lax.all_to_all(y, 'col', split_axis=0, concat_axis=0, tiled=True)  7.76 us
    all_to_all x1, starting transfers between devices, per_device(): x = lax.all_to_all(gated, 'row', split_axis=0, concat_axis=0, tiled=True)  6.64 us
    pallas_call x1, Pallas kernels, filter_layout(): pl.pallas_call(filter_body, grid_spec=pltpu.PrefetchScalarGridSpec(num_sc...  5.23 us
    pallas_call x2, Pallas kernels, filter_send(): pl.pallas_call(functools.partial(filter_send_body, part), in_specs=[pl.Bl...  4.76 us
  transfers between devices with their start and end apart: 5, of which 2 were waited for; matrix products, arithmetic and copies ran while one was open for 4% of the time, Pallas kernels for 10%

profile of v2, /device:TPU:0, one launch (start us, length us, event | category | flops | bytes accessed | tf_op | source)
XLA Modules:
  0.0 102.9 jit_solution(12286499074021204347)
XLA Ops:
  0.0 2.7 %filter_send.2 = (bf16[2,64,2048]{2,1,0:T(8,128)(2,1)}, bf16[16,2048]{1,0:T(8,128)(2,1)}) custom-call(s32[1]{0:T(128)} %bitcast.refs_0_.half_ref, f32[2,4,64,2048]{3,2,1,0:T(8,128)} %own_ref.1), custom_call_target="tpu_custom_call" | custom-call | bytes 1700000 | tf_op jit(solution)/shard_map/filter_send/pallas_call | solution.py:166
  2.7 4.7 %collective-permute-start = (bf16[2,64,2048]{2,1,0:T(8,128)(2,1)}, bf16[2,64,2048]{2,1,0:T(8,128)(2,1)}, u32[]{:S(2)}, u32[]{:S(2)}) collective-permute-start(bf16[2,64,2048]{2,1,0:T(8,128)(2,1)} %get-tuple-element.8), channel_id=1, source_target_pairs={{0,15},{1,14},{2,13},{3,12},{4,11},{5,10},{6,9},{7,8},{8,7},{9,6},... | collective-permute-start | bytes 1572872 | tf_op jit(solution)/shard_map/ppermute | solution.py:501
  7.3 1.0 fusion.refs_2_
  8.3 6.6 %all-to-all-start = ((bf16[32,64,128]{2,1,0:T(8,128)(2,1)}), bf16[32,64,128]{2,1,0:T(8,128)(2,1)S(1)}, u32[]{:S(2)}, u32[]{:S(2)}) async-start(bf16[32,64,128]{2,1,0:T(8,128)(2,1)} %fusion.refs_2_), calls=%async_computation | async-start | bytes 1048576 | tf_op jit(solution)/shard_map/all_to_all | solution.py:506
  15.0 0.0 copy-start
  15.0 0.0 copy-start.1
  15.0 0.0 copy-start.2
  15.0 2.1 %filter_send.3 = bf16[2,64,2048]{2,1,0:T(8,128)(2,1)} custom-call(s32[1]{0:T(128)} %bitcast.refs_0_.half_ref, f32[2,4,64,2048]{3,2,1,0:T(8,128)} %own_ref.1, bf16[32,64,128]{2,1,0:T(8,128)(2,1)} %fusion.refs_2_), custom_call_target="tpu_custom_call" | custom-call | bytes 1700000 | tf_op jit(solution)/shard_map/filter_send/pallas_call | solution.py:166
  17.1 0.1 collective-permute-start.1
  17.2 0.6 collective-permute-start.2
  17.9 0.1 fusion.13
  17.9 0.1 multiply_cosine_fusion
  18.1 10.7 %all-to-all-done = bf16[32,64,128]{2,1,0:T(8,128)(2,1)S(1)} async-done(((bf16[32,64,128]{2,1,0:T(8,128)(2,1)}), bf16[32,64,128]{2,1,0:T(8,128)(2,1)S(1)}, u32[]{:S(2)}, u32[]{:S(2)}) %all-to-all-start) | async-done | bytes 524320 | tf_op jit(solution)/shard_map/all_to_all | solution.py:506
  28.8 0.0 copy-start.11
  28.8 3.1 %row_forward.1 = bf16[16,2,128,128]{3,2,1,0:T(8,128)(2,1)} custom-call(bf16[8,4,64,128]{3,2,1,0:T(8,128)(2,1)S(1)} %bitcast.4, bf16[512,2048]{1,0:T(8,128)(2,1)S(1)} %copy-done, f32[3,128,128]{2,1,0:T(8,128)S(1)} %copy-done.1, f32[2,8,1,128]{3,2,1,0:T(1,128)S(1)} %pad_maximum_fusion.2.phase_ref, bf16[128,128]{1,0:T(8,128)(2,1)S(1)} %copy-done.2), custom_call_target="tpu_custom_call" | custom-call | flops 1100000000 | bytes 5000000 | tf_op jit(solution)/shard_map/row_forward/pallas_call | solution.py:244
  31.9 0.0 copy-start.8
  31.9 0.0 copy-start.9
  31.9 4.5 %all-to-all-start.1 = ((bf16[16,2,128,128]{3,2,1,0:T(8,128)(2,1)}), bf16[16,2,128,128]{3,2,1,0:T(8,128)(2,1)}, u32[]{:S(2)}, u32[]{:S(2)}) async-start(bf16[16,2,128,128]{3,2,1,0:T(8,128)(2,1)} %row_forward.1), calls=%async_computation.1 | async-start | bytes 2097152 | tf_op jit(solution)/shard_map/all_to_all | solution.py:515
  36.4 0.1 fusion.15
  36.5 0.3 fusion.5
  36.8 0.6 pad_maximum_fusion.1.between_ref
  37.5 0.7 pad_maximum_fusion.within_ref
  38.1 0.8 broadcast_select_fusion.moves_ref
  38.9 0.5 compare_convert_fusion.special_ref
  39.4 0.6 copy-done.10
  40.0 5.2 %filter_layout.1.filt_hbm = bf16[2,2,2048,128]{3,2,1,0:T(8,128)(2,1)} custom-call(s32[1]{0:T(128)} %bitcast.refs_0_.half_ref, f32[2,4,64,2048]{3,2,1,0:T(8,128)} %own_ref.1, bf16[2,64,2048]{2,1,0:T(8,128)(2,1)} %collective-permute-done.early_ref, bf16[2,64,2048]{2,1,0:T(8,128)(2,1)} %collective-permute-done.1.late_ref, bf16[16,2048]{1,0:T(8,128)(2,1)} %copy-done.10, ...), custom_call_target="tpu_custom_call" | custom-call | flops 600000000 | bytes 5000000 | tf_op jit(solution)/shard_map/filter_layout/pallas_call | solution.py:276
  45.3 7.8 %all-to-all-done.1.y_hbm = bf16[16,2,128,128]{3,2,1,0:T(8,128)(2,1)} async-done(((bf16[16,2,128,128]{3,2,1,0:T(8,128)(2,1)}), bf16[16,2,128,128]{3,2,1,0:T(8,128)(2,1)}, u32[]{:S(2)}, u32[]{:S(2)}) %all-to-all-start.1) | async-done | bytes 1048608 | tf_op jit(solution)/shard_map/all_to_all | solution.py:515
  53.0 8.3 %column_step.1 = bf16[16,2,128,128]{3,2,1,0:T(8,128)(2,1)} custom-call(bf16[16,2,128,128]{3,2,1,0:T(8,128)(2,1)} %all-to-all-done.1.y_hbm, bf16[2,2,2048,128]{3,2,1,0:T(8,128)(2,1)} %filter_layout.1.filt_hbm, bf16[6,256,256]{2,1,0:T(8,128)(2,1)} %constant.110.clone.step_hbm, f32[2,2,128,128]{3,2,1,0:T(8,128)} %constant.111.clone.mid_ref, ...), custom_call_target="tpu_custom_call" | custom-call | flops 2000000000 | bytes 10000000 | tf_op jit(solution)/shard_map/column_step/pallas_call | solution.py:425
  61.4 20.3 %all_to_all.20.z_ref = bf16[16,2,128,128]{3,2,1,0:T(8,128)(2,1)S(1)} all-to-all(bf16[16,2,128,128]{3,2,1,0:T(8,128)(2,1)} %column_step.1), channel_id=1, replica_groups=mesh['row'=8,'col'=16] {'col'}, dimensions={0} | all-to-all | bytes 2097152 | tf_op jit(solution)/shard_map/all_to_all | solution.py:531
  81.7 2.8 %row_inverse.1 = bf16[8,4,64,128]{3,2,1,0:T(8,128)(2,1)S(1)} custom-call(bf16[16,2,128,128]{3,2,1,0:T(8,128)(2,1)S(1)} %all_to_all.20.z_ref, bf16[512,2048]{1,0:T(8,128)(2,1)S(1)} %copy-done, bf16[128,128]{1,0:T(8,128)(2,1)S(1)} %copy-done.2), custom_call_target="tpu_custom_call" | custom-call | flops 1100000000 | bytes 4000000 | tf_op jit(solution)/shard_map/row_inverse/pallas_call | solution.py:474
  84.6 17.0 %all_to_all.21 = bf16[32,64,128]{2,1,0:T(8,128)(2,1)S(1)} all-to-all(bf16[32,64,128]{2,1,0:T(8,128)(2,1)S(1)} %bitcast.5), channel_id=1, replica_groups=mesh['row'=8,'col'=16] {'row'}, dimensions={0} | all-to-all | bytes 1048576 | tf_op jit(solution)/shard_map/all_to_all | solution.py:534
  101.6 1.3 %add_multiply_fusion = f32[32,64,128]{2,1,0:T(8,128)} fusion(bf16[32,64,128]{2,1,0:T(8,128)(2,1)S(1)} %all_to_all.21, bf16[32,64,128]{2,1,0:T(8,128)(2,1)S(1)} %copy-done.7, bf16[32,64,128]{2,1,0:T(8,128)(2,1)S(1)} %copy-done.4, bf16[32,64,128]{2,1,0:T(8,128)(2,1)S(1)} %copy-done.6, f32[32]{0:T(128)S(1)} %copy-done.12), kind=kLoop, calls=%fused_computation | loop fusion | flops 2097152 | bytes 3145856 | tf_op jit(solution)/shard_map/mul | solution.py:536
  (28 shorter events, 0.1 us)
Async XLA Ops:
  0.0 7.3 %copy-start.3 = (bf16[32,64,128]{2,1,0:T(8,128)(2,1)S(1)}, bf16[32,64,128]{2,1,0:T(8,128)(2,1)}, u32[]{:S(2)}) copy-start(bf16[32,64,128]{2,1,0:T(8,128)(2,1)} %param.15) | copy-start | bytes 1572868
  0.0 7.3 %copy-start.5 = (bf16[32,64,128]{2,1,0:T(8,128)(2,1)S(1)}, bf16[32,64,128]{2,1,0:T(8,128)(2,1)}, u32[]{:S(2)}) copy-start(bf16[32,64,128]{2,1,0:T(8,128)(2,1)} %param.14) | copy-start | bytes 1572868
  2.7 36.8 %collective-permute-start = (bf16[2,64,2048]{2,1,0:T(8,128)(2,1)}, bf16[2,64,2048]{2,1,0:T(8,128)(2,1)}, u32[]{:S(2)}, u32[]{:S(2)}) collective-permute-start(bf16[2,64,2048]{2,1,0:T(8,128)(2,1)} %get-tuple-element.8), channel_id=1, source_target_pairs={{0,15},{1,14},{2,13},{3,12},{4,11},{5,10},{6,9},{7,8},{8,7},{9,6},... | collective-permute-start | bytes 1572872 | tf_op jit(solution)/shard_map/ppermute | solution.py:501
  8.3 20.5 %all-to-all-start = ((bf16[32,64,128]{2,1,0:T(8,128)(2,1)}), bf16[32,64,128]{2,1,0:T(8,128)(2,1)S(1)}, u32[]{:S(2)}, u32[]{:S(2)}) async-start(bf16[32,64,128]{2,1,0:T(8,128)(2,1)} %fusion.refs_2_), calls=%async_computation | async-start | bytes 1048576 | tf_op jit(solution)/shard_map/all_to_all | solution.py:506
  15.0 2.2 %copy-start.13 = (bf16[16,2048]{1,0:T(8,128)(2,1)S(1)}, bf16[16,2048]{1,0:T(8,128)(2,1)}, u32[]{:S(2)}) copy-start(bf16[16,2048]{1,0:T(8,128)(2,1)} %get-tuple-element.10) | copy-start | bytes 196612
  15.0 13.9 %copy-start = (bf16[512,2048]{1,0:T(8,128)(2,1)S(1)}, bf16[512,2048]{1,0:T(8,128)(2,1)}, u32[]{:S(2)}) copy-start(bf16[512,2048]{1,0:T(8,128)(2,1)} %constant.104.clone.table_ref) | copy-start | bytes 6291460
  15.0 13.9 %copy-start.1 = (f32[3,128,128]{2,1,0:T(8,128)S(1)}, f32[3,128,128]{2,1,0:T(8,128)}, u32[]{:S(2)}) copy-start(f32[3,128,128]{2,1,0:T(8,128)} %constant.108.clone.base_ref) | copy-start | bytes 589828
  15.0 13.8 %copy-start.2 = (bf16[128,128]{1,0:T(8,128)(2,1)S(1)}, bf16[128,128]{1,0:T(8,128)(2,1)}, u32[]{:S(2)}) copy-start(bf16[128,128]{1,0:T(8,128)(2,1)} %constant.105.clone.order_ref) | copy-start | bytes 98308
  17.1 22.3 %collective-permute-start.1 = (bf16[2,64,2048]{2,1,0:T(8,128)(2,1)}, bf16[2,64,2048]{2,1,0:T(8,128)(2,1)}, u32[]{:S(2)}, u32[]{:S(2)}) collective-permute-start(bf16[2,64,2048]{2,1,0:T(8,128)(2,1)} %filter_send.3), channel_id=1, source_target_pairs={{0,15},{1,14},{2,13},{3,12},{4,11},{5,10},{6,9},{7,8},{8,7},{9,6},... | collective-permute-start | bytes 1572872 | tf_op jit(solution)/shard_map/ppermute | solution.py:507
  17.2 22.2 %collective-permute-start.2 = (bf16[16,2048]{1,0:T(8,128)(2,1)S(1)}, bf16[16,2048]{1,0:T(8,128)(2,1)S(1)}, u32[]{:S(2)}, u32[]{:S(2)}) collective-permute-start(bf16[16,2048]{1,0:T(8,128)(2,1)S(1)} %copy-done.13), channel_id=1, source_target_pairs={{0,8},{1,15},{2,14},{3,13},{4,12},{5,11},{6,10},{7,9},{8,0},{9,7},... | collective-permute-start | bytes 196616 | tf_op jit(solution)/shard_map/ppermute | solution.py:502
  28.8 7.7 %copy-start.11 = (s32[128]{0:T(128)S(1)}, s32[128]{0:T(128)}, u32[]{:S(2)}) copy-start(s32[128]{0:T(128)} %constant.109.clone) | copy-start | bytes 1540
  31.9 6.2 %copy-start.8 = (bf16[2,272,256]{2,1,0:T(8,128)(2,1)S(1)}, bf16[2,272,256]{2,1,0:T(8,128)(2,1)}, u32[]{:S(2)}) copy-start(bf16[2,272,256]{2,1,0:T(8,128)(2,1)} %constant.106.clone) | copy-start | bytes 835588
  31.9 6.2 %copy-start.9 = (bf16[2,272,256]{2,1,0:T(8,128)(2,1)S(1)}, bf16[2,272,256]{2,1,0:T(8,128)(2,1)}, u32[]{:S(2)}) copy-start(bf16[2,272,256]{2,1,0:T(8,128)(2,1)} %constant.107.clone) | copy-start | bytes 835588
  31.9 21.1 %all-to-all-start.1 = ((bf16[16,2,128,128]{3,2,1,0:T(8,128)(2,1)}), bf16[16,2,128,128]{3,2,1,0:T(8,128)(2,1)}, u32[]{:S(2)}, u32[]{:S(2)}) async-start(bf16[16,2,128,128]{3,2,1,0:T(8,128)(2,1)} %row_forward.1), calls=%async_computation.1 | async-start | bytes 2097152 | tf_op jit(solution)/shard_map/all_to_all | solution.py:515
  39.4 0.6 copy-start.10
  81.7 19.9 %copy-start.4 = (bf16[32,64,128]{2,1,0:T(8,128)(2,1)S(1)}, bf16[32,64,128]{2,1,0:T(8,128)(2,1)}, u32[]{:S(2)}) copy-start(bf16[32,64,128]{2,1,0:T(8,128)(2,1)} %param.15) | copy-start | bytes 1572868
  81.7 19.9 %copy-start.6 = (bf16[32,64,128]{2,1,0:T(8,128)(2,1)S(1)}, bf16[32,64,128]{2,1,0:T(8,128)(2,1)}, u32[]{:S(2)}) copy-start(bf16[32,64,128]{2,1,0:T(8,128)(2,1)} %param.14) | copy-start | bytes 1572868
  81.7 19.9 %copy-start.7 = (bf16[32,64,128]{2,1,0:T(8,128)(2,1)S(1)}, bf16[32,64,128]{2,1,0:T(8,128)(2,1)}, u32[]{:S(2)}) copy-start(bf16[32,64,128]{2,1,0:T(8,128)(2,1)} %param.13) | copy-start | bytes 1572868
  81.7 19.9 %copy-start.12 = (f32[32]{0:T(128)S(1)}, f32[32]{0:T(128)}, u32[]{:S(2)}) copy-start(f32[32]{0:T(128)} %param.17) | copy-start | bytes 388

commit v3 on v2

--- a/solution.py
+++ b/solution.py
@@ -75,14 +75,13 @@
     return narrow(np.stack(outer_tables() + inner_tables()))
 
 
-def middle_tables():
-    angle = grid_angle(np.arange(OUTER + 1), np.arange(INNER), COLS)
+def middle_index():
+    product = np.arange(OUTER + 1)[:, None] * np.arange(INNER)[None, :]
     sides = []
     for side in range(2):
-        own = angle[side : side + OUTER].reshape(16, 4, 16, 2).transpose(0, 2, 1, 3).reshape(COLS, 1)
-        own = np.pad(own.reshape(16, LANES).T, ((0, 0), (0, LANES - 16)))
-        sides.append(np.stack([np.cos(own), np.sin(own)]))
-    return np.stack(sides).astype(np.float32)
+        own = product[side : side + OUTER].reshape(16, 4, 16, 2).transpose(0, 2, 1, 3).reshape(16, LANES).T
+        sides.append(np.pad(own, ((0, 0), (0, LANES - 16))))
+    return np.stack(sides).astype(np.int32)
 
 
 def place_order():
@@ -288,35 +287,16 @@
             out_specs=pl.BlockSpec((2, 2, step, LANES), lambda i, half: (0, 0, i, 0)),
         ),
         out_shape=jax.ShapeDtypeStruct((2, 2, COLS, LANES), BF16),
-        compiler_params=pltpu.CompilerParams(vmem_limit_bytes=61 * 1024 * 1024),
+        compiler_params=pltpu.CompilerParams(vmem_limit_bytes=55 * 1024 * 1024),
         cost_estimate=pl.CostEstimate(flops=600_000_000, bytes_accessed=5_000_000, transcendentals=0),
         name="filter_layout",
     )(half, spec, early, late, extra, moves)
 
 
 def column_body(
-    y_hbm, filt_hbm, step_hbm, mid_ref, within_ref, between_ref, special_ref, out_ref,
-    y_ref, turn_ref, filt_ref, step_ref, work_ref, sems,
+    y_ref, filt_ref, step_ref, mid_ref, within_ref, between_ref, special_ref, out_ref, turn_ref, work_ref,
 ):
-    copies = []
-
-    def fetch(source, target):
-        copies.append(pltpu.make_async_copy(source, target, sems.at[len(copies)]))
-        copies[-1].start()
-        return copies[-1]
-
-    y_copies = [fetch(y_hbm.at[pl.ds(8 * part, 8)], y_ref.at[pl.ds(8 * part, 8)]) for part in range(2)]
-    step_copy = fetch(step_hbm.at[pl.ds(0, 2)], step_ref.at[pl.ds(0, 2)])
-    later_copy = fetch(step_hbm.at[pl.ds(2, 4)], step_ref.at[pl.ds(2, 4)])
-    filt_copies = []
-    for part in range(4):
-        rows = pl.ds(part * 512, 512)
-        filt_copies.append(fetch(filt_hbm.at[:, :, rows], filt_ref.at[:, :, rows]))
-
     special = special_ref[...] > 0.5
-    for copy in y_copies:
-        copy.wait()
-    step_copy.wait()
 
     def outer_forward(step):
         rows = slice(step * 16, step * 16 + 16)
@@ -354,10 +334,8 @@
                         ]
 
     def inner_step(step):
-        if step % 4 == 0:
-            filt_copies[step // 4].wait()
         rows = slice(step * LANES, (step + 1) * LANES)
-        mid = [[mid_ref[side, part, :, step : step + 1] for part in range(2)] for side in range(2)]
+        mid = [[mid_ref[part, side, :, step : step + 1] for part in range(2)] for side in range(2)]
         sides = []
         for side in range(2):
             real, imag = rotate(
@@ -412,7 +390,6 @@
 
     for step in range(8):
         outer_forward(step)
-    later_copy.wait()
     for step in range(16):
         inner_step(step)
     for step in range(8):
@@ -420,23 +397,15 @@
 
 
 def column_step(y, filt, steps, mid, within, between, special):
-    anywhere = pl.BlockSpec(memory_space=pl.ANY)
-    block = (16, 2, LANES, LANES)
+    inside = pl.BlockSpec(memory_space=pltpu.VMEM)
     return pl.pallas_call(
         column_body,
-        in_specs=[anywhere] * 3 + [pl.BlockSpec(memory_space=pltpu.VMEM)] * 4,
-        out_specs=pl.BlockSpec(memory_space=pltpu.VMEM),
-        out_shape=jax.ShapeDtypeStruct(block, BF16),
-        scratch_shapes=[
-            pltpu.VMEM(block, BF16),
-            pltpu.VMEM((2, 16, LANES, LANES), F32),
-            pltpu.VMEM((2, 2, COLS, LANES), BF16),
-            pltpu.VMEM((6, 256, 256), BF16),
-            pltpu.VMEM((4, COLS, LANES), F32),
-            pltpu.SemaphoreType.DMA((8,)),
-        ],
-        compiler_params=pltpu.CompilerParams(vmem_limit_bytes=60 * 1024 * 1024),
-        cost_estimate=pl.CostEstimate(flops=2_000_000_000, bytes_accessed=10_000_000, transcendentals=0),
+        in_specs=[inside] * 7,
+        out_specs=inside,
+        out_shape=jax.ShapeDtypeStruct((16, 2, LANES, LANES), BF16),
+        scratch_shapes=[pltpu.VMEM((2, 16, LANES, LANES), F32), pltpu.VMEM((4, COLS, LANES), F32)],
+        compiler_params=pltpu.CompilerParams(vmem_limit_bytes=24 * 1024 * 1024),
+        cost_estimate=pl.CostEstimate(flops=2_000_000_000, bytes_accessed=5_000_000, transcendentals=0),
         name="column_step",
     )(y, filt, steps, mid, within, between, special)
 
@@ -519,15 +488,9 @@
     turn_k1 = jnp.where(special, -HALF, own_k1)
     within = turn(jnp.asarray(place_order(), jnp.int32)[:, None], turn_k1[None, :], TOTAL)
     between = turn(jnp.arange(16, dtype=jnp.int32)[:, None], turn_k1[None, :], ROWS * 16)
-    z = column_step(
-        y,
-        filt,
-        jnp.asarray(step_tables()),
-        jnp.asarray(middle_tables()),
-        within,
-        between,
-        special.astype(F32)[None, :],
-    )
+    mid = turn(jnp.asarray(middle_index()), 1, COLS)
+    steps = jnp.asarray(step_tables()) * (col >= 0).astype(BF16)
+    z = column_step(y, filt, steps, mid, within, between, special.astype(F32)[None, :])
     z = lax.all_to_all(z, "col", split_axis=0, concat_axis=0, tiled=True)
 
     convolved = row_inverse(z, table, order).reshape(32, 64, LANES)

time: 103 us -> 100 us (0.971)
  Pallas kernels: 24.2 us -> 20.2 us
  waiting for transfers between devices: 18.5 us -> 20.9 us
  other arithmetic: 5.48 us -> 3.73 us
  local copies, waits for them, and re-layouts: 0.67 us -> 2.26 us
  blocking collectives: 37.3 us -> 35.9 us
    pallas_call x1, Pallas kernels: 8.35 us -> 4.34 us  [column_step(): pl.pallas_call(column_body, in_specs=[inside] * 7, out_specs=inside, out_...]
    all_to_all x1, waiting for transfers between devices: 7.76 us -> 9.75 us  [per_device(): y = lax.all_to_all(y, 'col', split_axis=0, concat_axis=0, tiled=True)]
    ppermute x1, starting transfers between devices: 4.65 us -> 3.01 us  [per_device(): early = lax.ppermute(early_half, 'col', mirror)]
    unnamed x28 -> x34, local copies, waits for them, and re-layouts: 0.67 us -> 2.26 us
    another operation x3, other arithmetic: 1.28 us -> 0.02 us  [turn(): return jnp.stack([jnp.cos(angle), jnp.sin(angle)])]
    ppermute x1, starting transfers between devices: 0.64 us -> 1.74 us  [per_device(): lax.ppermute(first_rows, 'col', [(i, 16 - i if i % 8 else 8 - i) for i in...]
    all_to_all x1, blocking collectives: 20.3 us -> 19.2 us  [per_device(): z = lax.all_to_all(z, 'col', split_axis=0, concat_axis=0, tiled=True)]
  transfers between devices with their start and end apart: 5 -> 5, of which waited for: 2 -> 2; matrix products, arithmetic and copies ran while one was open for 4% -> 2% of each run, Pallas kernels for 10% -> 10%
where the time goes in v3:
time: 100 us; the launch traced here: 99.6 us
  blocking collectives  35.9 us (36%)
  waiting for transfers between devices  20.9 us (21%)
  Pallas kernels  20.2 us (20%)
  starting transfers between devices  16.2 us (16%)
  other arithmetic  3.73 us (4%)
  local copies, waits for them, and re-layouts  2.26 us (2%)
    all_to_all x1, blocking collectives, per_device(): z = lax.all_to_all(z, 'col', split_axis=0, concat_axis=0, tiled=True)  19.2 us
    all_to_all x1, blocking collectives, per_device(): lax.all_to_all(convolved, 'row', split_axis=0, concat_axis=0, tiled=True)  16.7 us
    all_to_all x1, waiting for transfers between devices, per_device(): x = lax.all_to_all(gated, 'row', split_axis=0, concat_axis=0, tiled=True)  11.1 us
    all_to_all x1, waiting for transfers between devices, per_device(): y = lax.all_to_all(y, 'col', split_axis=0, concat_axis=0, tiled=True)  9.75 us
    all_to_all x1, starting transfers between devices, per_device(): x = lax.all_to_all(gated, 'row', split_axis=0, concat_axis=0, tiled=True)  6.64 us
    pallas_call x1, Pallas kernels, filter_layout(): pl.pallas_call(filter_body, grid_spec=pltpu.PrefetchScalarGridSpec(num_sc...  5.27 us
    all_to_all x1, starting transfers between devices, per_device(): y = lax.all_to_all(y, 'col', split_axis=0, concat_axis=0, tiled=True)  4.75 us
    pallas_call x2, Pallas kernels, filter_send(): pl.pallas_call(functools.partial(filter_send_body, part), in_specs=[pl.Bl...  4.73 us
  transfers between devices with their start and end apart: 5, of which 2 were waited for; matrix products, arithmetic and copies ran while one was open for 2% of the time, Pallas kernels for 10%

profile of v3, /device:TPU:0, one launch (start us, length us, event | category | flops | bytes accessed | tf_op | source)
XLA Modules:
  0.0 99.6 jit_solution(18181570987326780883)
XLA Ops:
  0.0 2.6 %filter_send.2 = (bf16[2,64,2048]{2,1,0:T(8,128)(2,1)}, bf16[16,2048]{1,0:T(8,128)(2,1)}) custom-call(s32[1]{0:T(128)} %bitcast.refs_0_.half_ref, f32[2,4,64,2048]{3,2,1,0:T(8,128)} %own_ref.1), custom_call_target="tpu_custom_call" | custom-call | bytes 1700000 | tf_op jit(solution)/shard_map/filter_send/pallas_call | solution.py:165
  2.6 1.7 %collective-permute-start.2 = (bf16[16,2048]{1,0:T(8,128)(2,1)}, bf16[16,2048]{1,0:T(8,128)(2,1)S(1)}, u32[]{:S(2)}, u32[]{:S(2)}) collective-permute-start(bf16[16,2048]{1,0:T(8,128)(2,1)} %get-tuple-element.10), channel_id=1, source_target_pairs={{0,8},{1,15},{2,14},{3,13},{4,12},{5,11},{6,10},{7,9},{8,0},{9,7},... | collective-permute-start | bytes 196616 | tf_op jit(solution)/shard_map/ppermute | solution.py:471
  4.4 3.0 %collective-permute-start = (bf16[2,64,2048]{2,1,0:T(8,128)(2,1)}, bf16[2,64,2048]{2,1,0:T(8,128)(2,1)}, u32[]{:S(2)}, u32[]{:S(2)}) collective-permute-start(bf16[2,64,2048]{2,1,0:T(8,128)(2,1)} %get-tuple-element.8), channel_id=1, source_target_pairs={{0,15},{1,14},{2,13},{3,12},{4,11},{5,10},{6,9},{7,8},{8,7},{9,6},... | collective-permute-start | bytes 1572872 | tf_op jit(solution)/shard_map/ppermute | solution.py:470
  7.4 1.0 fusion.refs_2_
  8.4 6.6 %all-to-all-start = ((bf16[32,64,128]{2,1,0:T(8,128)(2,1)}), bf16[32,64,128]{2,1,0:T(8,128)(2,1)S(1)}, u32[]{:S(2)}, u32[]{:S(2)}) async-start(bf16[32,64,128]{2,1,0:T(8,128)(2,1)} %fusion.refs_2_), calls=%async_computation | async-start | bytes 1048576 | tf_op jit(solution)/shard_map/all_to_all | solution.py:475
  15.0 0.0 copy-start.1
  15.0 0.0 copy-start.4
  15.1 2.1 %filter_send.3 = bf16[2,64,2048]{2,1,0:T(8,128)(2,1)} custom-call(s32[1]{0:T(128)} %bitcast.refs_0_.half_ref, f32[2,4,64,2048]{3,2,1,0:T(8,128)} %own_ref.1, bf16[32,64,128]{2,1,0:T(8,128)(2,1)} %fusion.refs_2_), custom_call_target="tpu_custom_call" | custom-call | bytes 1700000 | tf_op jit(solution)/shard_map/filter_send/pallas_call | solution.py:165
  17.2 0.1 collective-permute-start.1
  17.3 0.1 fusion.13
  17.4 0.1 multiply_cosine_fusion
  17.6 0.3 fusion.5
  17.9 11.1 %all-to-all-done = bf16[32,64,128]{2,1,0:T(8,128)(2,1)S(1)} async-done(((bf16[32,64,128]{2,1,0:T(8,128)(2,1)}), bf16[32,64,128]{2,1,0:T(8,128)(2,1)S(1)}, u32[]{:S(2)}, u32[]{:S(2)}) %all-to-all-start) | async-done | bytes 524320 | tf_op jit(solution)/shard_map/all_to_all | solution.py:475
  29.0 3.1 %row_forward.1 = bf16[16,2,128,128]{3,2,1,0:T(8,128)(2,1)} custom-call(bf16[8,4,64,128]{3,2,1,0:T(8,128)(2,1)S(1)} %bitcast.4, bf16[512,2048]{1,0:T(8,128)(2,1)S(1)} %copy-done.1, f32[3,128,128]{2,1,0:T(8,128)S(1)} %copy-done.4, f32[2,8,1,128]{3,2,1,0:T(1,128)S(1)} %pad_maximum_fusion.2.phase_ref, bf16[128,128]{1,0:T(8,128)(2,1)S(1)} %copy-done.5), custom_call_target="tpu_custom_call" | custom-call | flops 1100000000 | bytes 5000000 | tf_op jit(solution)/shard_map/row_forward/pallas_call | solution.py:243
  32.1 0.0 copy-start.12
  32.1 0.0 copy-start.13
  32.1 0.0 copy-start.10
  32.1 4.7 %all-to-all-start.1 = ((bf16[16,2,128,128]{3,2,1,0:T(8,128)(2,1)}), bf16[16,2,128,128]{3,2,1,0:T(8,128)(2,1)S(1)}, u32[]{:S(2)}, u32[]{:S(2)}) async-start(bf16[16,2,128,128]{3,2,1,0:T(8,128)(2,1)} %row_forward.1), calls=%async_computation.1 | async-start | bytes 2097152 | tf_op jit(solution)/shard_map/all_to_all | solution.py:484
  36.9 0.1 fusion.15
  37.0 0.8 broadcast_select_fusion.moves_ref
  37.8 0.1 broadcast_multiply_fusion.step_ref
  37.8 0.0 copy-start.3
  37.9 0.6 copy-done.14
  38.5 5.3 %filter_layout.1.filt_ref = bf16[2,2,2048,128]{3,2,1,0:T(8,128)(2,1)} custom-call(s32[1]{0:T(128)} %bitcast.refs_0_.half_ref, f32[2,4,64,2048]{3,2,1,0:T(8,128)} %own_ref.1, bf16[2,64,2048]{2,1,0:T(8,128)(2,1)} %collective-permute-done.early_ref, bf16[2,64,2048]{2,1,0:T(8,128)(2,1)} %collective-permute-done.1.late_ref, bf16[16,2048]{1,0:T(8,128)(2,1)} %copy-done.14, ...), custom_call_target="tpu_custom_call" | custom-call | flops 600000000 | bytes 5000000 | tf_op jit(solution)/shard_map/filter_layout/pallas_call | solution.py:275
  43.8 9.7 %all-to-all-done.1.y_ref = bf16[16,2,128,128]{3,2,1,0:T(8,128)(2,1)S(1)} async-done(((bf16[16,2,128,128]{3,2,1,0:T(8,128)(2,1)}), bf16[16,2,128,128]{3,2,1,0:T(8,128)(2,1)S(1)}, u32[]{:S(2)}, u32[]{:S(2)}) %all-to-all-start.1) | async-done | bytes 1048608 | tf_op jit(solution)/shard_map/all_to_all | solution.py:484
  53.5 1.6 %copy-done = bf16[2,2,2048,128]{3,2,1,0:T(8,128)(2,1)S(1)} copy-done((bf16[2,2,2048,128]{3,2,1,0:T(8,128)(2,1)S(1)}, bf16[2,2,2048,128]{3,2,1,0:T(8,128)(2,1)}, u32[]{:S(2)}) %copy-start) | copy-done | bytes 2097176
  55.1 4.3 %column_step.1 = bf16[16,2,128,128]{3,2,1,0:T(8,128)(2,1)S(1)} custom-call(bf16[16,2,128,128]{3,2,1,0:T(8,128)(2,1)S(1)} %all-to-all-done.1.y_ref, bf16[2,2,2048,128]{3,2,1,0:T(8,128)(2,1)S(1)} %copy-done, bf16[6,256,256]{2,1,0:T(8,128)(2,1)S(1)} %broadcast_multiply_fusion.step_ref, f32[2,2,128,128]{3,2,1,0:T(8,128)S(1)} %copy-done.3, ...), custom_call_target="tpu_custom_call" | custom-call | flops 2000000000 | bytes 5000000 | tf_op jit(solution)/shard_map/column_step/pallas_call | solution.py:401
  59.5 0.0 copy-start.2
  59.5 19.2 %all_to_all.20.z_ref = bf16[16,2,128,128]{3,2,1,0:T(8,128)(2,1)S(1)} all-to-all(bf16[16,2,128,128]{3,2,1,0:T(8,128)(2,1)S(1)} %column_step.1), channel_id=1, replica_groups=mesh['row'=8,'col'=16] {'col'}, dimensions={0} | all-to-all | bytes 2097152 | tf_op jit(solution)/shard_map/all_to_all | solution.py:494
  78.7 2.8 %row_inverse.1 = bf16[8,4,64,128]{3,2,1,0:T(8,128)(2,1)S(1)} custom-call(bf16[16,2,128,128]{3,2,1,0:T(8,128)(2,1)S(1)} %all_to_all.20.z_ref, bf16[512,2048]{1,0:T(8,128)(2,1)S(1)} %copy-done.2, bf16[128,128]{1,0:T(8,128)(2,1)S(1)} %copy-done.5), custom_call_target="tpu_custom_call" | custom-call | flops 1100000000 | bytes 4000000 | tf_op jit(solution)/shard_map/row_inverse/pallas_call | solution.py:443
  81.6 16.7 %all_to_all.21 = bf16[32,64,128]{2,1,0:T(8,128)(2,1)S(1)} all-to-all(bf16[32,64,128]{2,1,0:T(8,128)(2,1)S(1)} %bitcast.5), channel_id=1, replica_groups=mesh['row'=8,'col'=16] {'row'}, dimensions={0} | all-to-all | bytes 1048576 | tf_op jit(solution)/shard_map/all_to_all | solution.py:497
  98.3 1.3 %add_multiply_fusion = f32[32,64,128]{2,1,0:T(8,128)} fusion(bf16[32,64,128]{2,1,0:T(8,128)(2,1)S(1)} %all_to_all.21, bf16[32,64,128]{2,1,0:T(8,128)(2,1)S(1)} %copy-done.11, bf16[32,64,128]{2,1,0:T(8,128)(2,1)S(1)} %copy-done.7, bf16[32,64,128]{2,1,0:T(8,128)(2,1)S(1)} %copy-done.9, f32[32]{0:T(128)S(1)} %copy-done.16), kind=kLoop, calls=%fused_computation | loop fusion | flops 2097152 | bytes 3145856 | tf_op jit(solution)/shard_map/mul | solution.py:499
  (35 shorter events, 0.1 us)
Async XLA Ops:
  0.0 7.4 %copy-start.6 = (bf16[32,64,128]{2,1,0:T(8,128)(2,1)S(1)}, bf16[32,64,128]{2,1,0:T(8,128)(2,1)}, u32[]{:S(2)}) copy-start(bf16[32,64,128]{2,1,0:T(8,128)(2,1)} %param.15) | copy-start | bytes 1572868
  0.0 7.4 %copy-start.8 = (bf16[32,64,128]{2,1,0:T(8,128)(2,1)S(1)}, bf16[32,64,128]{2,1,0:T(8,128)(2,1)}, u32[]{:S(2)}) copy-start(bf16[32,64,128]{2,1,0:T(8,128)(2,1)} %param.14) | copy-start | bytes 1572868
  2.6 35.2 %collective-permute-start.2 = (bf16[16,2048]{1,0:T(8,128)(2,1)}, bf16[16,2048]{1,0:T(8,128)(2,1)S(1)}, u32[]{:S(2)}, u32[]{:S(2)}) collective-permute-start(bf16[16,2048]{1,0:T(8,128)(2,1)} %get-tuple-element.10), channel_id=1, source_target_pairs={{0,8},{1,15},{2,14},{3,13},{4,12},{5,11},{6,10},{7,9},{8,0},{9,7},... | collective-permute-start | bytes 196616 | tf_op jit(solution)/shard_map/ppermute | solution.py:471
  4.4 33.5 %collective-permute-start = (bf16[2,64,2048]{2,1,0:T(8,128)(2,1)}, bf16[2,64,2048]{2,1,0:T(8,128)(2,1)}, u32[]{:S(2)}, u32[]{:S(2)}) collective-permute-start(bf16[2,64,2048]{2,1,0:T(8,128)(2,1)} %get-tuple-element.8), channel_id=1, source_target_pairs={{0,15},{1,14},{2,13},{3,12},{4,11},{5,10},{6,9},{7,8},{8,7},{9,6},... | collective-permute-start | bytes 1572872 | tf_op jit(solution)/shard_map/ppermute | solution.py:470
  8.4 20.7 %all-to-all-start = ((bf16[32,64,128]{2,1,0:T(8,128)(2,1)}), bf16[32,64,128]{2,1,0:T(8,128)(2,1)S(1)}, u32[]{:S(2)}, u32[]{:S(2)}) async-start(bf16[32,64,128]{2,1,0:T(8,128)(2,1)} %fusion.refs_2_), calls=%async_computation | async-start | bytes 1048576 | tf_op jit(solution)/shard_map/all_to_all | solution.py:475
  15.0 2.5 %copy-start.15 = (s32[128]{0:T(128)S(1)}, s32[128]{0:T(128)}, u32[]{:S(2)}) copy-start(s32[128]{0:T(128)} %constant.125.clone) | copy-start | bytes 1540
  15.0 14.0 %copy-start.1 = (bf16[512,2048]{1,0:T(8,128)(2,1)S(1)}, bf16[512,2048]{1,0:T(8,128)(2,1)}, u32[]{:S(2)}) copy-start(bf16[512,2048]{1,0:T(8,128)(2,1)} %constant.120.clone.table_ref) | copy-start | bytes 6291460
  15.0 14.0 %copy-start.4 = (f32[3,128,128]{2,1,0:T(8,128)S(1)}, f32[3,128,128]{2,1,0:T(8,128)}, u32[]{:S(2)}) copy-start(f32[3,128,128]{2,1,0:T(8,128)} %constant.124.clone.base_ref) | copy-start | bytes 589828
  15.0 14.0 %copy-start.5 = (bf16[128,128]{1,0:T(8,128)(2,1)S(1)}, bf16[128,128]{1,0:T(8,128)(2,1)}, u32[]{:S(2)}) copy-start(bf16[128,128]{1,0:T(8,128)(2,1)} %constant.121.clone.order_ref) | copy-start | bytes 98308
  17.2 20.7 %collective-permute-start.1 = (bf16[2,64,2048]{2,1,0:T(8,128)(2,1)}, bf16[2,64,2048]{2,1,0:T(8,128)(2,1)}, u32[]{:S(2)}, u32[]{:S(2)}) collective-permute-start(bf16[2,64,2048]{2,1,0:T(8,128)(2,1)} %filter_send.3), channel_id=1, source_target_pairs={{0,15},{1,14},{2,13},{3,12},{4,11},{5,10},{6,9},{7,8},{8,7},{9,6},... | collective-permute-start | bytes 1572872 | tf_op jit(solution)/shard_map/ppermute | solution.py:476
  32.1 4.9 %copy-start.12 = (bf16[2,272,256]{2,1,0:T(8,128)(2,1)S(1)}, bf16[2,272,256]{2,1,0:T(8,128)(2,1)}, u32[]{:S(2)}) copy-start(bf16[2,272,256]{2,1,0:T(8,128)(2,1)} %constant.123.clone) | copy-start | bytes 835588
  32.1 4.9 %copy-start.13 = (bf16[2,272,256]{2,1,0:T(8,128)(2,1)S(1)}, bf16[2,272,256]{2,1,0:T(8,128)(2,1)}, u32[]{:S(2)}) copy-start(bf16[2,272,256]{2,1,0:T(8,128)(2,1)} %constant.122.clone) | copy-start | bytes 835588
  32.1 5.6 %copy-start.10 = (bf16[6,256,256]{2,1,0:T(8,128)(2,1)S(1)}, bf16[6,256,256]{2,1,0:T(8,128)(2,1)}, u32[]{:S(2)}) copy-start(bf16[6,256,256]{2,1,0:T(8,128)(2,1)} %constant.127.clone) | copy-start | bytes 2359300
  32.1 21.4 %all-to-all-start.1 = ((bf16[16,2,128,128]{3,2,1,0:T(8,128)(2,1)}), bf16[16,2,128,128]{3,2,1,0:T(8,128)(2,1)S(1)}, u32[]{:S(2)}, u32[]{:S(2)}) async-start(bf16[16,2,128,128]{3,2,1,0:T(8,128)(2,1)} %row_forward.1), calls=%async_computation.1 | async-start | bytes 2097152 | tf_op jit(solution)/shard_map/all_to_all | solution.py:484
  37.8 15.7 %copy-start.3 = (f32[2,2,128,128]{3,2,1,0:T(8,128)S(1)}, f32[2,2,128,128]{3,2,1,0:T(8,128)}, u32[]{:S(2)}) copy-start(f32[2,2,128,128]{3,2,1,0:T(8,128)} %constant.146.mid_ref) | copy-start | bytes 786436
  37.9 0.6 copy-start.14
  53.5 1.6 %copy-start = (bf16[2,2,2048,128]{3,2,1,0:T(8,128)(2,1)S(1)}, bf16[2,2,2048,128]{3,2,1,0:T(8,128)(2,1)}, u32[]{:S(2)}) copy-start(bf16[2,2,2048,128]{3,2,1,0:T(8,128)(2,1)} %filter_layout.1.filt_ref) | copy-start | bytes 6291460
  59.5 19.3 %copy-start.2 = (bf16[512,2048]{1,0:T(8,128)(2,1)S(1)}, bf16[512,2048]{1,0:T(8,128)(2,1)}, u32[]{:S(2)}) copy-start(bf16[512,2048]{1,0:T(8,128)(2,1)} %constant.120.clone.table_ref) | copy-start | bytes 6291460
  78.7 19.6 %copy-start.7 = (bf16[32,64,128]{2,1,0:T(8,128)(2,1)S(1)}, bf16[32,64,128]{2,1,0:T(8,128)(2,1)}, u32[]{:S(2)}) copy-start(bf16[32,64,128]{2,1,0:T(8,128)(2,1)} %param.15) | copy-start | bytes 1572868
  78.7 19.6 %copy-start.9 = (bf16[32,64,128]{2,1,0:T(8,128)(2,1)S(1)}, bf16[32,64,128]{2,1,0:T(8,128)(2,1)}, u32[]{:S(2)}) copy-start(bf16[32,64,128]{2,1,0:T(8,128)(2,1)} %param.14) | copy-start | bytes 1572868
  78.7 19.6 %copy-start.11 = (bf16[32,64,128]{2,1,0:T(8,128)(2,1)S(1)}, bf16[32,64,128]{2,1,0:T(8,128)(2,1)}, u32[]{:S(2)}) copy-start(bf16[32,64,128]{2,1,0:T(8,128)(2,1)} %param.13) | copy-start | bytes 1572868
  78.7 19.6 %copy-start.16 = (f32[32]{0:T(128)S(1)}, f32[32]{0:T(128)}, u32[]{:S(2)}) copy-start(f32[32]{0:T(128)} %param.17) | copy-start | bytes 388

commit v4 on v3

--- a/solution.py
+++ b/solution.py
@@ -39,6 +39,11 @@
     sines[:, 0] = 1.0 - 2.0 * (np.arange(HALF) % 2)
     parts = np.stack([cosines, sines], 0).reshape(2, HALF, BLOCKS, PER).transpose(1, 2, 0, 3)
     return narrow(np.repeat(parts[:, :, :, None, :], 2, 3).reshape(HALF, BLOCKS * 2 * 2 * PER))
+
+
+def row_forward_table():
+    both = row_table().reshape(HALF, BLOCKS, 2, 2, PER)
+    return both[:, :, :, 0].reshape(HALF, BLOCKS * 2 * PER)
 
 
 def pair_order(table, first, second):
@@ -122,9 +127,9 @@
 
 def filter_send_body(part, *refs):
     if part == 0:
-        half_ref, spec_hbm, send_hbm, rows_ref, wide_ref, narrow_ref, in_sems, out_sems, lead_ref = refs
+        half_ref, spec_hbm, send_ref, rows_ref, wide_ref, in_sems, lead_ref = refs
     else:
-        half_ref, spec_hbm, ahead_ref, send_hbm, wide_ref, narrow_ref, in_sems, out_sems = refs
+        half_ref, spec_hbm, ahead_ref, send_hbm, wide_ref, in_sems, send_ref, out_sems = refs
     away = 2 * (1 - half_ref[0])
     loads, stores = [], []
 
@@ -136,11 +141,6 @@
         for cut in range(2):
             rows = pl.ds(cut * 32, 32)
             load(spec_hbm.at[part, away + chan, rows], wide_ref.at[chan, rows])
-            stores.append(
-                pltpu.make_async_copy(
-                    narrow_ref.at[chan, rows], send_hbm.at[chan, rows], out_sems.at[2 * chan + cut]
-                )
-            )
     if part == 0:
         for chan in range(2):
             load(spec_hbm.at[1, away + chan, pl.ds(0, 8)], lead_ref.at[chan])
@@ -148,8 +148,14 @@
         for cut in range(2):
             rows = pl.ds(cut * 32, 32)
             loads[2 * chan + cut].wait()
-            narrow_ref[chan, rows] = wide_ref[chan, rows].astype(BF16)
-            stores[2 * chan + cut].start()
+            send_ref[chan, rows] = wide_ref[chan, rows].astype(BF16)
+            if part == 1:
+                stores.append(
+                    pltpu.make_async_copy(
+                        send_ref.at[chan, rows], send_hbm.at[chan, rows], out_sems.at[2 * chan + cut]
+                    )
+                )
+                stores[-1].start()
     if part == 0:
         for copy in loads[4:]:
             copy.wait()
@@ -165,38 +171,32 @@
     return pl.pallas_call(
         functools.partial(filter_send_body, part),
         in_specs=[pl.BlockSpec(memory_space=pltpu.SMEM), anywhere] + ([] if first else [anywhere]),
-        out_specs=[anywhere] + ([pl.BlockSpec(memory_space=pltpu.VMEM)] if first else []),
-        out_shape=[jax.ShapeDtypeStruct((2, PER, COLS), BF16)]
-        + ([jax.ShapeDtypeStruct((16, COLS), BF16)] if first else []),
+        out_specs=[pl.BlockSpec(memory_space=pltpu.VMEM)] * 2 if first else [anywhere],
+        out_shape=[pltpu.VMEM((2, PER, COLS), BF16), jax.ShapeDtypeStruct((16, COLS), BF16)]
+        if first
+        else [jax.ShapeDtypeStruct((2, PER, COLS), BF16)],
         scratch_shapes=[
             pltpu.VMEM((2, PER, COLS), F32),
-            pltpu.VMEM((2, PER, COLS), BF16),
             pltpu.SemaphoreType.DMA((6,)),
-            pltpu.SemaphoreType.DMA((4,)),
         ]
-        + ([pltpu.VMEM((2, 8, COLS), F32)] if first else []),
-        compiler_params=pltpu.CompilerParams(vmem_limit_bytes=61 * 1024 * 1024),
+        + (
+            [pltpu.VMEM((2, 8, COLS), F32)]
+            if first
+            else [pltpu.VMEM((2, PER, COLS), BF16), pltpu.SemaphoreType.DMA((4,))]
+        ),
+        compiler_params=pltpu.CompilerParams(vmem_limit_bytes=(61 if first else 59) * 1024 * 1024),
         cost_estimate=pl.CostEstimate(flops=0, bytes_accessed=1_700_000, transcendentals=0),
         name="filter_send",
     )(*([half, spec] if first else [half, spec, ahead]))
 
 
 def row_forward_body(
-    x_hbm, table_ref, base_ref, phase_ref, order_ref, out_ref, x_ref, turned_ref, sems,
+    x_ref, table_ref, base_ref, phase_ref, order_ref, out_ref, turned_ref,
 ):
-    copies = []
-
-    def fetch(source, target):
-        copies.append(pltpu.make_async_copy(source, target, sems.at[len(copies)]))
-        copies[-1].start()
-        return copies[-1]
-
-    x_copies = [fetch(x_hbm.at[:, chan], x_ref.at[chan]) for chan in range(4)]
     for chan in range(4):
-        x_copies[chan].wait()
         turned_ref[chan * LANES : (chan + 1) * LANES, :] = lax.dot_general(
             order_ref[...],
-            x_ref[chan].reshape(HALF, LANES),
+            x_ref[:, chan].reshape(HALF, LANES),
             (((1,), (1,)), ((), ())),
             preferred_element_type=F32,
         ).astype(BF16)
@@ -214,18 +214,20 @@
 
     high = []
     for block in range(BLOCKS):
-        sums = jnp.dot(
-            turned_ref[...], table_ref[:, block * 256 : (block + 1) * 256], preferred_element_type=F32
-        )
+        if block % 2 == 0:
+            sums = jnp.dot(
+                turned_ref[...], table_ref[:, block * LANES : (block + 2) * LANES], preferred_element_type=F32
+            )
         cosine, sine = rotate(
             *own, base_ref[1, :, block : block + 1], base_ref[2, :, block : block + 1]
         )
         cosine, sine = rotate(cosine, sine, phase_ref[0, block], phase_ref[1, block])
         for pair in range(2):
-            upper = sums[pair * 256 : pair * 256 + 128]
-            lower = sums[pair * 256 + 128 : pair * 256 + 256]
-            real = jnp.where(first, upper[:, :LANES], lower[:, :LANES])
-            imag = jnp.where(first, upper[:, LANES:], lower[:, LANES:])
+            lanes = slice(block % 2 * LANES, block % 2 * LANES + LANES)
+            upper = sums[pair * 256 : pair * 256 + 128, lanes]
+            lower = sums[pair * 256 + 128 : pair * 256 + 256, lanes]
+            real = jnp.where(first, upper, pltpu.roll(lower, PER, 1))
+            imag = jnp.where(first, pltpu.roll(upper, PER, 1), lower)
             real, imag = rotate(real, imag, cosine, -sine)
             if pair == 0:
                 emit(block, real, imag)
@@ -237,18 +239,15 @@
 
 
 def row_forward(x, table, base, phase, order):
-    anywhere = pl.BlockSpec(memory_space=pl.ANY)
     inside = pl.BlockSpec(memory_space=pltpu.VMEM)
     block = (16, 2, LANES, LANES)
     return pl.pallas_call(
         row_forward_body,
-        in_specs=[anywhere, inside, inside, inside, inside],
+        in_specs=[inside] * 5,
         out_specs=inside,
         out_shape=jax.ShapeDtypeStruct(block, BF16),
         scratch_shapes=[
-            pltpu.VMEM((4, 8, 64, LANES), BF16),
             pltpu.VMEM((4 * LANES, HALF), BF16),
-            pltpu.SemaphoreType.DMA((4,)),
         ],
         compiler_params=pltpu.CompilerParams(vmem_limit_bytes=16 * 1024 * 1024),
         cost_estimate=pl.CostEstimate(flops=1_100_000_000, bytes_accessed=5_000_000, transcendentals=0),
@@ -480,7 +479,7 @@
     lane = jnp.arange(LANES, dtype=jnp.int32) % PER
     all_k1 = (PER * jnp.arange(BLOCKS, dtype=jnp.int32))[:, None, None] + lane[None, None, :]
     phase = turn(all_k1, col, ROWS * 16)
-    y = row_forward(x.reshape(8, 4, 64, LANES), table, twist_base(), phase, order)
+    y = row_forward(x.reshape(8, 4, 64, LANES), jnp.asarray(row_forward_table()), twist_base(), phase, order)
     y = lax.all_to_all(y, "col", split_axis=0, concat_axis=0, tiled=True)
 
     own_k1 = PER * jnp.where(low_side, col, jnp.where(lane == 0, (16 - col) % 8, 15 - col)) + lane

time: 100 us -> 99.6 us (level)
  Pallas kernels: 20.2 us -> 18.7 us
  blocking collectives: 35.9 us -> 37.2 us
  other arithmetic: 3.73 us -> 4.87 us
    mul x1, other arithmetic: 0.06 us -> 1.19 us  [per_device(): steps = jnp.asarray(step_tables()) * (col >= 0).astype(BF16)]
    unnamed x34 -> x28, local copies, waits for them, and re-layouts: 2.26 us -> 1.66 us
  transfers between devices with their start and end apart: 5 -> 5, of which waited for: 2 -> 2; matrix products, arithmetic and copies ran while one was open for 2% -> 4% of each run, Pallas kernels for 10% -> 10%
where the time goes in v4:
time: 99.6 us; the launch traced here: 99 us
  blocking collectives  37.2 us (37%)
  waiting for transfers between devices  20.6 us (21%)
  Pallas kernels  18.7 us (19%)
  starting transfers between devices  15.8 us (16%)
  other arithmetic  4.87 us (5%)
  local copies, waits for them, and re-layouts  1.66 us (2%)
    all_to_all x1, blocking collectives, per_device(): z = lax.all_to_all(z, 'col', split_axis=0, concat_axis=0, tiled=True)  19.6 us
    all_to_all x1, blocking collectives, per_device(): lax.all_to_all(convolved, 'row', split_axis=0, concat_axis=0, tiled=True)  17.6 us
    all_to_all x1, waiting for transfers between devices, per_device(): x = lax.all_to_all(gated, 'row', split_axis=0, concat_axis=0, tiled=True)  11.4 us
    all_to_all x1, waiting for transfers between devices, per_device(): y = lax.all_to_all(y, 'col', split_axis=0, concat_axis=0, tiled=True)  9.21 us
    all_to_all x1, starting transfers between devices, per_device(): x = lax.all_to_all(gated, 'row', split_axis=0, concat_axis=0, tiled=True)  6.64 us
    pallas_call x1, Pallas kernels, filter_layout(): pl.pallas_call(filter_body, grid_spec=pltpu.PrefetchScalarGridSpec(num_sc...  5.29 us
    pallas_call x1, Pallas kernels, column_step(): pl.pallas_call(column_body, in_specs=[inside] * 7, out_specs=inside, out_...  4.34 us
    all_to_all x1, starting transfers between devices, per_device(): y = lax.all_to_all(y, 'col', split_axis=0, concat_axis=0, tiled=True)  4.3 us
  transfers between devices with their start and end apart: 5, of which 2 were waited for; matrix products, arithmetic and copies ran while one was open for 4% of the time, Pallas kernels for 10%

profile of v4, /device:TPU:0, one launch (start us, length us, event | category | flops | bytes accessed | tf_op | source)
XLA Modules:
  0.0 99.0 jit_solution(6593107116772271700)
XLA Ops:
  0.0 2.0 %filter_send.2 = (bf16[2,64,2048]{2,1,0:T(8,128)(2,1)S(1)}, bf16[16,2048]{1,0:T(8,128)(2,1)}) custom-call(s32[1]{0:T(128)} %bitcast.refs_0_.half_ref, f32[2,4,64,2048]{3,2,1,0:T(8,128)} %own_ref.1), custom_call_target="tpu_custom_call" | custom-call | bytes 1700000 | tf_op jit(solution)/shard_map/filter_send/pallas_call | solution.py:171
  2.0 1.7 %collective-permute-start.2 = (bf16[16,2048]{1,0:T(8,128)(2,1)}, bf16[16,2048]{1,0:T(8,128)(2,1)}, u32[]{:S(2)}, u32[]{:S(2)}) collective-permute-start(bf16[16,2048]{1,0:T(8,128)(2,1)} %get-tuple-element.10), channel_id=1, source_target_pairs={{0,8},{1,15},{2,14},{3,13},{4,12},{5,11},{6,10},{7,9},{8,0},{9,7},... | collective-permute-start | bytes 196616 | tf_op jit(solution)/shard_map/ppermute | solution.py:470
  3.8 3.0 %collective-permute-start = (bf16[2,64,2048]{2,1,0:T(8,128)(2,1)S(1)}, bf16[2,64,2048]{2,1,0:T(8,128)(2,1)}, u32[]{:S(2)}, u32[]{:S(2)}) collective-permute-start(bf16[2,64,2048]{2,1,0:T(8,128)(2,1)S(1)} %get-tuple-element.8), channel_id=1, source_target_pairs={{0,15},{1,14},{2,13},{3,12},{4,11},{5,10},{6,9},{7,8},{8,7},{9,6},... | collective-permute-start | bytes 1572872 | tf_op jit(solution)/shard_map/ppermute | solution.py:469
  6.8 1.0 fusion.refs_2_
  7.7 6.6 %all-to-all-start = ((bf16[32,64,128]{2,1,0:T(8,128)(2,1)}), bf16[32,64,128]{2,1,0:T(8,128)(2,1)S(1)}, u32[]{:S(2)}, u32[]{:S(2)}) async-start(bf16[32,64,128]{2,1,0:T(8,128)(2,1)} %fusion.refs_2_), calls=%async_computation | async-start | bytes 1048576 | tf_op jit(solution)/shard_map/all_to_all | solution.py:474
  14.4 0.0 copy-start.2
  14.4 0.0 copy-start.4
  14.4 0.0 copy-start.5
  14.4 2.1 %filter_send.3 = bf16[2,64,2048]{2,1,0:T(8,128)(2,1)} custom-call(s32[1]{0:T(128)} %bitcast.refs_0_.half_ref, f32[2,4,64,2048]{3,2,1,0:T(8,128)} %own_ref.1, bf16[32,64,128]{2,1,0:T(8,128)(2,1)} %fusion.refs_2_), custom_call_target="tpu_custom_call" | custom-call | bytes 1700000 | tf_op jit(solution)/shard_map/filter_send/pallas_call | solution.py:171
  16.5 0.1 collective-permute-start.1
  16.6 0.1 fusion.13
  16.7 0.1 multiply_cosine_fusion
  16.9 0.3 fusion.5
  17.2 11.4 %all-to-all-done = bf16[32,64,128]{2,1,0:T(8,128)(2,1)S(1)} async-done(((bf16[32,64,128]{2,1,0:T(8,128)(2,1)}), bf16[32,64,128]{2,1,0:T(8,128)(2,1)S(1)}, u32[]{:S(2)}, u32[]{:S(2)}) %all-to-all-start) | async-done | bytes 524320 | tf_op jit(solution)/shard_map/all_to_all | solution.py:474
  28.6 0.0 copy-start.10
  28.6 0.0 copy-start.11
  28.6 2.2 %row_forward.1 = bf16[16,2,128,128]{3,2,1,0:T(8,128)(2,1)} custom-call(bf16[8,4,64,128]{3,2,1,0:T(8,128)(2,1)S(1)} %bitcast.4, bf16[512,1024]{1,0:T(8,128)(2,1)S(1)} %copy-done.2, f32[3,128,128]{2,1,0:T(8,128)S(1)} %copy-done.4, f32[2,8,1,128]{3,2,1,0:T(1,128)S(1)} %pad_maximum_fusion.2.phase_ref, bf16[128,128]{1,0:T(8,128)(2,1)S(1)} %copy-done.5), custom_call_target="tpu_custom_call" | custom-call | flops 1100000000 | bytes 5000000 | tf_op jit(solution)/shard_map/row_forward/pallas_call | solution.py:244
  30.8 4.3 %all-to-all-start.1 = ((bf16[16,2,128,128]{3,2,1,0:T(8,128)(2,1)}), bf16[16,2,128,128]{3,2,1,0:T(8,128)(2,1)S(1)}, u32[]{:S(2)}, u32[]{:S(2)}) async-start(bf16[16,2,128,128]{3,2,1,0:T(8,128)(2,1)} %row_forward.1), calls=%async_computation.1 | async-start | bytes 2097152 | tf_op jit(solution)/shard_map/all_to_all | solution.py:483
  35.2 0.1 fusion.15
  35.2 0.7 broadcast_select_fusion.moves_ref
  36.0 1.2 %broadcast_multiply_fusion.step_ref = bf16[6,256,256]{2,1,0:T(8,128)(2,1)S(1)} fusion(bf16[6,256,256]{2,1,0:T(8,128)(2,1)} %constant.130.clone, bf16[]{:T(256)S(6)} %convert_element_type.83), kind=kLoop, calls=%fused_computation.3 | loop fusion | flops 393216 | bytes 1572866 | tf_op jit(solution)/shard_map/mul | solution.py:491
  37.2 0.0 copy-start.3
  37.2 0.0 collective-permute-done.2.extra_ref
  37.2 5.3 %filter_layout.1.filt_ref = bf16[2,2,2048,128]{3,2,1,0:T(8,128)(2,1)} custom-call(s32[1]{0:T(128)} %bitcast.refs_0_.half_ref, f32[2,4,64,2048]{3,2,1,0:T(8,128)} %own_ref.1, bf16[2,64,2048]{2,1,0:T(8,128)(2,1)} %collective-permute-done.early_ref, bf16[2,64,2048]{2,1,0:T(8,128)(2,1)} %collective-permute-done.1.late_ref, ...), custom_call_target="tpu_custom_call" | custom-call | flops 600000000 | bytes 5000000 | tf_op jit(solution)/shard_map/filter_layout/pallas_call | solution.py:274
  42.5 9.2 %all-to-all-done.1.y_ref = bf16[16,2,128,128]{3,2,1,0:T(8,128)(2,1)S(1)} async-done(((bf16[16,2,128,128]{3,2,1,0:T(8,128)(2,1)}), bf16[16,2,128,128]{3,2,1,0:T(8,128)(2,1)S(1)}, u32[]{:S(2)}, u32[]{:S(2)}) %all-to-all-start.1) | async-done | bytes 1048608 | tf_op jit(solution)/shard_map/all_to_all | solution.py:483
  51.8 1.6 %copy-done = bf16[2,2,2048,128]{3,2,1,0:T(8,128)(2,1)S(1)} copy-done((bf16[2,2,2048,128]{3,2,1,0:T(8,128)(2,1)S(1)}, bf16[2,2,2048,128]{3,2,1,0:T(8,128)(2,1)}, u32[]{:S(2)}) %copy-start) | copy-done | bytes 2097176
  53.3 4.3 %column_step.1 = bf16[16,2,128,128]{3,2,1,0:T(8,128)(2,1)S(1)} custom-call(bf16[16,2,128,128]{3,2,1,0:T(8,128)(2,1)S(1)} %all-to-all-done.1.y_ref, bf16[2,2,2048,128]{3,2,1,0:T(8,128)(2,1)S(1)} %copy-done, bf16[6,256,256]{2,1,0:T(8,128)(2,1)S(1)} %broadcast_multiply_fusion.step_ref, f32[2,2,128,128]{3,2,1,0:T(8,128)S(1)} %copy-done.3, ...), custom_call_target="tpu_custom_call" | custom-call | flops 2000000000 | bytes 5000000 | tf_op jit(solution)/shard_map/column_step/pallas_call | solution.py:400
  57.7 0.0 copy-start.1
  57.7 19.6 %all_to_all.20.z_ref = bf16[16,2,128,128]{3,2,1,0:T(8,128)(2,1)S(1)} all-to-all(bf16[16,2,128,128]{3,2,1,0:T(8,128)(2,1)S(1)} %column_step.1), channel_id=1, replica_groups=mesh['row'=8,'col'=16] {'col'}, dimensions={0} | all-to-all | bytes 2097152 | tf_op jit(solution)/shard_map/all_to_all | solution.py:493
  77.3 2.8 %row_inverse.1 = bf16[8,4,64,128]{3,2,1,0:T(8,128)(2,1)S(1)} custom-call(bf16[16,2,128,128]{3,2,1,0:T(8,128)(2,1)S(1)} %all_to_all.20.z_ref, bf16[512,2048]{1,0:T(8,128)(2,1)S(1)} %copy-done.1, bf16[128,128]{1,0:T(8,128)(2,1)S(1)} %copy-done.5), custom_call_target="tpu_custom_call" | custom-call | flops 1100000000 | bytes 4000000 | tf_op jit(solution)/shard_map/row_inverse/pallas_call | solution.py:442
  80.2 17.6 %all_to_all.21 = bf16[32,64,128]{2,1,0:T(8,128)(2,1)S(1)} all-to-all(bf16[32,64,128]{2,1,0:T(8,128)(2,1)S(1)} %bitcast.5), channel_id=1, replica_groups=mesh['row'=8,'col'=16] {'row'}, dimensions={0} | all-to-all | bytes 1048576 | tf_op jit(solution)/shard_map/all_to_all | solution.py:496
  97.8 1.3 %add_multiply_fusion = f32[32,64,128]{2,1,0:T(8,128)} fusion(bf16[32,64,128]{2,1,0:T(8,128)(2,1)S(1)} %all_to_all.21, bf16[32,64,128]{2,1,0:T(8,128)(2,1)S(1)} %copy-done.9, bf16[32,64,128]{2,1,0:T(8,128)(2,1)S(1)} %copy-done.6, bf16[32,64,128]{2,1,0:T(8,128)(2,1)S(1)} %copy-done.8, f32[32]{0:T(128)S(1)} %copy-done.13), kind=kLoop, calls=%fused_computation | loop fusion | flops 2097152 | bytes 3145856 | tf_op jit(solution)/shard_map/mul | solution.py:498
  (29 shorter events, 0.1 us)
Async XLA Ops:
  0.0 6.8 %copy-start.6 = (bf16[32,64,128]{2,1,0:T(8,128)(2,1)S(1)}, bf16[32,64,128]{2,1,0:T(8,128)(2,1)}, u32[]{:S(2)}) copy-start(bf16[32,64,128]{2,1,0:T(8,128)(2,1)} %param.16) | copy-start | bytes 1572868
  0.0 6.8 %copy-start.7 = (bf16[32,64,128]{2,1,0:T(8,128)(2,1)S(1)}, bf16[32,64,128]{2,1,0:T(8,128)(2,1)}, u32[]{:S(2)}) copy-start(bf16[32,64,128]{2,1,0:T(8,128)(2,1)} %param.15) | copy-start | bytes 1572868
  2.0 35.2 %collective-permute-start.2 = (bf16[16,2048]{1,0:T(8,128)(2,1)}, bf16[16,2048]{1,0:T(8,128)(2,1)}, u32[]{:S(2)}, u32[]{:S(2)}) collective-permute-start(bf16[16,2048]{1,0:T(8,128)(2,1)} %get-tuple-element.10), channel_id=1, source_target_pairs={{0,8},{1,15},{2,14},{3,13},{4,12},{5,11},{6,10},{7,9},{8,0},{9,7},... | collective-permute-start | bytes 196616 | tf_op jit(solution)/shard_map/ppermute | solution.py:470
  3.8 33.5 %collective-permute-start = (bf16[2,64,2048]{2,1,0:T(8,128)(2,1)S(1)}, bf16[2,64,2048]{2,1,0:T(8,128)(2,1)}, u32[]{:S(2)}, u32[]{:S(2)}) collective-permute-start(bf16[2,64,2048]{2,1,0:T(8,128)(2,1)S(1)} %get-tuple-element.8), channel_id=1, source_target_pairs={{0,15},{1,14},{2,13},{3,12},{4,11},{5,10},{6,9},{7,8},{8,7},{9,6},... | collective-permute-start | bytes 1572872 | tf_op jit(solution)/shard_map/ppermute | solution.py:469
  7.7 20.9 %all-to-all-start = ((bf16[32,64,128]{2,1,0:T(8,128)(2,1)}), bf16[32,64,128]{2,1,0:T(8,128)(2,1)S(1)}, u32[]{:S(2)}, u32[]{:S(2)}) async-start(bf16[32,64,128]{2,1,0:T(8,128)(2,1)} %fusion.refs_2_), calls=%async_computation | async-start | bytes 1048576 | tf_op jit(solution)/shard_map/all_to_all | solution.py:474
  14.4 2.5 %copy-start.12 = (s32[128]{0:T(128)S(1)}, s32[128]{0:T(128)}, u32[]{:S(2)}) copy-start(s32[128]{0:T(128)} %constant.128.clone) | copy-start | bytes 1540
  14.4 14.2 %copy-start.2 = (bf16[512,1024]{1,0:T(8,128)(2,1)S(1)}, bf16[512,1024]{1,0:T(8,128)(2,1)}, u32[]{:S(2)}) copy-start(bf16[512,1024]{1,0:T(8,128)(2,1)} %constant.126.clone.table_ref) | copy-start | bytes 3145732
  14.4 14.2 %copy-start.4 = (f32[3,128,128]{2,1,0:T(8,128)S(1)}, f32[3,128,128]{2,1,0:T(8,128)}, u32[]{:S(2)}) copy-start(f32[3,128,128]{2,1,0:T(8,128)} %constant.127.clone.base_ref) | copy-start | bytes 589828
  14.4 14.2 %copy-start.5 = (bf16[128,128]{1,0:T(8,128)(2,1)S(1)}, bf16[128,128]{1,0:T(8,128)(2,1)}, u32[]{:S(2)}) copy-start(bf16[128,128]{1,0:T(8,128)(2,1)} %constant.123.clone.order_ref) | copy-start | bytes 98308
  16.5 20.7 %collective-permute-start.1 = (bf16[2,64,2048]{2,1,0:T(8,128)(2,1)}, bf16[2,64,2048]{2,1,0:T(8,128)(2,1)}, u32[]{:S(2)}, u32[]{:S(2)}) collective-permute-start(bf16[2,64,2048]{2,1,0:T(8,128)(2,1)} %filter_send.3), channel_id=1, source_target_pairs={{0,15},{1,14},{2,13},{3,12},{4,11},{5,10},{6,9},{7,8},{8,7},{9,6},... | collective-permute-start | bytes 1572872 | tf_op jit(solution)/shard_map/ppermute | solution.py:475
  28.6 6.6 %copy-start.10 = (bf16[2,272,256]{2,1,0:T(8,128)(2,1)S(1)}, bf16[2,272,256]{2,1,0:T(8,128)(2,1)}, u32[]{:S(2)}) copy-start(bf16[2,272,256]{2,1,0:T(8,128)(2,1)} %constant.125.clone) | copy-start | bytes 835588
  28.6 6.6 %copy-start.11 = (bf16[2,272,256]{2,1,0:T(8,128)(2,1)S(1)}, bf16[2,272,256]{2,1,0:T(8,128)(2,1)}, u32[]{:S(2)}) copy-start(bf16[2,272,256]{2,1,0:T(8,128)(2,1)} %constant.124.clone) | copy-start | bytes 835588
  30.8 20.9 %all-to-all-start.1 = ((bf16[16,2,128,128]{3,2,1,0:T(8,128)(2,1)}), bf16[16,2,128,128]{3,2,1,0:T(8,128)(2,1)S(1)}, u32[]{:S(2)}, u32[]{:S(2)}) async-start(bf16[16,2,128,128]{3,2,1,0:T(8,128)(2,1)} %row_forward.1), calls=%async_computation.1 | async-start | bytes 2097152 | tf_op jit(solution)/shard_map/all_to_all | solution.py:483
  37.2 14.6 %copy-start.3 = (f32[2,2,128,128]{3,2,1,0:T(8,128)S(1)}, f32[2,2,128,128]{3,2,1,0:T(8,128)}, u32[]{:S(2)}) copy-start(f32[2,2,128,128]{3,2,1,0:T(8,128)} %constant.149.mid_ref) | copy-start | bytes 786436
  51.8 1.6 %copy-start = (bf16[2,2,2048,128]{3,2,1,0:T(8,128)(2,1)S(1)}, bf16[2,2,2048,128]{3,2,1,0:T(8,128)(2,1)}, u32[]{:S(2)}) copy-start(bf16[2,2,2048,128]{3,2,1,0:T(8,128)(2,1)} %filter_layout.1.filt_ref) | copy-start | bytes 6291460
  57.7 19.6 %copy-start.1 = (bf16[512,2048]{1,0:T(8,128)(2,1)S(1)}, bf16[512,2048]{1,0:T(8,128)(2,1)}, u32[]{:S(2)}) copy-start(bf16[512,2048]{1,0:T(8,128)(2,1)} %constant.122.clone.table_ref) | copy-start | bytes 6291460
  77.3 20.4 %copy-start.8 = (bf16[32,64,128]{2,1,0:T(8,128)(2,1)S(1)}, bf16[32,64,128]{2,1,0:T(8,128)(2,1)}, u32[]{:S(2)}) copy-start(bf16[32,64,128]{2,1,0:T(8,128)(2,1)} %param.15) | copy-start | bytes 1572868
  77.3 20.4 %copy-start.9 = (bf16[32,64,128]{2,1,0:T(8,128)(2,1)S(1)}, bf16[32,64,128]{2,1,0:T(8,128)(2,1)}, u32[]{:S(2)}) copy-start(bf16[32,64,128]{2,1,0:T(8,128)(2,1)} %param.14) | copy-start | bytes 1572868
  77.3 20.4 %copy-start.13 = (f32[32]{0:T(128)S(1)}, f32[32]{0:T(128)}, u32[]{:S(2)}) copy-start(f32[32]{0:T(128)} %param.18) | copy-start | bytes 388

commit v5 on v4

--- a/solution.py
+++ b/solution.py
@@ -38,12 +38,7 @@
     cosines, sines = np.cos(angle), -np.sin(angle)
     sines[:, 0] = 1.0 - 2.0 * (np.arange(HALF) % 2)
     parts = np.stack([cosines, sines], 0).reshape(2, HALF, BLOCKS, PER).transpose(1, 2, 0, 3)
-    return narrow(np.repeat(parts[:, :, :, None, :], 2, 3).reshape(HALF, BLOCKS * 2 * 2 * PER))
-
-
-def row_forward_table():
-    both = row_table().reshape(HALF, BLOCKS, 2, 2, PER)
-    return both[:, :, :, 0].reshape(HALF, BLOCKS * 2 * PER)
+    return narrow(parts.reshape(HALF, BLOCKS * 2 * PER))
 
 
 def pair_order(table, first, second):
@@ -415,15 +410,21 @@
     lead = lane % PER == 0
     for pair in range(2):
         for block in range(BLOCKS):
+            parts = []
             for part in range(2):
                 if pair == 0:
                     values = z_ref[block, part]
                 else:
                     values = jnp.where(lead, z_ref[16 - block if block else 8, part], z_ref[15 - block, part])
-                lanes = slice((block * 2 + part) * LANES, (block * 2 + part + 1) * LANES)
-                zero = jnp.zeros_like(values)
-                split_ref[pair * 256 : pair * 256 + 128, lanes] = jnp.where(first, values, zero)
-                split_ref[pair * 256 + 128 : pair * 256 + 256, lanes] = jnp.where(first, zero, values)
+                parts.append(values.astype(F32))
+            real, imag = parts
+            lanes = slice(block * LANES, (block + 1) * LANES)
+            split_ref[pair * 256 : pair * 256 + 128, lanes] = jnp.where(
+                first, real, pltpu.roll(imag, PER, 1)
+            ).astype(BF16)
+            split_ref[pair * 256 + 128 : pair * 256 + 256, lanes] = jnp.where(
+                first, pltpu.roll(real, PER, 1), imag
+            ).astype(BF16)
         sums = lax.dot_general(
             table_ref[...],
             split_ref[pair * 256 : (pair + 1) * 256, :],
@@ -444,7 +445,7 @@
         in_specs=[inside] * 3,
         out_specs=inside,
         out_shape=jax.ShapeDtypeStruct((8, 4, 64, LANES), BF16),
-        scratch_shapes=[pltpu.VMEM((4 * LANES, COLS), BF16)],
+        scratch_shapes=[pltpu.VMEM((4 * LANES, ROWS), BF16)],
         compiler_params=pltpu.CompilerParams(vmem_limit_bytes=16 * 1024 * 1024),
         cost_estimate=pl.CostEstimate(flops=1_100_000_000, bytes_accessed=4_000_000, transcendentals=0),
         name="row_inverse",
@@ -479,7 +480,7 @@
     lane = jnp.arange(LANES, dtype=jnp.int32) % PER
     all_k1 = (PER * jnp.arange(BLOCKS, dtype=jnp.int32))[:, None, None] + lane[None, None, :]
     phase = turn(all_k1, col, ROWS * 16)
-    y = row_forward(x.reshape(8, 4, 64, LANES), jnp.asarray(row_forward_table()), twist_base(), phase, order)
+    y = row_forward(x.reshape(8, 4, 64, LANES), table, twist_base(), phase, order)
     y = lax.all_to_all(y, "col", split_axis=0, concat_axis=0, tiled=True)
 
     own_k1 = PER * jnp.where(low_side, col, jnp.where(lane == 0, (16 - col) % 8, 15 - col)) + lane

time: 99.6 us -> 98.3 us (0.987)
  Pallas kernels: 18.7 us -> 17.2 us
    pallas_call x1, Pallas kernels: 2.84 us -> 1.73 us  [row_inverse(): pl.pallas_call(row_inverse_body, in_specs=[inside] * 3, out_specs=inside,...]
where the time goes in v5:
time: 98.3 us; the launch traced here: 97.7 us
  blocking collectives  37.2 us (38%)
  waiting for transfers between devices  20.8 us (21%)
  Pallas kernels  17.2 us (17%)
  starting transfers between devices  15.8 us (16%)
  other arithmetic  4.87 us (5%)
  local copies, waits for them, and re-layouts  1.67 us (2%)
    all_to_all x1, blocking collectives, per_device(): z = lax.all_to_all(z, 'col', split_axis=0, concat_axis=0, tiled=True)  19.6 us
    all_to_all x1, blocking collectives, per_device(): lax.all_to_all(convolved, 'row', split_axis=0, concat_axis=0, tiled=True)  17.5 us
    all_to_all x1, waiting for transfers between devices, per_device(): x = lax.all_to_all(gated, 'row', split_axis=0, concat_axis=0, tiled=True)  11.5 us
    all_to_all x1, waiting for transfers between devices, per_device(): y = lax.all_to_all(y, 'col', split_axis=0, concat_axis=0, tiled=True)  9.23 us
    all_to_all x1, starting transfers between devices, per_device(): x = lax.all_to_all(gated, 'row', split_axis=0, concat_axis=0, tiled=True)  6.64 us
    pallas_call x1, Pallas kernels, filter_layout(): pl.pallas_call(filter_body, grid_spec=pltpu.PrefetchScalarGridSpec(num_sc...  5.27 us
    all_to_all x1, starting transfers between devices, per_device(): y = lax.all_to_all(y, 'col', split_axis=0, concat_axis=0, tiled=True)  4.3 us
    pallas_call x1, Pallas kernels, column_step(): pl.pallas_call(column_body, in_specs=[inside] * 7, out_specs=inside, out_...  4.08 us
  transfers between devices with their start and end apart: 5, of which 2 were waited for; matrix products, arithmetic and copies ran while one was open for 4% of the time, Pallas kernels for 10%

profile of v5, /device:TPU:0, one launch (start us, length us, event | category | flops | bytes accessed | tf_op | source)
XLA Modules:
  0.0 97.7 jit_solution(4650403931921836927)
XLA Ops:
  0.0 2.0 %filter_send.2 = (bf16[2,64,2048]{2,1,0:T(8,128)(2,1)S(1)}, bf16[16,2048]{1,0:T(8,128)(2,1)}) custom-call(s32[1]{0:T(128)} %bitcast.refs_0_.half_ref, f32[2,4,64,2048]{3,2,1,0:T(8,128)} %own_ref.1), custom_call_target="tpu_custom_call" | custom-call | bytes 1700000 | tf_op jit(solution)/shard_map/filter_send/pallas_call | solution.py:166
  2.0 0.0 copy-start.12
  2.0 0.0 copy-start.1
  2.0 0.0 copy-start.4
  2.0 0.0 copy-start.5
  2.1 1.7 %collective-permute-start.2 = (bf16[16,2048]{1,0:T(8,128)(2,1)}, bf16[16,2048]{1,0:T(8,128)(2,1)}, u32[]{:S(2)}, u32[]{:S(2)}) collective-permute-start(bf16[16,2048]{1,0:T(8,128)(2,1)} %get-tuple-element.10), channel_id=1, source_target_pairs={{0,8},{1,15},{2,14},{3,13},{4,12},{5,11},{6,10},{7,9},{8,0},{9,7},... | collective-permute-start | bytes 196616 | tf_op jit(solution)/shard_map/ppermute | solution.py:471
  3.8 3.0 %collective-permute-start = (bf16[2,64,2048]{2,1,0:T(8,128)(2,1)S(1)}, bf16[2,64,2048]{2,1,0:T(8,128)(2,1)}, u32[]{:S(2)}, u32[]{:S(2)}) collective-permute-start(bf16[2,64,2048]{2,1,0:T(8,128)(2,1)S(1)} %get-tuple-element.8), channel_id=1, source_target_pairs={{0,15},{1,14},{2,13},{3,12},{4,11},{5,10},{6,9},{7,8},{8,7},{9,6},... | collective-permute-start | bytes 1572872 | tf_op jit(solution)/shard_map/ppermute | solution.py:470
  6.8 1.0 %fusion.refs_2_ = bf16[32,64,128]{2,1,0:T(8,128)(2,1)} fusion(bf16[32,64,128]{2,1,0:T(8,128)(2,1)S(1)} %copy-done.6, bf16[32,64,128]{2,1,0:T(8,128)(2,1)S(1)} %copy-done.7), kind=kLoop, calls=%fused_computation.2 | loop fusion | flops 1048576 | bytes 1572864 | tf_op jit(solution)/shard_map/convert_element_type | solution.py:474
  7.8 6.6 %all-to-all-start = ((bf16[32,64,128]{2,1,0:T(8,128)(2,1)}), bf16[32,64,128]{2,1,0:T(8,128)(2,1)S(1)}, u32[]{:S(2)}, u32[]{:S(2)}) async-start(bf16[32,64,128]{2,1,0:T(8,128)(2,1)} %fusion.refs_2_), calls=%async_computation | async-start | bytes 1048576 | tf_op jit(solution)/shard_map/all_to_all | solution.py:475
  14.4 1.9 %filter_send.3 = bf16[2,64,2048]{2,1,0:T(8,128)(2,1)} custom-call(s32[1]{0:T(128)} %bitcast.refs_0_.half_ref, f32[2,4,64,2048]{3,2,1,0:T(8,128)} %own_ref.1, bf16[32,64,128]{2,1,0:T(8,128)(2,1)} %fusion.refs_2_), custom_call_target="tpu_custom_call" | custom-call | bytes 1700000 | tf_op jit(solution)/shard_map/filter_send/pallas_call | solution.py:166
  16.4 0.0 copy-start.10
  16.4 0.0 copy-start.11
  16.4 0.1 collective-permute-start.1
  16.5 0.1 fusion.13
  16.6 0.1 multiply_cosine_fusion
  16.8 0.3 fusion.5
  17.1 11.5 %all-to-all-done = bf16[32,64,128]{2,1,0:T(8,128)(2,1)S(1)} async-done(((bf16[32,64,128]{2,1,0:T(8,128)(2,1)}), bf16[32,64,128]{2,1,0:T(8,128)(2,1)S(1)}, u32[]{:S(2)}, u32[]{:S(2)}) %all-to-all-start) | async-done | bytes 524320 | tf_op jit(solution)/shard_map/all_to_all | solution.py:475
  28.7 2.2 %row_forward.1 = bf16[16,2,128,128]{3,2,1,0:T(8,128)(2,1)} custom-call(bf16[8,4,64,128]{3,2,1,0:T(8,128)(2,1)S(1)} %bitcast.4, bf16[512,1024]{1,0:T(8,128)(2,1)S(1)} %copy-done.1, f32[3,128,128]{2,1,0:T(8,128)S(1)} %copy-done.4, f32[2,8,1,128]{3,2,1,0:T(1,128)S(1)} %pad_maximum_fusion.2.phase_ref, bf16[128,128]{1,0:T(8,128)(2,1)S(1)} %copy-done.5), custom_call_target="tpu_custom_call" | custom-call | flops 1100000000 | bytes 5000000 | tf_op jit(solution)/shard_map/row_forward/pallas_call | solution.py:239
  30.9 4.3 %all-to-all-start.1 = ((bf16[16,2,128,128]{3,2,1,0:T(8,128)(2,1)}), bf16[16,2,128,128]{3,2,1,0:T(8,128)(2,1)S(1)}, u32[]{:S(2)}, u32[]{:S(2)}) async-start(bf16[16,2,128,128]{3,2,1,0:T(8,128)(2,1)} %row_forward.1), calls=%async_computation.1 | async-start | bytes 2097152 | tf_op jit(solution)/shard_map/all_to_all | solution.py:484
  35.2 0.1 fusion.15
  35.3 0.7 broadcast_select_fusion.moves_ref
  36.0 1.2 %broadcast_multiply_fusion.step_ref = bf16[6,256,256]{2,1,0:T(8,128)(2,1)S(1)} fusion(bf16[6,256,256]{2,1,0:T(8,128)(2,1)} %constant.127.clone, bf16[]{:T(256)S(6)} %convert_element_type.83), kind=kLoop, calls=%fused_computation.3 | loop fusion | flops 393216 | bytes 1572866 | tf_op jit(solution)/shard_map/mul | solution.py:492
  37.2 0.0 copy-start.3
  37.3 5.3 %filter_layout.1.filt_ref = bf16[2,2,2048,128]{3,2,1,0:T(8,128)(2,1)} custom-call(s32[1]{0:T(128)} %bitcast.refs_0_.half_ref, f32[2,4,64,2048]{3,2,1,0:T(8,128)} %own_ref.1, bf16[2,64,2048]{2,1,0:T(8,128)(2,1)} %collective-permute-done.early_ref, bf16[2,64,2048]{2,1,0:T(8,128)(2,1)} %collective-permute-done.1.late_ref, ...), custom_call_target="tpu_custom_call" | custom-call | flops 600000000 | bytes 5000000 | tf_op jit(solution)/shard_map/filter_layout/pallas_call | solution.py:269
  42.5 9.2 %all-to-all-done.1.y_ref = bf16[16,2,128,128]{3,2,1,0:T(8,128)(2,1)S(1)} async-done(((bf16[16,2,128,128]{3,2,1,0:T(8,128)(2,1)}), bf16[16,2,128,128]{3,2,1,0:T(8,128)(2,1)S(1)}, u32[]{:S(2)}, u32[]{:S(2)}) %all-to-all-start.1) | async-done | bytes 1048608 | tf_op jit(solution)/shard_map/all_to_all | solution.py:484
  51.8 1.6 %copy-done = bf16[2,2,2048,128]{3,2,1,0:T(8,128)(2,1)S(1)} copy-done((bf16[2,2,2048,128]{3,2,1,0:T(8,128)(2,1)S(1)}, bf16[2,2,2048,128]{3,2,1,0:T(8,128)(2,1)}, u32[]{:S(2)}) %copy-start) | copy-done | bytes 2097176
  53.4 4.1 %column_step.1 = bf16[16,2,128,128]{3,2,1,0:T(8,128)(2,1)S(1)} custom-call(bf16[16,2,128,128]{3,2,1,0:T(8,128)(2,1)S(1)} %all-to-all-done.1.y_ref, bf16[2,2,2048,128]{3,2,1,0:T(8,128)(2,1)S(1)} %copy-done, bf16[6,256,256]{2,1,0:T(8,128)(2,1)S(1)} %broadcast_multiply_fusion.step_ref, f32[2,2,128,128]{3,2,1,0:T(8,128)S(1)} %copy-done.3, ...), custom_call_target="tpu_custom_call" | custom-call | flops 2000000000 | bytes 5000000 | tf_op jit(solution)/shard_map/column_step/pallas_call | solution.py:395
  57.5 0.0 copy-start.8
  57.5 19.6 %all_to_all.20.z_ref = bf16[16,2,128,128]{3,2,1,0:T(8,128)(2,1)S(1)} all-to-all(bf16[16,2,128,128]{3,2,1,0:T(8,128)(2,1)S(1)} %column_step.1), channel_id=1, replica_groups=mesh['row'=8,'col'=16] {'col'}, dimensions={0} | all-to-all | bytes 2097152 | tf_op jit(solution)/shard_map/all_to_all | solution.py:494
  77.1 1.7 %row_inverse.1 = bf16[8,4,64,128]{3,2,1,0:T(8,128)(2,1)S(1)} custom-call(bf16[16,2,128,128]{3,2,1,0:T(8,128)(2,1)S(1)} %all_to_all.20.z_ref, bf16[512,1024]{1,0:T(8,128)(2,1)S(1)} %copy-done.2, bf16[128,128]{1,0:T(8,128)(2,1)S(1)} %copy-done.5), custom_call_target="tpu_custom_call" | custom-call | flops 1100000000 | bytes 4000000 | tf_op jit(solution)/shard_map/row_inverse/pallas_call | solution.py:443
  78.9 17.5 %all_to_all.21 = bf16[32,64,128]{2,1,0:T(8,128)(2,1)S(1)} all-to-all(bf16[32,64,128]{2,1,0:T(8,128)(2,1)S(1)} %bitcast.5), channel_id=1, replica_groups=mesh['row'=8,'col'=16] {'row'}, dimensions={0} | all-to-all | bytes 1048576 | tf_op jit(solution)/shard_map/all_to_all | solution.py:497
  96.4 1.3 %add_multiply_fusion = f32[32,64,128]{2,1,0:T(8,128)} fusion(bf16[32,64,128]{2,1,0:T(8,128)(2,1)S(1)} %all_to_all.21, bf16[32,64,128]{2,1,0:T(8,128)(2,1)S(1)} %copy-done.9, bf16[32,64,128]{2,1,0:T(8,128)(2,1)S(1)} %copy-done.6, bf16[32,64,128]{2,1,0:T(8,128)(2,1)S(1)} %copy-done.8, f32[32]{0:T(128)S(1)} %copy-done.13), kind=kLoop, calls=%fused_computation | loop fusion | flops 2097152 | bytes 3145856 | tf_op jit(solution)/shard_map/mul | solution.py:499
  (29 shorter events, 0.1 us)
Async XLA Ops:
  0.0 6.8 %copy-start.7 = (bf16[32,64,128]{2,1,0:T(8,128)(2,1)S(1)}, bf16[32,64,128]{2,1,0:T(8,128)(2,1)}, u32[]{:S(2)}) copy-start(bf16[32,64,128]{2,1,0:T(8,128)(2,1)} %param.14) | copy-start | bytes 1572868
  0.0 6.8 %copy-start.6 = (bf16[32,64,128]{2,1,0:T(8,128)(2,1)S(1)}, bf16[32,64,128]{2,1,0:T(8,128)(2,1)}, u32[]{:S(2)}) copy-start(bf16[32,64,128]{2,1,0:T(8,128)(2,1)} %param.15) | copy-start | bytes 1572868
  2.0 14.8 %copy-start.12 = (s32[128]{0:T(128)S(1)}, s32[128]{0:T(128)}, u32[]{:S(2)}) copy-start(s32[128]{0:T(128)} %constant.125.clone) | copy-start | bytes 1540
  2.0 26.6 %copy-start.1 = (bf16[512,1024]{1,0:T(8,128)(2,1)S(1)}, bf16[512,1024]{1,0:T(8,128)(2,1)}, u32[]{:S(2)}) copy-start(bf16[512,1024]{1,0:T(8,128)(2,1)} %constant.120.clone.table_ref) | copy-start | bytes 3145732
  2.0 26.6 %copy-start.4 = (f32[3,128,128]{2,1,0:T(8,128)S(1)}, f32[3,128,128]{2,1,0:T(8,128)}, u32[]{:S(2)}) copy-start(f32[3,128,128]{2,1,0:T(8,128)} %constant.124.clone.base_ref) | copy-start | bytes 589828
  2.0 26.6 %copy-start.5 = (bf16[128,128]{1,0:T(8,128)(2,1)S(1)}, bf16[128,128]{1,0:T(8,128)(2,1)}, u32[]{:S(2)}) copy-start(bf16[128,128]{1,0:T(8,128)(2,1)} %constant.121.clone.order_ref) | copy-start | bytes 98308
  2.1 35.2 %collective-permute-start.2 = (bf16[16,2048]{1,0:T(8,128)(2,1)}, bf16[16,2048]{1,0:T(8,128)(2,1)}, u32[]{:S(2)}, u32[]{:S(2)}) collective-permute-start(bf16[16,2048]{1,0:T(8,128)(2,1)} %get-tuple-element.10), channel_id=1, source_target_pairs={{0,8},{1,15},{2,14},{3,13},{4,12},{5,11},{6,10},{7,9},{8,0},{9,7},... | collective-permute-start | bytes 196616 | tf_op jit(solution)/shard_map/ppermute | solution.py:471
  3.8 33.5 %collective-permute-start = (bf16[2,64,2048]{2,1,0:T(8,128)(2,1)S(1)}, bf16[2,64,2048]{2,1,0:T(8,128)(2,1)}, u32[]{:S(2)}, u32[]{:S(2)}) collective-permute-start(bf16[2,64,2048]{2,1,0:T(8,128)(2,1)S(1)} %get-tuple-element.8), channel_id=1, source_target_pairs={{0,15},{1,14},{2,13},{3,12},{4,11},{5,10},{6,9},{7,8},{8,7},{9,6},... | collective-permute-start | bytes 1572872 | tf_op jit(solution)/shard_map/ppermute | solution.py:470
  7.8 20.9 %all-to-all-start = ((bf16[32,64,128]{2,1,0:T(8,128)(2,1)}), bf16[32,64,128]{2,1,0:T(8,128)(2,1)S(1)}, u32[]{:S(2)}, u32[]{:S(2)}) async-start(bf16[32,64,128]{2,1,0:T(8,128)(2,1)} %fusion.refs_2_), calls=%async_computation | async-start | bytes 1048576 | tf_op jit(solution)/shard_map/all_to_all | solution.py:475
  16.4 18.8 %copy-start.10 = (bf16[2,272,256]{2,1,0:T(8,128)(2,1)S(1)}, bf16[2,272,256]{2,1,0:T(8,128)(2,1)}, u32[]{:S(2)}) copy-start(bf16[2,272,256]{2,1,0:T(8,128)(2,1)} %constant.123.clone) | copy-start | bytes 835588
  16.4 18.8 %copy-start.11 = (bf16[2,272,256]{2,1,0:T(8,128)(2,1)S(1)}, bf16[2,272,256]{2,1,0:T(8,128)(2,1)}, u32[]{:S(2)}) copy-start(bf16[2,272,256]{2,1,0:T(8,128)(2,1)} %constant.122.clone) | copy-start | bytes 835588
  16.4 20.8 %collective-permute-start.1 = (bf16[2,64,2048]{2,1,0:T(8,128)(2,1)}, bf16[2,64,2048]{2,1,0:T(8,128)(2,1)}, u32[]{:S(2)}, u32[]{:S(2)}) collective-permute-start(bf16[2,64,2048]{2,1,0:T(8,128)(2,1)} %filter_send.3), channel_id=1, source_target_pairs={{0,15},{1,14},{2,13},{3,12},{4,11},{5,10},{6,9},{7,8},{8,7},{9,6},... | collective-permute-start | bytes 1572872 | tf_op jit(solution)/shard_map/ppermute | solution.py:476
  30.9 20.9 %all-to-all-start.1 = ((bf16[16,2,128,128]{3,2,1,0:T(8,128)(2,1)}), bf16[16,2,128,128]{3,2,1,0:T(8,128)(2,1)S(1)}, u32[]{:S(2)}, u32[]{:S(2)}) async-start(bf16[16,2,128,128]{3,2,1,0:T(8,128)(2,1)} %row_forward.1), calls=%async_computation.1 | async-start | bytes 2097152 | tf_op jit(solution)/shard_map/all_to_all | solution.py:484
  37.2 14.6 %copy-start.3 = (f32[2,2,128,128]{3,2,1,0:T(8,128)S(1)}, f32[2,2,128,128]{3,2,1,0:T(8,128)}, u32[]{:S(2)}) copy-start(f32[2,2,128,128]{3,2,1,0:T(8,128)} %constant.146.mid_ref) | copy-start | bytes 786436
  51.8 1.6 %copy-start = (bf16[2,2,2048,128]{3,2,1,0:T(8,128)(2,1)S(1)}, bf16[2,2,2048,128]{3,2,1,0:T(8,128)(2,1)}, u32[]{:S(2)}) copy-start(bf16[2,2,2048,128]{3,2,1,0:T(8,128)(2,1)} %filter_layout.1.filt_ref) | copy-start | bytes 6291460
  53.4 23.8 %copy-start.2 = (bf16[512,1024]{1,0:T(8,128)(2,1)S(1)}, bf16[512,1024]{1,0:T(8,128)(2,1)}, u32[]{:S(2)}) copy-start(bf16[512,1024]{1,0:T(8,128)(2,1)} %constant.120.clone.table_ref) | copy-start | bytes 3145732
  57.5 39.0 %copy-start.8 = (bf16[32,64,128]{2,1,0:T(8,128)(2,1)S(1)}, bf16[32,64,128]{2,1,0:T(8,128)(2,1)}, u32[]{:S(2)}) copy-start(bf16[32,64,128]{2,1,0:T(8,128)(2,1)} %param.14) | copy-start | bytes 1572868
  57.5 38.9 %copy-start.9 = (bf16[32,64,128]{2,1,0:T(8,128)(2,1)S(1)}, bf16[32,64,128]{2,1,0:T(8,128)(2,1)}, u32[]{:S(2)}) copy-start(bf16[32,64,128]{2,1,0:T(8,128)(2,1)} %param.13) | copy-start | bytes 1572868
  57.5 38.9 %copy-start.13 = (f32[32]{0:T(128)S(1)}, f32[32]{0:T(128)}, u32[]{:S(2)}) copy-start(f32[32]{0:T(128)} %param.17) | copy-start | bytes 388

commit v6 on v5

--- a/solution.py
+++ b/solution.py
@@ -250,37 +250,52 @@
     )(x, table, base, phase, order)
 
 
-def filter_body(half_ref, own_ref, early_ref, late_ref, extra_ref, moves_ref, out_ref):
-    for part in range(2):
-        own = own_ref[part].reshape(LANES, own_ref.shape[3]).astype(BF16)
-        got = (early_ref, late_ref)[part][...].reshape(LANES, early_ref.shape[2])
-        total = None
-        for source, low, high in ((own, 0, 128), (got, 128, 256), (extra_ref[...], 256, 272)):
-            term = lax.dot_general(
-                source, moves_ref[part, low:high, :], (((0,), (0,)), ((), ())), preferred_element_type=F32
-            )
-            total = term if total is None else total + term
-        out_ref[0, part] = total[:, :LANES].astype(BF16)
-        out_ref[1, part] = total[:, LANES:].astype(BF16)
+def filter_body(
+    half_ref, spec_hbm, early_hbm, late_hbm, extra_ref, moves_ref, out_ref, own_ref, early_ref, late_ref, sems,
+):
+    step = 512
+    copies = []
+    for index in range(COLS // step):
+        cols = pl.ds(index * step, step)
+        copies.append([])
+        for source, target in (
+            (spec_hbm.at[:, pl.ds(2 * half_ref[0], 2), :, cols], own_ref.at[:, :, :, cols]),
+            (early_hbm.at[:, :, cols], early_ref.at[:, :, cols]),
+            (late_hbm.at[:, :, cols], late_ref.at[:, :, cols]),
+        ):
+            copies[index].append(pltpu.make_async_copy(source, target, sems.at[index, len(copies[index])]))
+            copies[index][-1].start()
+    for index in range(COLS // step):
+        for copy in copies[index]:
+            copy.wait()
+        cols = slice(index * step, (index + 1) * step)
+        for part in range(2):
+            own = own_ref[part, :, :, cols].reshape(LANES, step).astype(BF16)
+            got = (early_ref, late_ref)[part][:, :, cols].reshape(LANES, step)
+            total = None
+            for source, low, high in ((own, 0, 128), (got, 128, 256), (extra_ref[:, cols], 256, 272)):
+                term = lax.dot_general(
+                    source, moves_ref[part, low:high, :], (((0,), (0,)), ((), ())), preferred_element_type=F32
+                )
+                total = term if total is None else total + term
+            out_ref[0, part, cols, :] = total[:, :LANES].astype(BF16)
+            out_ref[1, part, cols, :] = total[:, LANES:].astype(BF16)
 
 
 def filter_layout(spec, half, early, late, extra, moves):
-    step = 512
+    anywhere = pl.BlockSpec(memory_space=pl.ANY)
+    inside = pl.BlockSpec(memory_space=pltpu.VMEM)
     return pl.pallas_call(
         filter_body,
-        grid_spec=pltpu.PrefetchScalarGridSpec(
-            num_scalar_prefetch=1,
-            grid=(COLS // step,),
-            in_specs=[
-                pl.BlockSpec((2, 2, PER, step), lambda i, half: (0, half[0], 0, i)),
-                pl.BlockSpec((2, PER, step), lambda i, half: (0, 0, i)),
-                pl.BlockSpec((2, PER, step), lambda i, half: (0, 0, i)),
-                pl.BlockSpec((16, step), lambda i, half: (0, i)),
-                pl.BlockSpec((2, 272, 256), lambda i, half: (0, 0, 0)),
-            ],
-            out_specs=pl.BlockSpec((2, 2, step, LANES), lambda i, half: (0, 0, i, 0)),
-        ),
-        out_shape=jax.ShapeDtypeStruct((2, 2, COLS, LANES), BF16),
+        in_specs=[pl.BlockSpec(memory_space=pltpu.SMEM), anywhere, anywhere, anywhere, inside, inside],
+        out_specs=inside,
+        out_shape=pltpu.VMEM((2, 2, COLS, LANES), BF16),
+        scratch_shapes=[
+            pltpu.VMEM((2, 2, PER, COLS), F32),
+            pltpu.VMEM((2, PER, COLS), BF16),
+            pltpu.VMEM((2, PER, COLS), BF16),
+            pltpu.SemaphoreType.DMA((4, 3)),
+        ],
         compiler_params=pltpu.CompilerParams(vmem_limit_bytes=55 * 1024 * 1024),
         cost_estimate=pl.CostEstimate(flops=600_000_000, bytes_accessed=5_000_000, transcendentals=0),
         name="filter_layout",

time: 98.3 us -> 98.8 us (level)
  other arithmetic: 4.87 us -> 7.75 us
  waiting for transfers between devices: 20.8 us -> 18 us
  local copies, waits for them, and re-layouts: 1.67 us -> 2.75 us
    all_to_all x1, waiting for transfers between devices: 9.23 us -> 7.44 us  [per_device(): y = lax.all_to_all(y, 'col', split_axis=0, concat_axis=0, tiled=True)]
    unnamed x28 -> x26, local copies, waits for them, and re-layouts: 1.67 us -> 2.75 us
    convert_element_type x1, other arithmetic: 0.98 us -> 2.02 us  [per_device(): gated = gated.astype(BF16)]
  transfers between devices with their start and end apart: 5 -> 5, of which waited for: 2 -> 2; matrix products, arithmetic and copies ran while one was open for 4% -> 7% of each run, Pallas kernels for 10% -> 9%
where the time goes in v6:
time: 98.8 us; the launch traced here: 98.2 us
  blocking collectives  37.2 us (38%)
  waiting for transfers between devices  18 us (18%)
  Pallas kernels  16.6 us (17%)
  starting transfers between devices  15.8 us (16%)
  other arithmetic  7.75 us (8%)
  local copies, waits for them, and re-layouts  2.75 us (3%)
    all_to_all x1, blocking collectives, per_device(): z = lax.all_to_all(z, 'col', split_axis=0, concat_axis=0, tiled=True)  19.6 us
    all_to_all x1, blocking collectives, per_device(): lax.all_to_all(convolved, 'row', split_axis=0, concat_axis=0, tiled=True)  17.6 us
    all_to_all x1, waiting for transfers between devices, per_device(): x = lax.all_to_all(gated, 'row', split_axis=0, concat_axis=0, tiled=True)  10.5 us
    all_to_all x1, waiting for transfers between devices, per_device(): y = lax.all_to_all(y, 'col', split_axis=0, concat_axis=0, tiled=True)  7.44 us
    all_to_all x1, starting transfers between devices, per_device(): x = lax.all_to_all(gated, 'row', split_axis=0, concat_axis=0, tiled=True)  6.64 us
    pallas_call x1, Pallas kernels, filter_layout(): pl.pallas_call(filter_body, in_specs=[pl.BlockSpec(memory_space=pltpu.SME...  4.65 us
    all_to_all x1, starting transfers between devices, per_device(): y = lax.all_to_all(y, 'col', split_axis=0, concat_axis=0, tiled=True)  4.3 us
    pallas_call x1, Pallas kernels, column_step(): pl.pallas_call(column_body, in_specs=[inside] * 7, out_specs=inside, out_...  4.08 us
  transfers between devices with their start and end apart: 5, of which 2 were waited for; matrix products, arithmetic and copies ran while one was open for 7% of the time, Pallas kernels for 9%

profile of v6, /device:TPU:0, one launch (start us, length us, event | category | flops | bytes accessed | tf_op | source)
XLA Modules:
  0.0 98.2 jit_solution(3626120549976701767)
XLA Ops:
  0.0 2.0 %filter_send.2 = (bf16[2,64,2048]{2,1,0:T(8,128)(2,1)S(1)}, bf16[16,2048]{1,0:T(8,128)(2,1)}) custom-call(s32[1]{0:T(128)} %bitcast.refs_0_.half_ref, f32[2,4,64,2048]{3,2,1,0:T(8,128)} %spec_hbm.1), custom_call_target="tpu_custom_call" | custom-call | bytes 1700000 | tf_op jit(solution)/shard_map/filter_send/pallas_call | solution.py:166
  2.0 0.0 copy-start.11
  2.0 0.0 copy-start.1
  2.0 0.0 copy-start.4
  2.0 0.0 copy-start.5
  2.0 1.7 %collective-permute-start.2 = (bf16[16,2048]{1,0:T(8,128)(2,1)}, bf16[16,2048]{1,0:T(8,128)(2,1)S(1)}, u32[]{:S(2)}, u32[]{:S(2)}) collective-permute-start(bf16[16,2048]{1,0:T(8,128)(2,1)} %get-tuple-element.10), channel_id=1, source_target_pairs={{0,8},{1,15},{2,14},{3,13},{4,12},{5,11},{6,10},{7,9},{8,0},{9,7},... | collective-permute-start | bytes 196616 | tf_op jit(solution)/shard_map/ppermute | solution.py:486
  3.8 3.0 %collective-permute-start = (bf16[2,64,2048]{2,1,0:T(8,128)(2,1)S(1)}, bf16[2,64,2048]{2,1,0:T(8,128)(2,1)}, u32[]{:S(2)}, u32[]{:S(2)}) collective-permute-start(bf16[2,64,2048]{2,1,0:T(8,128)(2,1)S(1)} %get-tuple-element.8), channel_id=1, source_target_pairs={{0,15},{1,14},{2,13},{3,12},{4,11},{5,10},{6,9},{7,8},{8,7},{9,6},... | collective-permute-start | bytes 1572872 | tf_op jit(solution)/shard_map/ppermute | solution.py:485
  6.8 2.0 %fusion.refs_2_ = bf16[32,64,128]{2,1,0:T(8,128)(2,1)} fusion(bf16[32,64,128]{2,1,0:T(8,128)(2,1)S(1)} %copy-done.6, bf16[32,64,128]{2,1,0:T(8,128)(2,1)} %param.14), kind=kLoop, calls=%fused_computation.2 | loop fusion | flops 1048576 | bytes 1572864 | tf_op jit(solution)/shard_map/convert_element_type | solution.py:489
  8.8 6.6 %all-to-all-start = ((bf16[32,64,128]{2,1,0:T(8,128)(2,1)}), bf16[32,64,128]{2,1,0:T(8,128)(2,1)S(1)}, u32[]{:S(2)}, u32[]{:S(2)}) async-start(bf16[32,64,128]{2,1,0:T(8,128)(2,1)} %fusion.refs_2_), calls=%async_computation | async-start | bytes 1048576 | tf_op jit(solution)/shard_map/all_to_all | solution.py:490
  15.4 1.9 %filter_send.3 = bf16[2,64,2048]{2,1,0:T(8,128)(2,1)} custom-call(s32[1]{0:T(128)} %bitcast.refs_0_.half_ref, f32[2,4,64,2048]{3,2,1,0:T(8,128)} %spec_hbm.1, bf16[32,64,128]{2,1,0:T(8,128)(2,1)} %fusion.refs_2_), custom_call_target="tpu_custom_call" | custom-call | bytes 1700000 | tf_op jit(solution)/shard_map/filter_send/pallas_call | solution.py:166
  17.4 0.1 collective-permute-start.1
  17.5 0.1 fusion.13
  17.6 0.1 multiply_cosine_fusion
  17.8 0.3 fusion.5
  18.1 10.5 %all-to-all-done = bf16[32,64,128]{2,1,0:T(8,128)(2,1)S(1)} async-done(((bf16[32,64,128]{2,1,0:T(8,128)(2,1)}), bf16[32,64,128]{2,1,0:T(8,128)(2,1)S(1)}, u32[]{:S(2)}, u32[]{:S(2)}) %all-to-all-start) | async-done | bytes 524320 | tf_op jit(solution)/shard_map/all_to_all | solution.py:490
  28.6 2.2 %row_forward.1 = bf16[16,2,128,128]{3,2,1,0:T(8,128)(2,1)} custom-call(bf16[8,4,64,128]{3,2,1,0:T(8,128)(2,1)S(1)} %bitcast.4, bf16[512,1024]{1,0:T(8,128)(2,1)S(1)} %copy-done.1, f32[3,128,128]{2,1,0:T(8,128)S(1)} %copy-done.4, f32[2,8,1,128]{3,2,1,0:T(1,128)S(1)} %pad_maximum_fusion.2.phase_ref, bf16[128,128]{1,0:T(8,128)(2,1)S(1)} %copy-done.5), custom_call_target="tpu_custom_call" | custom-call | flops 1100000000 | bytes 5000000 | tf_op jit(solution)/shard_map/row_forward/pallas_call | solution.py:239
  30.9 4.3 %all-to-all-start.1 = ((bf16[16,2,128,128]{3,2,1,0:T(8,128)(2,1)}), bf16[16,2,128,128]{3,2,1,0:T(8,128)(2,1)S(1)}, u32[]{:S(2)}, u32[]{:S(2)}) async-start(bf16[16,2,128,128]{3,2,1,0:T(8,128)(2,1)} %row_forward.1), calls=%async_computation.1 | async-start | bytes 2097152 | tf_op jit(solution)/shard_map/all_to_all | solution.py:499
  35.2 0.1 fusion.15
  35.2 1.7 %broadcast_select_fusion.moves_ref = bf16[2,272,256]{2,1,0:T(8,128)(2,1)} fusion(bf16[2,272,256]{2,1,0:T(8,128)(2,1)} %constant.122.clone, bf16[2,272,256]{2,1,0:T(8,128)(2,1)} %constant.123.clone, pred[]{:T(512)S(6)} %lt.47), kind=kLoop, calls=%fused_computation.4 | loop fusion | flops 139264 | bytes 835585 | tf_op jit(solution)/shard_map/jit(_where)/select_n | solution.py:492
  37.0 2.1 %broadcast_multiply_fusion.step_ref = bf16[6,256,256]{2,1,0:T(8,128)(2,1)} fusion(bf16[6,256,256]{2,1,0:T(8,128)(2,1)} %constant.127.clone, bf16[]{:T(256)S(6)} %convert_element_type.83), kind=kLoop, calls=%fused_computation.3 | loop fusion | flops 393216 | bytes 1572866 | tf_op jit(solution)/shard_map/mul | solution.py:507
  39.1 0.6 copy-done.10
  39.7 4.6 %filter_layout.1.filt_ref = bf16[2,2,2048,128]{3,2,1,0:T(8,128)(2,1)S(1)} custom-call(s32[1]{0:T(128)} %bitcast.refs_0_.half_ref, f32[2,4,64,2048]{3,2,1,0:T(8,128)} %spec_hbm.1, bf16[2,64,2048]{2,1,0:T(8,128)(2,1)} %collective-permute-done.early_hbm, bf16[2,64,2048]{2,1,0:T(8,128)(2,1)} %collective-permute-done.1.late_hbm, bf16[16,2048]{1,0:T(8,128)(2,1)} %copy-done.10, ...), custom_call_target="tpu_custom_call" | custom-call | flops 600000000 | bytes 5000000 | tf_op jit(solution)/shard_map/filter_layout/pallas_call | solution.py:288
  44.3 7.4 %all-to-all-done.1.y_ref = bf16[16,2,128,128]{3,2,1,0:T(8,128)(2,1)S(1)} async-done(((bf16[16,2,128,128]{3,2,1,0:T(8,128)(2,1)}), bf16[16,2,128,128]{3,2,1,0:T(8,128)(2,1)S(1)}, u32[]{:S(2)}, u32[]{:S(2)}) %all-to-all-start.1) | async-done | bytes 1048608 | tf_op jit(solution)/shard_map/all_to_all | solution.py:499
  51.8 1.1 %copy-done = bf16[6,256,256]{2,1,0:T(8,128)(2,1)S(1)} copy-done((bf16[6,256,256]{2,1,0:T(8,128)(2,1)S(1)}, bf16[6,256,256]{2,1,0:T(8,128)(2,1)}, u32[]{:S(2)}) %copy-start) | copy-done | bytes 786456
  52.9 0.9 copy-done.3
  53.9 4.1 %column_step.1 = bf16[16,2,128,128]{3,2,1,0:T(8,128)(2,1)S(1)} custom-call(bf16[16,2,128,128]{3,2,1,0:T(8,128)(2,1)S(1)} %all-to-all-done.1.y_ref, bf16[2,2,2048,128]{3,2,1,0:T(8,128)(2,1)S(1)} %filter_layout.1.filt_ref, bf16[6,256,256]{2,1,0:T(8,128)(2,1)S(1)} %copy-done, f32[2,2,128,128]{3,2,1,0:T(8,128)S(1)} %copy-done.3, ...), custom_call_target="tpu_custom_call" | custom-call | flops 2000000000 | bytes 5000000 | tf_op jit(solution)/shard_map/column_step/pallas_call | solution.py:410
  58.0 0.0 copy-start.8
  58.0 0.0 copy-start.9
  58.0 19.6 %all_to_all.20.z_ref = bf16[16,2,128,128]{3,2,1,0:T(8,128)(2,1)S(1)} all-to-all(bf16[16,2,128,128]{3,2,1,0:T(8,128)(2,1)S(1)} %column_step.1), channel_id=1, replica_groups=mesh['row'=8,'col'=16] {'col'}, dimensions={0} | all-to-all | bytes 2097152 | tf_op jit(solution)/shard_map/all_to_all | solution.py:509
  77.6 1.7 %row_inverse.1 = bf16[8,4,64,128]{3,2,1,0:T(8,128)(2,1)S(1)} custom-call(bf16[16,2,128,128]{3,2,1,0:T(8,128)(2,1)S(1)} %all_to_all.20.z_ref, bf16[512,1024]{1,0:T(8,128)(2,1)S(1)} %copy-done.2, bf16[128,128]{1,0:T(8,128)(2,1)S(1)} %copy-done.5), custom_call_target="tpu_custom_call" | custom-call | flops 1100000000 | bytes 4000000 | tf_op jit(solution)/shard_map/row_inverse/pallas_call | solution.py:458
  79.3 17.6 %all_to_all.21 = bf16[32,64,128]{2,1,0:T(8,128)(2,1)S(1)} all-to-all(bf16[32,64,128]{2,1,0:T(8,128)(2,1)S(1)} %bitcast.5), channel_id=1, replica_groups=mesh['row'=8,'col'=16] {'row'}, dimensions={0} | all-to-all | bytes 1048576 | tf_op jit(solution)/shard_map/all_to_all | solution.py:512
  96.9 1.3 %add_multiply_fusion = f32[32,64,128]{2,1,0:T(8,128)} fusion(bf16[32,64,128]{2,1,0:T(8,128)(2,1)S(1)} %all_to_all.21, bf16[32,64,128]{2,1,0:T(8,128)(2,1)S(1)} %copy-done.9, bf16[32,64,128]{2,1,0:T(8,128)(2,1)S(1)} %copy-done.7, bf16[32,64,128]{2,1,0:T(8,128)(2,1)S(1)} %copy-done.8, f32[32]{0:T(128)S(1)} %copy-done.12), kind=kLoop, calls=%fused_computation | loop fusion | flops 2097152 | bytes 3145856 | tf_op jit(solution)/shard_map/mul | solution.py:514
  (27 shorter events, 0.1 us)
Async XLA Ops:
  0.0 6.8 %copy-start.6 = (bf16[32,64,128]{2,1,0:T(8,128)(2,1)S(1)}, bf16[32,64,128]{2,1,0:T(8,128)(2,1)}, u32[]{:S(2)}) copy-start(bf16[32,64,128]{2,1,0:T(8,128)(2,1)} %param.15) | copy-start | bytes 1572868
  2.0 15.8 %copy-start.11 = (s32[128]{0:T(128)S(1)}, s32[128]{0:T(128)}, u32[]{:S(2)}) copy-start(s32[128]{0:T(128)} %constant.125.clone) | copy-start | bytes 1540
  2.0 26.6 %copy-start.1 = (bf16[512,1024]{1,0:T(8,128)(2,1)S(1)}, bf16[512,1024]{1,0:T(8,128)(2,1)}, u32[]{:S(2)}) copy-start(bf16[512,1024]{1,0:T(8,128)(2,1)} %constant.120.clone.table_ref) | copy-start | bytes 3145732
  2.0 26.6 %copy-start.4 = (f32[3,128,128]{2,1,0:T(8,128)S(1)}, f32[3,128,128]{2,1,0:T(8,128)}, u32[]{:S(2)}) copy-start(f32[3,128,128]{2,1,0:T(8,128)} %constant.124.clone.base_ref) | copy-start | bytes 589828
  2.0 26.6 %copy-start.5 = (bf16[128,128]{1,0:T(8,128)(2,1)S(1)}, bf16[128,128]{1,0:T(8,128)(2,1)}, u32[]{:S(2)}) copy-start(bf16[128,128]{1,0:T(8,128)(2,1)} %constant.121.clone.order_ref) | copy-start | bytes 98308
  2.0 37.0 %collective-permute-start.2 = (bf16[16,2048]{1,0:T(8,128)(2,1)}, bf16[16,2048]{1,0:T(8,128)(2,1)S(1)}, u32[]{:S(2)}, u32[]{:S(2)}) collective-permute-start(bf16[16,2048]{1,0:T(8,128)(2,1)} %get-tuple-element.10), channel_id=1, source_target_pairs={{0,8},{1,15},{2,14},{3,13},{4,12},{5,11},{6,10},{7,9},{8,0},{9,7},... | collective-permute-start | bytes 196616 | tf_op jit(solution)/shard_map/ppermute | solution.py:486
  3.8 35.3 %collective-permute-start = (bf16[2,64,2048]{2,1,0:T(8,128)(2,1)S(1)}, bf16[2,64,2048]{2,1,0:T(8,128)(2,1)}, u32[]{:S(2)}, u32[]{:S(2)}) collective-permute-start(bf16[2,64,2048]{2,1,0:T(8,128)(2,1)S(1)} %get-tuple-element.8), channel_id=1, source_target_pairs={{0,15},{1,14},{2,13},{3,12},{4,11},{5,10},{6,9},{7,8},{8,7},{9,6},... | collective-permute-start | bytes 1572872 | tf_op jit(solution)/shard_map/ppermute | solution.py:485
  8.8 19.8 %all-to-all-start = ((bf16[32,64,128]{2,1,0:T(8,128)(2,1)}), bf16[32,64,128]{2,1,0:T(8,128)(2,1)S(1)}, u32[]{:S(2)}, u32[]{:S(2)}) async-start(bf16[32,64,128]{2,1,0:T(8,128)(2,1)} %fusion.refs_2_), calls=%async_computation | async-start | bytes 1048576 | tf_op jit(solution)/shard_map/all_to_all | solution.py:490
  17.4 21.7 %collective-permute-start.1 = (bf16[2,64,2048]{2,1,0:T(8,128)(2,1)}, bf16[2,64,2048]{2,1,0:T(8,128)(2,1)}, u32[]{:S(2)}, u32[]{:S(2)}) collective-permute-start(bf16[2,64,2048]{2,1,0:T(8,128)(2,1)} %filter_send.3), channel_id=1, source_target_pairs={{0,15},{1,14},{2,13},{3,12},{4,11},{5,10},{6,9},{7,8},{8,7},{9,6},... | collective-permute-start | bytes 1572872 | tf_op jit(solution)/shard_map/ppermute | solution.py:491
  30.9 20.9 %all-to-all-start.1 = ((bf16[16,2,128,128]{3,2,1,0:T(8,128)(2,1)}), bf16[16,2,128,128]{3,2,1,0:T(8,128)(2,1)S(1)}, u32[]{:S(2)}, u32[]{:S(2)}) async-start(bf16[16,2,128,128]{3,2,1,0:T(8,128)(2,1)} %row_forward.1), calls=%async_computation.1 | async-start | bytes 2097152 | tf_op jit(solution)/shard_map/all_to_all | solution.py:499
  39.0 0.6 copy-start.10
  51.8 1.1 %copy-start = (bf16[6,256,256]{2,1,0:T(8,128)(2,1)S(1)}, bf16[6,256,256]{2,1,0:T(8,128)(2,1)}, u32[]{:S(2)}) copy-start(bf16[6,256,256]{2,1,0:T(8,128)(2,1)} %broadcast_multiply_fusion.step_ref) | copy-start | bytes 2359300
  52.9 0.9 copy-start.3
  53.9 23.7 %copy-start.2 = (bf16[512,1024]{1,0:T(8,128)(2,1)S(1)}, bf16[512,1024]{1,0:T(8,128)(2,1)}, u32[]{:S(2)}) copy-start(bf16[512,1024]{1,0:T(8,128)(2,1)} %constant.120.clone.table_ref) | copy-start | bytes 3145732
  58.0 38.9 %copy-start.7 = (bf16[32,64,128]{2,1,0:T(8,128)(2,1)S(1)}, bf16[32,64,128]{2,1,0:T(8,128)(2,1)}, u32[]{:S(2)}) copy-start(bf16[32,64,128]{2,1,0:T(8,128)(2,1)} %param.15) | copy-start | bytes 1572868
  58.0 38.9 %copy-start.8 = (bf16[32,64,128]{2,1,0:T(8,128)(2,1)S(1)}, bf16[32,64,128]{2,1,0:T(8,128)(2,1)}, u32[]{:S(2)}) copy-start(bf16[32,64,128]{2,1,0:T(8,128)(2,1)} %param.14) | copy-start | bytes 1572868
  58.0 38.9 %copy-start.9 = (bf16[32,64,128]{2,1,0:T(8,128)(2,1)S(1)}, bf16[32,64,128]{2,1,0:T(8,128)(2,1)}, u32[]{:S(2)}) copy-start(bf16[32,64,128]{2,1,0:T(8,128)(2,1)} %param.13) | copy-start | bytes 1572868
  58.0 38.9 %copy-start.12 = (f32[32]{0:T(128)S(1)}, f32[32]{0:T(128)}, u32[]{:S(2)}) copy-start(f32[32]{0:T(128)} %param.17) | copy-start | bytes 388
